TPU v7x, 32 devices: a whole 2x2x4 slice. The times are simulated.
32 devices in a mesh: row: 4 (over y, x), col: 8 (over z, core).
Axes of the slice: x: 2, y: 2, z: 4, core: 2. Of those that a mesh axis runs over, the one named last changes fastest.
Arguments:
- activations: bfloat16 [128, 320, 512], P('row', 'col'), may hold values from -6 to 6
- gain_first: bfloat16 [512], replicated, may hold values from 0.5 to 1.5
- shift_first: bfloat16 [512], replicated, may hold values from -1.5 to 1.5
- in_weight: bfloat16 [512, 1024], replicated, may hold values from -0.25 to 0.25
- conv_kernel: bfloat16 [7, 7, 992], replicated, may hold values from -2.5 to 2.5
- mix_first: bfloat16 [32, 64], replicated, may hold values from -1 to 1
- mix_second: bfloat16 [64, 128], replicated, may hold values from -0.75 to 0.75
- mix_third: bfloat16 [128, 256], replicated, may hold values from -0.5 to 0.5
- mix_fourth: bfloat16 [256, 512], replicated, may hold values from -0.375 to 0.375
- out_weight: bfloat16 [512, 512], replicated, may hold values from -0.25 to 0.25
- scale_mixer: bfloat16 [512], replicated, may hold values from 0.5 to 1.5
- gain_second: bfloat16 [512], replicated, may hold values from 0.5 to 1.5
- shift_second: bfloat16 [512], replicated, may hold values from -1.5 to 1.5
- up_weight: bfloat16 [512, 2048], replicated, may hold values from -0.25 to 0.25
- up_bias: bfloat16 [2048], replicated, may hold values from -2.5 to 2.5
- down_weight: bfloat16 [2048, 512], replicated, may hold values from -0.125 to 0.125
- scale_mlp: bfloat16 [512], replicated, may hold values from 0.5 to 1.5
- valid_pixels: int32 [128, 320], P('row', 'col'), may hold values from 0 to 1, as said below
- tile_images: int32 [4, 8], replicated, may hold values from 0 to 33, as said below
- cotangent: bfloat16 [128, 320, 512], P('row', 'col'), may hold values from -6 to 6
Outputs:
- outputs: bfloat16 [128, 320, 512], P('row', 'col')
- grad_input: bfloat16 [128, 320, 512], P('row', 'col')
- grad_gain_first: float32 [512], replicated
- grad_shift_first: float32 [512], replicated
- grad_in_weight: float32 [512, 1024], replicated
- grad_conv_kernel: float32 [7, 7, 992], replicated
- grad_mix_first: float32 [32, 64], replicated
- grad_mix_second: float32 [64, 128], replicated
- grad_mix_third: float32 [128, 256], replicated
- grad_mix_fourth: float32 [256, 512], replicated
- grad_out_weight: float32 [512, 512], replicated
- grad_scale_mixer: float32 [512], replicated
- grad_gain_second: float32 [512], replicated
- grad_shift_second: float32 [512], replicated
- grad_up_weight: float32 [512, 2048], replicated
- grad_up_bias: float32 [2048], replicated
- grad_down_weight: float32 [2048, 512], replicated
- grad_scale_mlp: float32 [512], replicated
Inputs may be any that keep to these rules, and one draw needn't show every extreme that they name: `tile_images`: each image number covers a rectangle of whole tiles; image 0 covers every row of tiles and more than half of the columns of tiles, from the first. `valid_pixels`: in each image the pixels marked 1 form the top-left rectangle of its area, of three quarters or more of its height and width; image 0 has padding columns.
All inputs are finite; a program needn't handle non-finite values.
Results may differ from a plain program's by a relative error of at most 0.017.
Values may be sent and summed in bfloat16 or wider, within the bound.
No kernel may reach another device: no remote copies, remote signals or barrier semaphores. Data moves between devices by JAX's collectives and lax.ppermute only.
A program may use at most 192 MiB of HBM per device.

v0:
```python
from functools import partial

import jax
import jax.numpy as jnp
from jax import lax
from jax.sharding import PartitionSpec as P

EPS = 1e-06
DW_SCALE = 1.0 / 3.0


def extended(block, sides, width):
    for axis, dim in sides:
        count = lax.axis_size(axis)
        forward = [(i, i + 1) for i in range(count - 1)]
        backward = [(target, source) for source, target in forward]
        low = lax.ppermute(
            lax.slice_in_dim(block, block.shape[dim] - width, None, axis=dim), axis, forward
        )
        high = lax.ppermute(lax.slice_in_dim(block, 0, width, axis=dim), axis, backward)
        block = jnp.concatenate([low, block, high], axis=dim)
    return block


def matmul(left, right):
    return jnp.dot(left, right, preferred_element_type=jnp.float32)


def inner_left(left, right):
    return lax.dot_general(
        left, right, (((0,), (0,)), ((), ())), preferred_element_type=jnp.float32
    )


def inner_right(left, right):
    return lax.dot_general(
        left, right, (((1,), (1,)), ((), ())), preferred_element_type=jnp.float32
    )


def norm_forward(values, gain_vec, shift_vec, validity):
    center = values - jnp.mean(values, axis=-1, keepdims=True)
    inverse = lax.rsqrt(jnp.mean(center * center, axis=-1, keepdims=True) + EPS)
    normal = center * inverse
    return (validity * (normal * gain_vec + shift_vec), normal, inverse)


def norm_backward(grad_norm, normal, inverse, gain_vec, validity):
    masked = grad_norm * validity
    grad_gain = jnp.sum(masked * normal, axis=0)
    grad_shift = jnp.sum(masked, axis=0)
    scaled = masked * gain_vec
    centered = scaled - jnp.mean(scaled, axis=-1, keepdims=True)
    grad_values = inverse * (centered - normal * jnp.mean(scaled * normal, axis=-1, keepdims=True))
    return (grad_values, grad_gain, grad_shift)


def edge_weights(tile_images, tile_rows, tile_cols):
    row_at = lax.axis_index("row")
    col_at = lax.axis_index("col")
    row_total = lax.axis_size("row")
    col_total = lax.axis_size("col")
    offsets = jnp.arange(3, dtype=jnp.int32) - 1
    near_rows = row_at + offsets
    near_cols = col_at + offsets
    row_inside = jnp.logical_and(near_rows >= 0, near_rows < row_total)
    col_inside = jnp.logical_and(near_cols >= 0, near_cols < col_total)
    inside = jnp.logical_and(row_inside[:, None], col_inside[None, :])
    picked = tile_images[jnp.clip(near_rows, 0, row_total - 1)][
        :, jnp.clip(near_cols, 0, col_total - 1)
    ]
    own_image = tile_images[row_at, col_at]
    same_image = jnp.logical_and(inside, picked == own_image).astype(jnp.float32)
    row_zone = jnp.concatenate(
        [jnp.zeros(3, jnp.int32), jnp.ones(tile_rows, jnp.int32), jnp.full(3, 2, jnp.int32)]
    )
    col_zone = jnp.concatenate(
        [jnp.zeros(3, jnp.int32), jnp.ones(tile_cols, jnp.int32), jnp.full(3, 2, jnp.int32)]
    )
    row_onehot = (row_zone[:, None] == jnp.arange(3, dtype=jnp.int32)[None, :]).astype(jnp.float32)
    col_onehot = (col_zone[:, None] == jnp.arange(3, dtype=jnp.int32)[None, :]).astype(jnp.float32)
    return jnp.einsum("ia,ab,jb->ij", row_onehot, same_image, col_onehot)


def depthwise(gate_ext, kernel, tile_rows, tile_cols):
    summed = jnp.zeros((tile_rows, tile_cols, gate_ext.shape[-1]), jnp.float32)
    for row_off in range(7):
        for col_off in range(7):
            summed = (
                summed
                + kernel[row_off, col_off]
                * gate_ext[row_off : row_off + tile_rows, col_off : col_off + tile_cols]
            )
    return DW_SCALE * summed


def on_device(
    activations,
    gain_first,
    shift_first,
    in_weight,
    conv_kernel,
    mix_first,
    mix_second,
    mix_third,
    mix_fourth,
    out_weight,
    scale_mixer,
    gain_second,
    shift_second,
    up_weight,
    up_bias,
    down_weight,
    scale_mlp,
    valid_pixels,
    tile_images,
    cotangent,
):
    tile_rows, tile_cols, channels = activations.shape
    pixels = tile_rows * tile_cols
    gate_count = conv_kernel.shape[-1]
    lead_count = in_weight.shape[1] - gate_count
    mixes = (mix_first, mix_second, mix_third, mix_fourth)
    bounds = [0]
    for weight in mixes:
        bounds.append(bounds[-1] + weight.shape[0])
    bounds.append(bounds[-1] + mixes[-1].shape[1])
    edge_mask = edge_weights(tile_images, tile_rows, tile_cols)[..., None].astype(jnp.bfloat16)
    validity = valid_pixels.reshape(pixels, 1).astype(jnp.float32)
    inputs = activations.reshape(pixels, channels).astype(jnp.float32)
    gain_one = gain_first.astype(jnp.float32)
    gain_two = gain_second.astype(jnp.float32)
    normed_one, normal_one, inverse_one = norm_forward(
        inputs, gain_one, shift_first.astype(jnp.float32), validity
    )
    normed_low = normed_one.astype(jnp.bfloat16)
    joined = matmul(normed_low, in_weight)
    lead_vals = joined[:, :lead_count]
    gate_low = joined[:, lead_count:].astype(jnp.bfloat16).reshape(tile_rows, tile_cols, gate_count)
    gate_ext = extended(gate_low, (("row", 0), ("col", 1)), 3)
    gate_ext = gate_ext * edge_mask
    kernel = conv_kernel.astype(jnp.float32)
    spread = depthwise(gate_ext, kernel, tile_rows, tile_cols).reshape(pixels, gate_count)
    parts = [spread[:, bounds[section] : bounds[section + 1]] for section in range(5)]
    mixed = lead_vals * parts[0]
    kept_low = []
    kept_products = []
    for section, weight in enumerate(mixes):
        mixed_low = mixed.astype(jnp.bfloat16)
        kept_low.append(mixed_low)
        produced = matmul(mixed_low, weight)
        kept_products.append(produced)
        mixed = produced * parts[section + 1]
    last_low = mixed.astype(jnp.bfloat16)
    branch = matmul(last_low, out_weight)
    scale_one = scale_mixer.astype(jnp.float32)
    middle = inputs + scale_one * branch
    normed_two, normal_two, inverse_two = norm_forward(
        middle, gain_two, shift_second.astype(jnp.float32), validity
    )
    normed_two_low = normed_two.astype(jnp.bfloat16)
    pre_act = matmul(normed_two_low, up_weight) + up_bias.astype(jnp.float32)
    active_low = jax.nn.gelu(pre_act, approximate=False).astype(jnp.bfloat16)
    down_proj = matmul(active_low, down_weight)
    scale_two = scale_mlp.astype(jnp.float32)
    outputs = (
        (middle + scale_two * down_proj)
        .astype(jnp.bfloat16)
        .reshape(tile_rows, tile_cols, channels)
    )
    grad_out = cotangent.reshape(pixels, channels).astype(jnp.float32)
    grad_scale_mlp = jnp.sum(grad_out * down_proj, axis=0)
    grad_down_low = (grad_out * scale_two).astype(jnp.bfloat16)
    grad_down_weight = inner_left(active_low, grad_down_low)
    grad_active = inner_right(grad_down_low, down_weight)
    unused_value, gelu_pull = jax.vjp(partial(jax.nn.gelu, approximate=False), pre_act)
    grad_pre_low = gelu_pull(grad_active)[0].astype(jnp.bfloat16)
    grad_up_bias = jnp.sum(grad_pre_low.astype(jnp.float32), axis=0)
    grad_up_weight = inner_left(normed_two_low, grad_pre_low)
    grad_normed_two = inner_right(grad_pre_low, up_weight)
    grad_mid_part, grad_gain_second, grad_shift_second = norm_backward(
        grad_normed_two, normal_two, inverse_two, gain_two, validity
    )
    grad_middle = grad_out + grad_mid_part
    (
        grad_gain_second,
        grad_shift_second,
        grad_up_weight,
        grad_up_bias,
        grad_down_weight,
        grad_scale_mlp,
    ) = lax.psum(
        (
            grad_gain_second,
            grad_shift_second,
            grad_up_weight,
            grad_up_bias,
            grad_down_weight,
            grad_scale_mlp,
        ),
        ("row", "col"),
    )
    grad_scale_mixer = jnp.sum(grad_middle * branch, axis=0)
    grad_branch_low = (grad_middle * scale_one).astype(jnp.bfloat16)
    grad_out_weight = inner_left(last_low, grad_branch_low)
    grad_mixed = inner_right(grad_branch_low, out_weight)
    grad_parts = [None] * 5
    grad_mixes = [None] * 4
    for section in (3, 2, 1, 0):
        grad_parts[section + 1] = grad_mixed * kept_products[section]
        grad_product_low = (grad_mixed * parts[section + 1]).astype(jnp.bfloat16)
        grad_mixes[section] = inner_left(kept_low[section], grad_product_low)
        grad_mixed = inner_right(grad_product_low, mixes[section])
    grad_parts[0] = grad_mixed * lead_vals
    grad_lead = grad_mixed * parts[0]
    grad_spread_low = (
        jnp.concatenate(grad_parts, axis=1)
        .astype(jnp.bfloat16)
        .reshape(tile_rows, tile_cols, gate_count)
    )
    grad_ext = extended(grad_spread_low, (("row", 0), ("col", 1)), 3) * edge_mask
    grad_spread = grad_spread_low.astype(jnp.float32)
    kernel_rows = []
    for row_off in range(7):
        kernel_cols = []
        for col_off in range(7):
            kernel_cols.append(
                jnp.sum(
                    grad_spread
                    * gate_ext[row_off : row_off + tile_rows, col_off : col_off + tile_cols],
                    axis=(0, 1),
                )
            )
        kernel_rows.append(jnp.stack(kernel_cols))
    grad_kernel = DW_SCALE * jnp.stack(kernel_rows)
    grad_gates = depthwise(grad_ext, kernel[::-1, ::-1], tile_rows, tile_cols).reshape(
        pixels, gate_count
    )
    grad_joined_low = jnp.concatenate([grad_lead, grad_gates], axis=1).astype(jnp.bfloat16)
    grad_in_weight = inner_left(normed_low, grad_joined_low)
    grad_normed_one = inner_right(grad_joined_low, in_weight)
    grad_in_part, grad_gain_first, grad_shift_first = norm_backward(
        grad_normed_one, normal_one, inverse_one, gain_one, validity
    )
    grad_input = (
        (grad_middle + grad_in_part).astype(jnp.bfloat16).reshape(tile_rows, tile_cols, channels)
    )
    (
        grad_gain_first,
        grad_shift_first,
        grad_in_weight,
        grad_kernel,
        grad_mix_one,
        grad_mix_two,
        grad_mix_three,
        grad_mix_four,
        grad_out_weight,
        grad_scale_mixer,
    ) = lax.psum(
        (
            grad_gain_first,
            grad_shift_first,
            grad_in_weight,
            grad_kernel,
            grad_mixes[0],
            grad_mixes[1],
            grad_mixes[2],
            grad_mixes[3],
            grad_out_weight,
            grad_scale_mixer,
        ),
        ("row", "col"),
    )
    return (
        outputs,
        grad_input,
        grad_gain_first,
        grad_shift_first,
        grad_in_weight,
        grad_kernel,
        grad_mix_one,
        grad_mix_two,
        grad_mix_three,
        grad_mix_four,
        grad_out_weight,
        grad_scale_mixer,
        grad_gain_second,
        grad_shift_second,
        grad_up_weight,
        grad_up_bias,
        grad_down_weight,
        grad_scale_mlp,
    )


def solution(mesh):
    in_specs = (
        P("row", "col", None),
        P(),
        P(),
        P(),
        P(),
        P(),
        P(),
        P(),
        P(),
        P(),
        P(),
        P(),
        P(),
        P(),
        P(),
        P(),
        P(),
        P("row", "col"),
        P(),
        P("row", "col", None),
    )
    out_specs = (
        P("row", "col", None),
        P("row", "col", None),
        P(),
        P(),
        P(),
        P(),
        P(),
        P(),
        P(),
        P(),
        P(),
        P(),
        P(),
        P(),
        P(),
        P(),
        P(),
        P(),
    )
    return jax.shard_map(
        on_device, mesh=mesh, in_specs=in_specs, out_specs=out_specs, check_vma=False
    )
```

profile of v0, /device:TPU:0, one launch (start us, length us, event | category | flops | bytes accessed | tf_op | source)
XLA Modules:
  0.0 598.3 jit_solution(16646248807610418962)
XLA Ops:
  7.3 1.7 convert_reduce_fusion.1
  9.1 1.9 fusion.107
  14.4 2.6 fusion.115
  17.0 5.6 fusion.153
  22.6 1.5 copy-done.10
  26.4 6.2 %collective-permute-start = (bf16[3,40,992]{2,1,0:T(8,128)(2,1)}, bf16[3,40,992]{2,1,0:T(8,128)(2,1)}, u32[]{:S(2)}, u32[]{:S(2)}) collective-permute-start(bf16[3,40,992]{2,1,0:T(8,128)(2,1)} %bitcast.2), channel_id=1, source_target_pairs={{0,8},{8,16},{16,24},{1,9},{9,17},{17,25},{2,10},{10,18},{18,26},{... | collective-permute-start | bytes 714248 | tf_op jit(solution)/shard_map/ppermute | solution.py:17
  37.6 2.0 fusion.104
  39.6 1.8 convolution_convert_fusion
  41.4 4.7 slice.821
  50.0 1.8 pad_maximum_fusion.8
  51.9 1.5 collective-permute-start.2
  53.3 1.8 collective-permute-start.3
  55.9 3.1 collective-permute-done.3
  59.0 5.5 maximum_multiply_fusion
  64.9 40.2 %fusion.103 = f32[32,40,992]{2,1,0:T(8,128)S(1)} fusion(f32[992]{0:T(1024)S(1)} %bitcast.255, f32[992]{0:T(1024)S(1)} %bitcast.253, f32[992]{0:T(1024)S(1)} %bitcast.251, f32[992]{0:T(1024)S(1)} %bitcast.249, f32[992]{0:T(1024)S(1)} %bitcast.247, f32[992]{0:T(1024)S(1)} %bitcast.245, f32[992]{0:T(1024)S(1)} %bitcast.243, f32[992]{0:T(1024)S(1)} %bitcast.241, ...), kind=kLoop, calls=%fused_computation.216 | loop fusion | flops 186654720 | bytes 129709952 | tf_op jit(solution)/shard_map/mul | solution.py:94
  106.1 1.5 copy-done.5
  110.5 3.3 multiply_convert_fusion.12
  113.8 2.1 multiply_convert_fusion.9
  116.9 2.4 fusion.147
  119.9 27.9 %multiply_convert_fusion = (bf16[1280,2048]{1,0:T(8,128)(2,1)}, f32[1280,2048]{1,0:T(8,128)}, f32[1280,2048]{1,0:T(8,128)}) fusion(f32[2048]{0:T(1024)S(1)} %copy-done.139, bf16[512,2048]{1,0:T(8,128)(2,1)S(1)} %copy-done, f32[1280,512]{1,0:T(8,128)S(1)} %get-tuple-element.96, f32[512]{0:T(512)S(1)} %copy-done.143, f32[512]{0:T(512)S(1)} %copy-done.142, ...), kind=kOutput, calls=%fused_computation.55 | convolution fusion | flops 2861301760 | bytes 30960640 | tf_op jit(solution)/shard_map/dot_general | solution.py:26
  147.8 12.7 %convert_reduce_fusion = (f32[2048]{0:T(1024)S(1)}, bf16[1280,2048]{1,0:T(8,128)(2,1)}) fusion(f32[1280,2048]{1,0:T(8,128)} %get-tuple-element.94, bf16[1280,512]{1,0:T(8,128)(2,1)S(1)} %copy-done.38, bf16[2048,512]{1,0:T(8,128)(2,1)} %param.35, f32[1280,2048]{1,0:T(8,128)} %get-tuple-element.179, f32[2048]{0:T(1024)S(1)} %copy-done.139), kind=kOutput, calls=%fused_computation.53 | convolution fusion | flops 2728916992 | bytes 29638656 | tf_op jit(solution)/shard_map/dot_general | solution.py:36
  160.5 6.1 %multiply_reduce_fusion = (f32[512]{0:T(512)S(1)}, f32[1280]{0:T(1024)S(1)}, f32[1280]{0:T(1024)S(1)}, f32[512]{0:T(512)S(1)}, f32[1280,512]{1,0:T(8,128)S(1)}) fusion(f32[1280,512]{1,0:T(8,128)S(1)} %get-tuple-element.96, f32[1280]{0:T(1024)S(1)} %add_rsqrt_fusion.1, f32[1280]{0:T(1024)S(1)} %broadcast_multiply_fusion.6, f32[512]{0:T(512)S(1)} %copy-done.142, ...), kind=kOutput, calls=%fused_computation.247 | convolution fusion | flops 2690904576 | bytes 12614656 | tf_op jit(solution)/shard_map/dot_general | solution.py:36
  166.6 5.4 fusion.144
  172.1 4.5 fusion.158
  176.6 5.1 fusion.105
  181.8 1.9 fusion.125
  190.4 5.5 concatenate.42
  195.9 22.1 %fusion.100 = (f32[992]{0:T(1024)S(1)}, f32[992]{0:T(1024)S(1)}, f32[992]{0:T(1024)S(1)}, f32[992]{0:T(1024)S(1)}, f32[992]{0:T(1024)S(1)}, /*index=5*/f32[992]{...) fusion(bf16[32,40,992]{2,1,0:T(8,128)(2,1)} %concatenate.42, ...), kind=kLoop, calls=%fused_computation.212 | loop fusion | flops 50777504 | bytes 35604864 | tf_op jit(solution)/shard_map/reduce_sum | solution.py:228
  218.0 16.3 %fusion.102 = (f32[992]{0:T(1024)S(1)}, f32[992]{0:T(1024)S(1)}, f32[992]{0:T(1024)S(1)}, f32[992]{0:T(1024)S(1)}, f32[992]{0:T(1024)S(1)}, /*index=5*/f32[992]{...) fusion(bf16[32,40,992]{2,1,0:T(8,128)(2,1)S(1)} %copy-done.4, ...), kind=kLoop, calls=%fused_computation.214 | loop fusion | flops 69818944 | bytes 48322304 | tf_op jit(solution)/shard_map/reduce_sum | solution.py:228
  234.3 16.3 %fusion.101 = (f32[992]{0:T(1024)S(1)}, f32[992]{0:T(1024)S(1)}, f32[992]{0:T(1024)S(1)}, f32[992]{0:T(1024)S(1)}, f32[992]{0:T(1024)S(1)}, /*index=5*/f32[992]{...) fusion(bf16[32,40,992]{2,1,0:T(8,128)(2,1)S(1)} %copy-done.4, ...), kind=kLoop, calls=%fused_computation.213 | loop fusion | flops 69818944 | bytes 48322304 | tf_op jit(solution)/shard_map/reduce_sum | solution.py:228
  250.6 5.4 concatenate.36
  258.4 4.6 collective-permute-start.4
  268.1 6.9 %collective-permute-start.6 = (bf16[38,3,992]{2,1,0:T(4,128)(2,1)S(1)}, bf16[38,3,992]{2,1,0:T(4,128)(2,1)S(1)}, u32[]{:S(2)}, u32[]{:S(2)}) collective-permute-start(bf16[38,3,992]{2,1,0:T(4,128)(2,1)S(1)} %get-tuple-element.97), channel_id=1, source_target_pairs={{0,1},{1,2},{2,3},{3,4},{4,5},{5,6},{6,7},{8,9},{9,10},{10,11},{11... | collective-permute-start | bytes 678536 | tf_op jit(solution)/shard_map/ppermute | solution.py:17
  277.1 3.1 collective-permute-done.7
  280.2 5.8 maximum_multiply_fusion.1
  286.3 39.4 %multiply_convert_fusion.1 = bf16[32,40,992]{2,1,0:T(8,128)(2,1)S(1)} fusion(bf16[38,46,992]{2,1,0:T(8,128)(2,1)S(1)} %maximum_multiply_fusion.1, f32[992]{0:T(1024)S(1)} %bitcast.256, f32[992]{0:T(1024)S(1)} %bitcast.254, f32[992]{0:T(1024)S(1)} %bitcast.252, f32[992]{0:T(1024)S(1)} %bitcast.250, f32[992]{0:T(1024)S(1)} %bitcast.248, ...), kind=kLoop, calls=%fused_computation.215 | loop fusion | flops 187924480 | bytes 127170432 | tf_op jit(solution)/shard_map/convert.4
  325.8 1.6 copy-done.26
  327.3 3.0 fusion.122
  332.2 5.7 fusion.121
  337.9 51.0 %all-reduce = (f32[512]{0:T(512)}, f32[512]{0:T(512)}, f32[32,64]{1,0:T(8,128)}, f32[64,128]{1,0:T(8,128)}, f32[512]{0:T(512)}, /*index=5*/f32[512]{0:T(512)}, f32[512]{0:T(512)}, f32[2048]{0:T(1024)}, f32[512]{0:T(512)}) all-reduce(f32[512]{0:T(512)S(1)} %get-tuple-element.69, ...), channel_id=1, replica_groups=mesh['row'=4,'col'=8] {'row','col'}, use_global_device_ids=true, to_apply=%region_9.10 | all-reduce | flops 15360 | bytes 122880 | tf_op jit(solution)/shard_map/psum | solution.py:259
  388.9 4.0 fusion.120
  393.0 183.8 %all-reduce.4.cloned.1.call-done = (f32[512,1024]{1,0:T(8,128)}, f32[7,7,992]{2,1,0:T(8,128)}, f32[128,256]{1,0:T(8,128)}, f32[256,512]{1,0:T(8,128)}, f32[512,5...) async-done(((f32[512,1024]{1,0:T(8,128)}, f32[7,7,992]{2,1,0:T(8,128)}, f32[128,256]{1,0:T(8,128)}, f32[256,512]{1,0:T(8,128)}, f32[512,512]{1,0:T(8,128)}, ...) | async-done | bytes 12384144 | tf_op jit(solution)/shard_map/psum | solution.py:259
  576.8 3.3 copy.98
  580.1 1.6 copy.99
  581.8 1.6 copy.100
  583.3 1.9 copy.101
  586.2 2.1 copy.103
  589.3 2.0 copy.104
  (381 shorter events, 40.2 us)
Async XLA Ops:
  7.2 112.6 %copy-start = (bf16[512,2048]{1,0:T(8,128)(2,1)S(1)}, bf16[512,2048]{1,0:T(8,128)(2,1)}, u32[]{:S(2)}) copy-start(bf16[512,2048]{1,0:T(8,128)(2,1)} %param.33) | copy-start | bytes 6291460
  7.2 569.6 %all-reduce.4.cloned.1.call-start = ((), (), s32[]{:S(2)}) async-start(), calls=%async_computation | async-start | bytes 24838144 | tf_op jit(solution)/shard_map/psum | solution.py:259
  25.1 24.9 %collective-permute-start.1 = (bf16[3,40,992]{2,1,0:T(8,128)(2,1)}, bf16[3,40,992]{2,1,0:T(8,128)(2,1)}, u32[]{:S(2)}, u32[]{:S(2)}) collective-permute-start(bf16[3,40,992]{2,1,0:T(8,128)(2,1)} %bitcast.4), channel_id=1, source_target_pairs={{8,0},{16,8},{24,16},{9,1},{17,9},{25,17},{10,2},{18,10},{26,18},{... | collective-permute-start | bytes 714248 | tf_op jit(solution)/shard_map/ppermute | solution.py:20
  26.4 23.6 %collective-permute-start = (bf16[3,40,992]{2,1,0:T(8,128)(2,1)}, bf16[3,40,992]{2,1,0:T(8,128)(2,1)}, u32[]{:S(2)}, u32[]{:S(2)}) collective-permute-start(bf16[3,40,992]{2,1,0:T(8,128)(2,1)} %bitcast.2), channel_id=1, source_target_pairs={{0,8},{8,16},{16,24},{1,9},{9,17},{17,25},{2,10},{10,18},{18,26},{... | collective-permute-start | bytes 714248 | tf_op jit(solution)/shard_map/ppermute | solution.py:17
  35.6 29.0 %copy-start.55 = (f32[1,1,992]{2,1,0:T(1,128)}, f32[1,1,992]{2,1,0:T(1,128)S(1)}, u32[]{:S(2)}) copy-start(f32[1,1,992]{2,1,0:T(1,128)S(1)} %get-tuple-element.157) | copy-start | bytes 11908
  35.6 29.0 %copy-start.57 = (f32[1,1,992]{2,1,0:T(1,128)}, f32[1,1,992]{2,1,0:T(1,128)S(1)}, u32[]{:S(2)}) copy-start(f32[1,1,992]{2,1,0:T(1,128)S(1)} %get-tuple-element.158) | copy-start | bytes 11908
  35.6 29.0 %copy-start.59 = (f32[1,1,992]{2,1,0:T(1,128)}, f32[1,1,992]{2,1,0:T(1,128)S(1)}, u32[]{:S(2)}) copy-start(f32[1,1,992]{2,1,0:T(1,128)S(1)} %get-tuple-element.159) | copy-start | bytes 11908
  35.6 29.0 %copy-start.61 = (f32[1,1,992]{2,1,0:T(1,128)}, f32[1,1,992]{2,1,0:T(1,128)S(1)}, u32[]{:S(2)}) copy-start(f32[1,1,992]{2,1,0:T(1,128)S(1)} %get-tuple-element.160) | copy-start | bytes 11908
  35.6 29.0 %copy-start.63 = (f32[1,1,992]{2,1,0:T(1,128)}, f32[1,1,992]{2,1,0:T(1,128)S(1)}, u32[]{:S(2)}) copy-start(f32[1,1,992]{2,1,0:T(1,128)S(1)} %get-tuple-element.161) | copy-start | bytes 11908
  35.6 29.0 %copy-start.65 = (f32[1,1,992]{2,1,0:T(1,128)}, f32[1,1,992]{2,1,0:T(1,128)S(1)}, u32[]{:S(2)}) copy-start(f32[1,1,992]{2,1,0:T(1,128)S(1)} %get-tuple-element.162) | copy-start | bytes 11908
  49.7 59.7 %copy-start.31 = (f32[1280,32]{0,1:T(8,128)}, f32[1280,32]{0,1:T(8,128)S(1)}, u32[]{:S(2)}) copy-start(f32[1280,32]{0,1:T(8,128)S(1)} %copy.82) | copy-start | bytes 491524
  51.9 4.0 collective-permute-start.2
  53.3 5.6 collective-permute-start.3
  55.8 49.3 %copy-start.115 = (f32[1,1,992]{2,1,0:T(1,128)}, f32[1,1,992]{2,1,0:T(1,128)S(1)}, u32[]{:S(2)}) copy-start(f32[1,1,992]{2,1,0:T(1,128)S(1)} %get-tuple-element.119) | copy-start | bytes 11908
  55.8 49.3 %copy-start.117 = (f32[1,1,992]{2,1,0:T(1,128)}, f32[1,1,992]{2,1,0:T(1,128)S(1)}, u32[]{:S(2)}) copy-start(f32[1,1,992]{2,1,0:T(1,128)S(1)} %get-tuple-element.120) | copy-start | bytes 11908
  55.8 49.3 %copy-start.119 = (f32[1,1,992]{2,1,0:T(1,128)}, f32[1,1,992]{2,1,0:T(1,128)S(1)}, u32[]{:S(2)}) copy-start(f32[1,1,992]{2,1,0:T(1,128)S(1)} %get-tuple-element.121) | copy-start | bytes 11908
  55.8 49.3 %copy-start.121 = (f32[1,1,992]{2,1,0:T(1,128)}, f32[1,1,992]{2,1,0:T(1,128)S(1)}, u32[]{:S(2)}) copy-start(f32[1,1,992]{2,1,0:T(1,128)S(1)} %get-tuple-element.122) | copy-start | bytes 11908
  55.8 49.3 %copy-start.123 = (f32[1,1,992]{2,1,0:T(1,128)}, f32[1,1,992]{2,1,0:T(1,128)S(1)}, u32[]{:S(2)}) copy-start(f32[1,1,992]{2,1,0:T(1,128)S(1)} %get-tuple-element.123) | copy-start | bytes 11908
  55.8 49.3 %copy-start.125 = (f32[1,1,992]{2,1,0:T(1,128)}, f32[1,1,992]{2,1,0:T(1,128)S(1)}, u32[]{:S(2)}) copy-start(f32[1,1,992]{2,1,0:T(1,128)S(1)} %get-tuple-element.124) | copy-start | bytes 11908
  55.8 49.3 %copy-start.127 = (f32[1,1,992]{2,1,0:T(1,128)}, f32[1,1,992]{2,1,0:T(1,128)S(1)}, u32[]{:S(2)}) copy-start(f32[1,1,992]{2,1,0:T(1,128)S(1)} %get-tuple-element.125) | copy-start | bytes 11908
  55.8 49.3 %copy-start.129 = (f32[1,1,992]{2,1,0:T(1,128)}, f32[1,1,992]{2,1,0:T(1,128)S(1)}, u32[]{:S(2)}) copy-start(f32[1,1,992]{2,1,0:T(1,128)S(1)} %get-tuple-element.126) | copy-start | bytes 11908
  55.8 49.3 %copy-start.131 = (f32[1,1,992]{2,1,0:T(1,128)}, f32[1,1,992]{2,1,0:T(1,128)S(1)}, u32[]{:S(2)}) copy-start(f32[1,1,992]{2,1,0:T(1,128)S(1)} %get-tuple-element.127) | copy-start | bytes 11908
  55.8 49.3 %copy-start.132 = (f32[1,1,992]{2,1,0:T(1,128)}, f32[1,1,992]{2,1,0:T(1,128)S(1)}, u32[]{:S(2)}) copy-start(f32[1,1,992]{2,1,0:T(1,128)S(1)} %get-tuple-element.128) | copy-start | bytes 11908
  64.5 40.6 %copy-start.2 = (bf16[38,46,992]{2,1,0:T(8,128)(2,1)}, bf16[38,46,992]{2,1,0:T(8,128)(2,1)S(1)}, u32[]{:S(2)}) copy-start(bf16[38,46,992]{2,1,0:T(8,128)(2,1)S(1)} %maximum_multiply_fusion) | copy-start | bytes 10404100
  64.8 44.7 %copy-start.133 = (bf16[32,64]{1,0:T(8,128)(2,1)S(1)}, bf16[32,64]{1,0:T(8,128)(2,1)}, u32[]{:S(2)}) copy-start(bf16[32,64]{1,0:T(8,128)(2,1)} %param.25) | copy-start | bytes 12292
  119.9 27.9 %copy-start.38 = (bf16[1280,512]{1,0:T(8,128)(2,1)S(1)}, bf16[1280,512]{1,0:T(8,128)(2,1)}, u32[]{:S(2)}) copy-start(bf16[1280,512]{1,0:T(8,128)(2,1)} %fusion.104) | copy-start | bytes 3932164
  189.5 28.5 %copy-start.21 = (bf16[1280,128]{1,0:T(8,128)(2,1)}, bf16[1280,128]{1,0:T(8,128)(2,1)S(1)}, u32[]{:S(2)}) copy-start(bf16[1280,128]{1,0:T(8,128)(2,1)S(1)} %get-tuple-element.114) | copy-start | bytes 983044
  250.6 29.6 %copy-start.54 = (bf16[38,46]{1,0:T(8,128)(2,1)S(1)}, bf16[38,46]{1,0:T(8,128)(2,1)}, u32[]{:S(2)}) copy-start(bf16[38,46]{1,0:T(8,128)(2,1)} %copy-done.53) | copy-start | bytes 10492
  257.1 8.1 %collective-permute-start.5 = (bf16[3,40,992]{2,1,0:T(8,128)(2,1)S(1)}, bf16[3,40,992]{2,1,0:T(8,128)(2,1)S(1)}, u32[]{:S(2)}, u32[]{:S(2)}) collective-permute-start(bf16[3,40,992]{2,1,0:T(8,128)(2,1)S(1)} %bitcast.234), channel_id=1, source_target_pairs={{8,0},{16,8},{24,16},{9,1},{17,9},{25,17},{10,2},{18,10},{26,18},{... | collective-permute-start | bytes 714248 | tf_op jit(solution)/shard_map/ppermute | solution.py:20
  258.4 8.3 %collective-permute-start.4 = (bf16[3,40,992]{2,1,0:T(8,128)(2,1)S(1)}, bf16[3,40,992]{2,1,0:T(8,128)(2,1)S(1)}, u32[]{:S(2)}, u32[]{:S(2)}) collective-permute-start(bf16[3,40,992]{2,1,0:T(8,128)(2,1)S(1)} %bitcast.233), channel_id=1, source_target_pairs={{0,8},{8,16},{16,24},{1,9},{9,17},{17,25},{2,10},{10,18},{18,26},{... | collective-permute-start | bytes 714248 | tf_op jit(solution)/shard_map/ppermute | solution.py:17
  263.6 22.3 %copy-start.56 = (f32[1,1,992]{2,1,0:T(1,128)S(1)}, f32[1,1,992]{2,1,0:T(1,128)}, u32[]{:S(2)}) copy-start(f32[1,1,992]{2,1,0:T(1,128)} %copy-done.55) | copy-start | bytes 11908
  263.6 22.3 %copy-start.58 = (f32[1,1,992]{2,1,0:T(1,128)S(1)}, f32[1,1,992]{2,1,0:T(1,128)}, u32[]{:S(2)}) copy-start(f32[1,1,992]{2,1,0:T(1,128)} %copy-done.57) | copy-start | bytes 11908
  263.6 22.3 %copy-start.60 = (f32[1,1,992]{2,1,0:T(1,128)S(1)}, f32[1,1,992]{2,1,0:T(1,128)}, u32[]{:S(2)}) copy-start(f32[1,1,992]{2,1,0:T(1,128)} %copy-done.59) | copy-start | bytes 11908
  263.7 22.3 %copy-start.62 = (f32[1,1,992]{2,1,0:T(1,128)S(1)}, f32[1,1,992]{2,1,0:T(1,128)}, u32[]{:S(2)}) copy-start(f32[1,1,992]{2,1,0:T(1,128)} %copy-done.61) | copy-start | bytes 11908
  263.7 22.3 %copy-start.64 = (f32[1,1,992]{2,1,0:T(1,128)S(1)}, f32[1,1,992]{2,1,0:T(1,128)}, u32[]{:S(2)}) copy-start(f32[1,1,992]{2,1,0:T(1,128)} %copy-done.63) | copy-start | bytes 11908
  263.7 22.3 %copy-start.66 = (f32[1,1,992]{2,1,0:T(1,128)S(1)}, f32[1,1,992]{2,1,0:T(1,128)}, u32[]{:S(2)}) copy-start(f32[1,1,992]{2,1,0:T(1,128)} %copy-done.65) | copy-start | bytes 11908
  263.7 22.3 %copy-start.68 = (f32[1,1,992]{2,1,0:T(1,128)S(1)}, f32[1,1,992]{2,1,0:T(1,128)}, u32[]{:S(2)}) copy-start(f32[1,1,992]{2,1,0:T(1,128)} %get-tuple-element.163) | copy-start | bytes 11908
  263.7 22.3 %copy-start.70 = (f32[1,1,992]{2,1,0:T(1,128)S(1)}, f32[1,1,992]{2,1,0:T(1,128)}, u32[]{:S(2)}) copy-start(f32[1,1,992]{2,1,0:T(1,128)} %get-tuple-element.164) | copy-start | bytes 11908
  263.7 22.3 %copy-start.72 = (f32[1,1,992]{2,1,0:T(1,128)S(1)}, f32[1,1,992]{2,1,0:T(1,128)}, u32[]{:S(2)}) copy-start(f32[1,1,992]{2,1,0:T(1,128)} %get-tuple-element.165) | copy-start | bytes 11908
  263.7 22.3 %copy-start.74 = (f32[1,1,992]{2,1,0:T(1,128)S(1)}, f32[1,1,992]{2,1,0:T(1,128)}, u32[]{:S(2)}) copy-start(f32[1,1,992]{2,1,0:T(1,128)} %get-tuple-element.166) | copy-start | bytes 11908
  263.7 22.3 %copy-start.76 = (f32[1,1,992]{2,1,0:T(1,128)S(1)}, f32[1,1,992]{2,1,0:T(1,128)}, u32[]{:S(2)}) copy-start(f32[1,1,992]{2,1,0:T(1,128)} %get-tuple-element.167) | copy-start | bytes 11908
  263.7 22.3 %copy-start.78 = (f32[1,1,992]{2,1,0:T(1,128)S(1)}, f32[1,1,992]{2,1,0:T(1,128)}, u32[]{:S(2)}) copy-start(f32[1,1,992]{2,1,0:T(1,128)} %copy-done.77) | copy-start | bytes 11908
  263.8 22.3 %copy-start.80 = (f32[1,1,992]{2,1,0:T(1,128)S(1)}, f32[1,1,992]{2,1,0:T(1,128)}, u32[]{:S(2)}) copy-start(f32[1,1,992]{2,1,0:T(1,128)} %copy-done.79) | copy-start | bytes 11908
  263.8 22.3 %copy-start.82 = (f32[1,1,992]{2,1,0:T(1,128)S(1)}, f32[1,1,992]{2,1,0:T(1,128)}, u32[]{:S(2)}) copy-start(f32[1,1,992]{2,1,0:T(1,128)} %copy-done.81) | copy-start | bytes 11908
  263.8 22.3 %copy-start.84 = (f32[1,1,992]{2,1,0:T(1,128)S(1)}, f32[1,1,992]{2,1,0:T(1,128)}, u32[]{:S(2)}) copy-start(f32[1,1,992]{2,1,0:T(1,128)} %copy-done.83) | copy-start | bytes 11908
  268.1 9.0 %collective-permute-start.6 = (bf16[38,3,992]{2,1,0:T(4,128)(2,1)S(1)}, bf16[38,3,992]{2,1,0:T(4,128)(2,1)S(1)}, u32[]{:S(2)}, u32[]{:S(2)}) collective-permute-start(bf16[38,3,992]{2,1,0:T(4,128)(2,1)S(1)} %get-tuple-element.97), channel_id=1, source_target_pairs={{0,1},{1,2},{2,3},{3,4},{4,5},{5,6},{6,7},{8,9},{9,10},{10,11},{11... | collective-permute-start | bytes 678536 | tf_op jit(solution)/shard_map/ppermute | solution.py:17
  275.1 5.1 collective-permute-start.7
  286.3 41.0 %copy-start.13 = (bf16[1280,512]{1,0:T(8,128)(2,1)S(1)}, bf16[1280,512]{1,0:T(8,128)(2,1)}, u32[]{:S(2)}) copy-start(bf16[1280,512]{1,0:T(8,128)(2,1)} %copy-done.12) | copy-start | bytes 3932164
  (112 other events, 1254.5 us)
Sparse Core Ops, SparseCore 0:
  330.6 246.1 all-reduce.3
where the time goes:
time: 605 us; the launch traced here: 598 us
  waiting for transfers between devices  193 us (32%)
  other arithmetic  168 us (28%)
  matrix products  95.8 us (16%)
  blocking collectives  51 us (8%)
  local copies, waits for them, and re-layouts  49.1 us (8%)
  starting transfers between devices  24.8 us (4%)
  between operations  16.4 us (3%)
    psum x1, waiting for transfers between devices, on_device(): lax.psum((grad_gain_first, grad_shift_first, grad_in_weight, grad_kernel,...  184 us
    reduce_sum x3, other arithmetic, on_device(): jnp.sum(grad_spread * gate_ext[row_off:row_off + tile_rows, col_off:col_o...  54.6 us
    psum x1, blocking collectives, on_device(): lax.psum((grad_gain_first, grad_shift_first, grad_in_weight, grad_kernel,...  51 us
    dot_general x8, matrix products, matmul(): return jnp.dot(left, right, preferred_element_type=jnp.float32)  48.2 us
    mul x1, other arithmetic, depthwise(): return DW_SCALE * summed  40.2 us
    another operation x1, other arithmetic  39.4 us
    dot_general x8, matrix products, inner_right(): lax.dot_general(left, right, (((1,), (1,)), ((), ())), preferred_element_...  28.4 us
    unnamed x318, local copies, waits for them, and re-layouts  24 us
  transfers between devices with their start and end apart: 9, of which 5 were waited for; matrix products, arithmetic and copies ran while one was open for 5% of the time, Pallas kernels for 0%

commit v1 on v0

v1 whole, which is shorter than its diff:
```python
import math
from functools import partial

import jax
import jax.numpy as jnp
import ml_dtypes
import numpy as np
from jax import lax
from jax.experimental import pallas as pl
from jax.experimental.pallas import tpu as pltpu
from jax.sharding import PartitionSpec as P

EPS = 1e-06
TAPS = 7
HALO = 3
OUT = 8
WIN = OUT + TAPS - 1
PITCH = 16
SLOTS = 112
OUTSIDE = 64.0
COS_SCALE = 1.422015
SIN_SCALE = 1.818765
TILES = 5
LANES = 512
BF16 = jnp.bfloat16
F32 = jnp.float32


def frequencies():
    pairs, own, seen = [], [], set()
    for u in range(WIN):
        for v in range(WIN):
            if (u, v) in seen:
                continue
            twin = ((-u) % WIN, (-v) % WIN)
            seen.update([(u, v), twin])
            (own if twin == (u, v) else pairs).append((u, v))
    return np.array(pairs + own), np.array([2.0] * len(pairs) + [1.0] * len(own))


def angles(rows, cols, pitch):
    freq, _ = frequencies()
    a = np.arange(rows)[:, None]
    b = np.arange(pitch)[None, :]
    theta = 2 * np.pi * (freq[:, 0, None, None] * a + freq[:, 1, None, None] * b) / WIN
    live = np.broadcast_to(b < cols, (rows, pitch))
    cos = np.zeros((SLOTS, rows * pitch))
    sin = np.zeros((SLOTS, rows * pitch))
    cos[: len(freq)] = (np.cos(theta) * live).reshape(len(freq), -1)
    sin[: len(freq)] = (np.sin(theta) * live).reshape(len(freq), -1)
    return cos, sin


def tables():
    _, weight = frequencies()
    weight = np.concatenate([weight, np.zeros(SLOTS - len(weight))])[:, None]
    area = WIN * WIN

    def ahead(cos, sin):
        return np.concatenate([COS_SCALE * cos, -SIN_SCALE * sin])

    def back(cos, sin):
        return np.concatenate([weight * COS_SCALE * cos, -weight * SIN_SCALE * sin]).T

    window = angles(WIN, WIN, PITCH)
    tile = angles(OUT, OUT, OUT)
    cos, sin = angles(TAPS, TAPS, TAPS)
    third = 1.0 / 3.0
    spectrum = np.concatenate(
        [
            cos * (third / (area * COS_SCALE**2)),
            -sin * (third / (area * COS_SCALE * SIN_SCALE)),
            cos * (third / (area * SIN_SCALE**2)),
        ]
    )
    wide = weight * third / area
    kernel_back = np.concatenate(
        [
            wide * cos / COS_SCALE**2,
            wide * cos / SIN_SCALE**2,
            -wide * sin / (COS_SCALE * SIN_SCALE),
            wide * sin / (COS_SCALE * SIN_SCALE),
        ]
    ).T
    kernel_back = np.concatenate([kernel_back, np.zeros((7, 4 * SLOTS))])
    half = ml_dtypes.bfloat16
    return dict(
        window=ahead(*window).astype(half),
        tile=ahead(*tile).astype(half),
        window_back=back(*window).astype(half),
        tile_back=back(*tile).astype(half),
        spectrum=np.concatenate([spectrum, spectrum[:, ::-1]]).astype(np.float32),
        kernel_back=kernel_back.astype(np.float32),
    )


def dot(left, right):
    return jnp.dot(left, right, preferred_element_type=F32)


def dot_right(left, right):
    return lax.dot_general(left, right, (((1,), (1,)), ((), ())), preferred_element_type=F32)


def dot_left(left, right):
    return lax.dot_general(left, right, (((0,), (0,)), ((), ())), preferred_element_type=F32)


def normalize(values):
    center = values - jnp.mean(values, axis=-1, keepdims=True)
    inverse = lax.rsqrt(jnp.mean(center * center, axis=-1, keepdims=True) + EPS)
    return center * inverse, inverse


def norm_back(masked, normal, inverse, gain):
    scaled = masked * gain
    centered = scaled - jnp.mean(scaled, axis=-1, keepdims=True)
    return inverse * (centered - normal * jnp.mean(scaled * normal, axis=-1, keepdims=True))


def gelu_pair(x):
    cumulative = 0.5 + 0.5 * lax.erf(x * math.sqrt(0.5))
    density = jnp.exp(-0.5 * x * x) * (1.0 / math.sqrt(2.0 * math.pi))
    return x * cumulative, cumulative + x * density


def depthwise(ext, first_row, spec, tx, ty, waves, mixed_waves, result_ref, kept=None):
    span = 48

    def block_of_lanes(block, carry):
        lanes = pl.ds(pl.multiple_of(LANES * block, LANES), LANES)
        window = jnp.concatenate(
            [
                jnp.concatenate(
                    [
                        ext[pl.ds(pl.multiple_of((first_row + r) * span + OUT * col, 8), PITCH), lanes]
                        for r in range(WIN)
                    ],
                    axis=0,
                ).astype(BF16)
                for col in range(TILES)
            ],
            axis=1,
        )
        waves[...] = dot(tx[...], window)
        for row in range(0, SLOTS, 16):
            here, there = slice(row, row + 16), slice(SLOTS + row, SLOTS + row + 16)
            low, cross, high = (spec[pl.ds(SLOTS * k + row, 16), lanes] for k in range(3))
            for col in range(TILES):
                at = slice(LANES * col, LANES * col + LANES)
                real, imag = waves[here, at], waves[there, at]
                mixed_waves[here, at] = (low * real + cross * imag).astype(BF16)
                mixed_waves[there, at] = (high * imag - cross * real).astype(BF16)
                if kept is not None:
                    base = 2 * SLOTS * col + row
                    kept[base : base + 16, lanes] = real.astype(BF16)
                    kept[base + SLOTS : base + SLOTS + 16, lanes] = imag.astype(BF16)
        result = dot(ty[...], mixed_waves[...])
        for col in range(TILES):
            for r in range(OUT):
                result_ref[r * 40 + OUT * col : r * 40 + OUT * col + OUT, lanes] = result[
                    OUT * r : OUT * r + OUT, LANES * col : LANES * col + LANES
                ]
        return carry

    lax.fori_loop(0, 1024 // LANES, block_of_lanes, 0)


GAIN_1, SHIFT_1, SCALE_1, GAIN_2, SHIFT_2, SCALE_2 = range(6)


def forward_kernel(
    x_ext, x_own, valid, cot, vecs, up_bias, in_w, w1, w2, w3, w4, out_w, up_w, spec, tx, ty,
    waves_out, spread, prods, lead_out, middle_out, active_out, slope_out, grad_down,
    ext, waves, mixed_waves, active_all, gdown_all,
):
    step = pl.program_id(0)
    span = 48
    chunk = spread.shape[0]
    gain = vecs[GAIN_1 : GAIN_1 + 1, :]
    shift = vecs[SHIFT_1 : SHIFT_1 + 1, :]

    def project(start, rows):
        at = pl.ds(start, rows)
        values = x_ext[at, :].astype(F32)
        normal, _ = normalize(values)
        normed = jnp.where(values[:, :1] < 0.5 * OUTSIDE, normal * gain + shift, 0.0).astype(BF16)
        for block in range(2):
            lanes = slice(512 * block, 512 * block + 512)
            joined = dot(normed, in_w[:, lanes])
            if block == 0:
                ext[at, 1024:1152] = joined[:, :128]
            low = joined.astype(BF16)
            ext[at, lanes] = low.astype(F32)

    @pl.when(step == 0)
    def _():
        project(0, 6 * span)

    project(pl.multiple_of((OUT * step + 6) * span, 16), OUT * span)

    depthwise(ext, OUT * step, spec, tx, ty, waves, mixed_waves, spread, waves_out)

    lead = jnp.concatenate(
        [
            ext[pl.ds(pl.multiple_of((OUT * step + HALO + r) * span, 8), span), 1024:1152][HALO : HALO + 40]
            for r in range(OUT)
        ],
        axis=0,
    )
    lead = pltpu.roll(lead, 32, 1)
    lead_out[...] = lead
    mixed = lead * spread[:, :128]
    for weight, lo, hi in ((w1, 0, 128), (w2, 128, 256), (w3, 256, 512), (w4, 512, 1024)):
        produced = dot(mixed.astype(BF16), weight[...])
        prods[:, lo:hi] = produced
        mixed = produced * spread[:, lo:hi]
    branch = dot(mixed.astype(BF16), out_w[...])
    middle = x_own[...].astype(F32) + vecs[SCALE_1 : SCALE_1 + 1, :] * branch
    middle_out[...] = middle
    normal, _ = normalize(middle)
    normed = (
        (normal * vecs[GAIN_2 : GAIN_2 + 1, :] + vecs[SHIFT_2 : SHIFT_2 + 1, :]) * valid[...]
    ).astype(BF16)
    rows = pl.ds(pl.multiple_of(step * chunk, 16), chunk)
    for block in range(4):
        lanes = slice(512 * block, 512 * block + 512)
        pre = dot(normed, up_w[:, lanes]) + up_bias[:, lanes]
        active, slope = gelu_pair(pre)
        active = active.astype(BF16)
        active_out[:, lanes] = active
        active_all[rows, lanes] = active
        slope_out[:, lanes] = slope.astype(BF16)
    gdown_all[rows, :] = (cot[...].astype(F32) * vecs[SCALE_2 : SCALE_2 + 1, :]).astype(BF16)

    @pl.when(step == pl.num_programs(0) - 1)
    def _():
        for block in range(4):
            lanes = slice(512 * block, 512 * block + 512)
            grad_down[lanes, :] = dot_left(gdown_all[...], active_all[:, lanes]).astype(BF16)


def ffn_back_kernel(
    cot, slope, middle, valid, vecs, down_w, up_w, grad_down,
    gmiddle, sent, kept, vec_sums, bias_sum,
    normed_all, gpre_all,
):
    step = pl.program_id(0)
    chunk = cot.shape[0]
    rows = pl.ds(pl.multiple_of(step * chunk, 16), chunk)

    @pl.when(step == 0)
    def _():
        vec_sums[...] = jnp.zeros_like(vec_sums)
        bias_sum[...] = jnp.zeros_like(bias_sum)

    grad = cot[...].astype(F32)
    gdown = (grad * vecs[SCALE_2 : SCALE_2 + 1, :]).astype(BF16)
    gnormed = jnp.zeros((chunk, 512), F32)
    for block in range(4):
        lanes = slice(512 * block, 512 * block + 512)
        gactive = dot_right(gdown, down_w[lanes, :])
        gpre = (gactive * slope[:, lanes].astype(F32)).astype(BF16)
        gpre_all[rows, lanes] = gpre
        bias_sum[0:1, lanes] += jnp.sum(gpre.astype(F32), axis=0, keepdims=True)
        gnormed = gnormed + dot_right(gpre, up_w[:, lanes])
    normal, inverse = normalize(middle[...])
    gain = vecs[GAIN_2 : GAIN_2 + 1, :]
    mask = valid[...]
    normed_all[rows, :] = ((normal * gain + vecs[SHIFT_2 : SHIFT_2 + 1, :]) * mask).astype(BF16)
    masked = gnormed * mask
    vec_sums[0:1, :] += jnp.sum(masked * normal, axis=0, keepdims=True)
    vec_sums[1:2, :] += jnp.sum(masked, axis=0, keepdims=True)
    gmiddle[...] = grad + norm_back(masked, normal, inverse, gain)

    @pl.when(step == pl.num_programs(0) - 1)
    def _():
        def finish(for_up, for_down):
            for block in range(4):
                lanes = slice(512 * block, 512 * block + 512)
                for_up[lanes, :] = dot_left(normed_all[...], gpre_all[:, lanes]).astype(BF16)
            for_down[...] = grad_down[...]

        even = lax.axis_index("col") % 2 == 0
        pl.when(even)(lambda: finish(sent, kept))
        pl.when(jnp.logical_not(even))(lambda: finish(kept, sent))


def mixer_back_kernel(
    gmiddle, spread, prods, lead, vecs, w1, w2, w3, w4, out_w,
    gspread, glead, grads,
    d_out, d_4, d_3, d_2, d_1,
):
    step = pl.program_id(0)

    @pl.when(step == 0)
    def _():
        for total in (d_out, d_4, d_3, d_2, d_1):
            total[...] = jnp.zeros_like(total)

    grad = gmiddle[...]
    glow = (grad * vecs[SCALE_1 : SCALE_1 + 1, :]).astype(BF16)
    part, prod = spread[:, 512:1024], prods[:, 512:1024]
    d_out[...] += dot_left((prod * part).astype(BF16), glow)
    gmixed = dot_right(glow, out_w[...])
    for weight, total, lo, hi, below in (
        (w4, d_4, 512, 1024, 256), (w3, d_3, 256, 512, 128), (w2, d_2, 128, 256, 0)
    ):
        gspread[:, lo:hi] = (gmixed * prods[:, lo:hi]).astype(BF16)
        gprod = (gmixed * spread[:, lo:hi]).astype(BF16)
        mixed = (prods[:, below:lo] * spread[:, below:lo]).astype(BF16)
        total[...] += dot_left(mixed, gprod)
        gmixed = dot_right(gprod, weight[...])
    part, prod, head = spread[:, :128], prods[:, :128], lead[...]
    gprod = (gmixed * part).astype(BF16)
    d_1[...] += dot_left((head * part).astype(BF16), gprod)
    gfirst = dot_right(gprod, w1[...])
    gspread[:, :128] = (gmixed * prod + gfirst * head).astype(BF16)
    glead[...] = pltpu.roll(gfirst * part, 96, 1)

    @pl.when(step == pl.num_programs(0) - 1)
    def _():
        grads[0:512, :] = d_out[...].astype(BF16)
        grads[512:768, :] = d_4[...].astype(BF16)
        grads[768:896, 0:256] = d_3[...].astype(BF16)
        grads[768:896, 256:384] = d_2[...].astype(BF16)
        grads[768:896, 384:512] = d_1[...].astype(BF16)


def down_kernel(active, middle, vecs, down_w, before, outputs):
    down = dot(active[...], down_w[...])
    outputs[...] = (middle[...] + vecs[SCALE_2 : SCALE_2 + 1, :] * down).astype(BF16)


def kernel_back_kernel(xwaves, gspread, tg, td, out, gs, gwaves, total):
    step = pl.program_id(0)

    @pl.when(step == 0)
    def _():
        total[...] = jnp.zeros_like(total)

    gs[...] = gspread[...].astype(F32)

    def block_of_lanes(block, carry):
        lanes = pl.ds(pl.multiple_of(LANES * block, LANES), LANES)
        square = jnp.concatenate(
            [
                jnp.concatenate(
                    [gs[r * 40 + OUT * col : r * 40 + OUT * col + OUT, lanes] for r in range(OUT)], axis=0
                ).astype(BF16)
                for col in range(TILES)
            ],
            axis=1,
        )
        gwaves[...] = dot(tg[...], square)
        for row in range(0, SLOTS, 16):
            here, there = slice(row, row + 16), slice(SLOTS + row, SLOTS + row + 16)
            sums = [total[pl.ds(SLOTS * k + row, 16), lanes] for k in range(4)]
            for col in range(TILES):
                at = slice(LANES * col, LANES * col + LANES)
                base = 2 * SLOTS * col + row
                real = xwaves[base : base + 16, lanes].astype(F32)
                imag = xwaves[base + SLOTS : base + SLOTS + 16, lanes].astype(F32)
                greal, gimag = gwaves[here, at], gwaves[there, at]
                sums = [
                    sums[0] + greal * real, sums[1] + gimag * imag, sums[2] + greal * imag, sums[3] + gimag * real
                ]
            for k in range(4):
                total[pl.ds(SLOTS * k + row, 16), lanes] = sums[k]
        return carry

    lax.fori_loop(0, 1024 // LANES, block_of_lanes, 0)

    @pl.when(step == pl.num_programs(0) - 1)
    def _():
        taps = jnp.dot(
            td[...], total[...], preferred_element_type=F32, precision=lax.Precision.HIGHEST
        )
        out[...] = jnp.concatenate([taps[:, :512], taps[:, 512:]], axis=0).astype(BF16)


def gates_back_kernel(gs_ext, glead, spec, tx, ty, gjoined, ext, waves, mixed_waves, ggates):
    step = pl.program_id(0)
    span = 48

    def widen(start, count):
        at = pl.ds(start, count)
        ext[at, :] = gs_ext[at, :].astype(F32)

    @pl.when(step == 0)
    def _():
        widen(0, 6 * span)

    widen(pl.multiple_of((OUT * step + 6) * span, 16), OUT * span)
    depthwise(ext, OUT * step, spec, tx, ty, waves, mixed_waves, ggates)
    gjoined[:, :128] = (ggates[:, :128] + glead[...]).astype(BF16)
    gjoined[:, 128:] = ggates[:, 128:].astype(BF16)


def in_back_kernel(
    gjoined, x_own, gmiddle, valid, vecs, in_w, mixer_grads, grad_kernel, ffn_sums, bias_sum,
    ginput, sent, kept,
    normed_all, gjoined_all, vec_sums,
):
    step = pl.program_id(0)
    chunk = x_own.shape[0]
    rows = pl.ds(pl.multiple_of(step * chunk, 16), chunk)

    @pl.when(step == 0)
    def _():
        vec_sums[...] = jnp.zeros_like(vec_sums)

    gjoined_all[rows, :] = gjoined[...]
    gnormed = dot_right(gjoined[...], in_w[...])
    normal, inverse = normalize(x_own[...].astype(F32))
    gain = vecs[GAIN_1 : GAIN_1 + 1, :]
    mask = valid[...]
    normed_all[rows, :] = ((normal * gain + vecs[SHIFT_1 : SHIFT_1 + 1, :]) * mask).astype(BF16)
    masked = gnormed * mask
    vec_sums[0:1, :] += jnp.sum(masked * normal, axis=0, keepdims=True)
    vec_sums[1:2, :] += jnp.sum(masked, axis=0, keepdims=True)
    ginput[...] = (gmiddle[...] + norm_back(masked, normal, inverse, gain)).astype(BF16)

    @pl.when(step == pl.num_programs(0) - 1)
    def _():
        def finish(for_in, for_others):
            for block in range(2):
                lanes = slice(512 * block, 512 * block + 512)
                for_in[lanes, :] = dot_left(normed_all[...], gjoined_all[:, lanes]).astype(BF16)
            for_others[0:896, :] = mixer_grads[...]
            for_others[896:1008, :] = grad_kernel[...]
            pieces = [vec_sums[0:2, :], ffn_sums[0:2, :]]
            pieces += [bias_sum[0:1, 512 * k : 512 * k + 512] for k in range(4)]
            pieces.append(jnp.zeros((8, 512), F32))
            for_others[1008:1024, :] = jnp.concatenate(pieces, axis=0).astype(BF16)

        even = lax.axis_index("col") % 2 == 0
        pl.when(even)(lambda: finish(kept, sent))
        pl.when(jnp.logical_not(even))(lambda: finish(sent, kept))


def expand_ffn_kernel(own, got, down_w, vecs, grad_down, grad_up, grad_scale):
    step = pl.program_id(0)

    @pl.when(step == 0)
    def _():
        grad_scale[...] = jnp.zeros_like(grad_scale)

    def expand(down, up):
        block = down[...].astype(F32).T
        grad_down[...] = block
        grad_up[...] = up[...].astype(F32)
        grad_scale[...] += jnp.sum(block * down_w[...].astype(F32), axis=0, keepdims=True)

    even = lax.axis_index("col") % 2 == 0
    pl.when(even)(lambda: expand(own, got))
    pl.when(jnp.logical_not(even))(lambda: expand(got, own))

    @pl.when(step == pl.num_programs(0) - 1)
    def _():
        grad_scale[...] = grad_scale[...] / vecs[SCALE_2 : SCALE_2 + 1, :]


def expand_rest_kernel(
    own, got, out_w, vecs, grad_in, grad_conv, grad_1, grad_2, grad_3, grad_4, grad_out,
    gain_1, shift_1, scale_1, gain_2, shift_2, grad_bias,
):
    def expand(first, other):
        grad_in[:, :512] = first[:512, :].astype(F32)
        grad_in[:, 512:] = first[512:, :].astype(F32)
        block = other[:512, :].astype(F32)
        grad_out[...] = block
        scaled = jnp.sum(block * out_w[...].astype(F32), axis=0, keepdims=True)
        scale_1[...] = scaled / vecs[SCALE_1 : SCALE_1 + 1, :]
        grad_4[...] = other[512:768, :].astype(F32)
        square = other[768:896, :].astype(F32)
        grad_3[...] = square[:, 0:256]
        grad_2[...] = square[64:128, 256:384]
        grad_1[...] = square[32:64, 384 + 64 : 512]
        tail = other[896:1024, :].astype(F32)
        taps = jnp.concatenate([tail[:56], tail[56:112]], axis=1)[:, 32:]
        for row in range(TAPS):
            grad_conv[row] = taps[TAPS * row : TAPS * row + TAPS]
        for row, ref in enumerate((gain_1, shift_1, gain_2, shift_2)):
            ref[...] = tail[112 + row : 113 + row]
        for k in range(4):
            grad_bias[:, 512 * k : 512 * k + 512] = tail[116 + k : 117 + k]

    even = lax.axis_index("col") % 2 == 0
    pl.when(even)(lambda: expand(own, got))
    pl.when(jnp.logical_not(even))(lambda: expand(got, own))


def whole(shape):
    return pl.BlockSpec(shape, lambda i: (0,) * len(shape), pipeline_mode=pl.Buffered(1))


def chunked(shape):
    return pl.BlockSpec(shape, lambda i: (i,) + (0,) * (len(shape) - 1))


def held(shape):
    return pl.BlockSpec(shape, lambda i: (0,) * len(shape))


def params(limit_mib):
    return pltpu.CompilerParams(vmem_limit_bytes=limit_mib * 1024 * 1024, dimension_semantics=("arbitrary",))


def cost(micros):
    return pl.CostEstimate(flops=int(micros * 1e10), bytes_accessed=int(micros * 3e7), transcendentals=0)


def shaped(shape, dtype):
    return jax.ShapeDtypeStruct(shape, dtype)


AXES = ("row", "col")


class Reducer:
    def __init__(self):
        self.rows = lax.axis_size("row")
        self.cols = lax.axis_size("col")
        self.row_at = lax.axis_index("row")
        self.col_at = lax.axis_index("col")
        bits = [("row", 1 << b) for b in range(self.rows.bit_length() - 1)]
        bits += [("col", 1 << b) for b in range(1, self.cols.bit_length() - 1)]
        self.steps = list(zip(bits, bits[1:-1] + [bits[0], bits[-1]]))
        self.core_step = (("col", 1), ("col", 1))
        self.core = self.col_at & 1

    def pairs(self, step):
        result = []
        for r in range(self.rows):
            for c in range(self.cols):
                axis, mask = step[c & 1]
                r2, c2 = (r ^ mask, c) if axis == "row" else (r, c ^ mask)
                result.append((r * self.cols + c, r2 * self.cols + c2))
        return result

    def bit(self, step):
        values = [((self.row_at if axis == "row" else self.col_at) & mask) != 0 for axis, mask in step]
        return jnp.where(self.core == 0, values[0], values[1]).astype(jnp.int32)

    def swap(self, block, step):
        return lax.ppermute(block, AXES, self.pairs(step))

    def open(self, sent, kept):
        return Sum(self, sent, kept)


class Sum:
    def __init__(self, reducer, sent, kept):
        self.reducer = reducer
        self.sent, self.kept, self.got = sent, kept, None
        count = len(reducer.steps)
        self.plan = [reducer.core_step] + reducer.steps + reducer.steps[-2::-1] + [reducer.core_step]
        self.halvings = count
        self.stage = 0

    @property
    def done(self):
        return self.stage == len(self.plan)

    def swap(self):
        self.got = self.reducer.swap(self.sent, self.plan[self.stage])

    def combine(self):
        sent, kept, got, stage = self.sent, self.kept, self.got, self.stage
        self.stage += 1
        self.got = None
        steps = self.reducer.steps
        if stage < self.halvings - 1:
            bit = self.reducer.bit(steps[stage])
            half = kept.shape[0] // 2

            def summed(at):
                pieces = [lax.dynamic_slice_in_dim(a, at * half, half, 0).astype(F32) for a in (kept, got)]
                return (pieces[0] + pieces[1]).astype(BF16)

            self.sent, self.kept = summed(1 - bit), summed(bit)
        elif stage <= self.halvings:
            self.sent = self.kept = (kept.astype(F32) + got.astype(F32)).astype(BF16)
        elif not self.done:
            bit = self.reducer.bit(self.plan[stage]) == 1
            self.sent = self.kept = jnp.concatenate([jnp.where(bit, got, kept), jnp.where(bit, kept, got)], axis=0)
        else:
            self.got = got

    def advance(self):
        self.swap()
        self.combine()


def shift_pairs(count):
    forward = [(i, i + 1) for i in range(count - 1)]
    return forward, [(b, a) for a, b in forward]


def on_device(
    activations, gain_first, shift_first, in_weight, conv_kernel, mix_first, mix_second, mix_third,
    mix_fourth, out_weight, scale_mixer, gain_second, shift_second, up_weight, up_bias, down_weight,
    scale_mlp, valid_pixels, tile_images, cotangent,
):
    tile_rows, tile_cols, width = activations.shape
    pixels = tile_rows * tile_cols
    hidden = up_weight.shape[1]
    gate_count = conv_kernel.shape[-1]
    joined_count = in_weight.shape[1]
    lead_count = joined_count - gate_count
    span = tile_cols + 8
    ext_rows = tile_rows + 2 * HALO
    ext_pixels = ext_rows * span
    tab = tables()
    down_pairs, up_pairs = shift_pairs(lax.axis_size("row"))
    right_pairs, left_pairs = shift_pairs(lax.axis_size("col"))

    row_at, col_at = lax.axis_index("row"), lax.axis_index("col")
    row_last, col_last = lax.axis_size("row") - 1, lax.axis_size("col") - 1
    own_image = tile_images[row_at, col_at]

    def same(row, col, inside):
        return jnp.logical_and(inside, tile_images[row, col] == own_image)

    same_up = same(jnp.maximum(row_at - 1, 0), col_at, row_at > 0)
    same_down = same(jnp.minimum(row_at + 1, row_last), col_at, row_at < row_last)
    same_left = same(row_at, jnp.maximum(col_at - 1, 0), col_at > 0)
    same_right = same(row_at, jnp.minimum(col_at + 1, col_last), col_at < col_last)

    def rows_around(block):
        return lax.ppermute(block[-HALO:], "row", down_pairs), lax.ppermute(block[:HALO], "row", up_pairs)

    def taller(above, block, below, outside):
        blank = jnp.asarray(outside, BF16)
        above, below = jnp.where(same_up, above, blank), jnp.where(same_down, below, blank)
        return jnp.concatenate([above, block, below], axis=0)

    def cols_around(from_left, from_right):
        return lax.ppermute(from_left, "col", right_pairs), lax.ppermute(from_right, "col", left_pairs)

    def wider(left, tall, right, outside):
        depth = tall.shape[-1]
        blank = jnp.asarray(outside, BF16)
        left, right = jnp.where(same_left, left, blank), jnp.where(same_right, right, blank)
        filler = jnp.full((ext_rows, span - tile_cols - 2 * HALO, depth), blank)
        return jnp.concatenate([left, tall, right, filler], axis=1).reshape(ext_pixels, depth)

    marked = jnp.where(valid_pixels[..., None] != 0, activations, jnp.asarray(OUTSIDE, BF16))
    above, below = rows_around(marked)
    tall = taller(above, marked, below, OUTSIDE)
    sides = tall[:, -HALO:], tall[:, :HALO]
    (sides, conv_kernel, mix_first, mix_second, valid_pixels) = lax.optimization_barrier(
        (sides, conv_kernel, mix_first, mix_second, valid_pixels)
    )
    left, right = cols_around(*sides)

    x_own = activations.reshape(pixels, width)
    cot = cotangent.reshape(pixels, width)
    valid = valid_pixels.astype(F32).reshape(pixels, 1)
    vecs = jnp.stack(
        [gain_first, shift_first, scale_mixer, gain_second, shift_second, scale_mlp, scale_mlp, scale_mlp]
    ).astype(F32)
    bias = up_bias.astype(F32).reshape(1, hidden)
    taps = jnp.pad(conv_kernel.astype(F32).reshape(TAPS * TAPS, gate_count), ((0, 0), (lead_count, 0)))
    spec = jnp.dot(tab["spectrum"], taps, precision=lax.Precision.HIGHEST, preferred_element_type=F32)
    w1 = jnp.zeros((128, 128), BF16).at[32:64, 64:128].set(mix_first)
    w2 = jnp.zeros((128, 128), BF16).at[64:128, :].set(mix_second)
    w3, w4 = mix_third, mix_fourth
    (left, right, spec, w1, w2, valid, vecs, bias) = lax.optimization_barrier(
        (left, right, spec, w1, w2, valid, vecs, bias)
    )
    x_ext = wider(left, tall, right, OUTSIDE)

    chunk = OUT * tile_cols
    steps = tile_rows // OUT
    (
        xwaves, spread, prods, lead, middle, active, slope, grad_down,
    ) = pl.pallas_call(
        forward_kernel,
        grid=(steps,),
        in_specs=[
            whole((ext_pixels, width)), chunked((chunk, width)), chunked((chunk, 1)),
            chunked((chunk, width)), whole((8, width)), whole((1, hidden)), whole((width, joined_count)),
            whole((128, 128)), whole((128, 128)), whole(w3.shape), whole(w4.shape), whole((width, width)),
            whole((width, hidden)), whole((3 * SLOTS, joined_count)), whole(tab["window"].shape),
            whole(tab["tile_back"].shape),
        ],
        out_specs=[
            chunked((2 * SLOTS * TILES, joined_count)), chunked((chunk, joined_count)),
            chunked((chunk, joined_count)), chunked((chunk, 128)), chunked((chunk, width)), chunked((chunk, hidden)),
            chunked((chunk, hidden)), held((hidden, width)),
        ],
        out_shape=[
            shaped((steps * 2 * SLOTS * TILES, joined_count), BF16), shaped((pixels, joined_count), F32),
            shaped((pixels, joined_count), F32), shaped((pixels, 128), F32),
            shaped((pixels, width), F32), shaped((pixels, hidden), BF16), shaped((pixels, hidden), BF16),
            shaped((hidden, width), BF16),
        ],
        scratch_shapes=[
            pltpu.VMEM((ext_pixels, joined_count + 128), F32),
            pltpu.VMEM((2 * SLOTS, LANES * TILES), F32), pltpu.VMEM((2 * SLOTS, LANES * TILES), BF16),
            pltpu.VMEM((pixels, hidden), BF16), pltpu.VMEM((pixels, width), BF16),
        ],
        compiler_params=params(58),
        cost_estimate=cost(40),
        name="forward",
    )(
        x_ext, x_own, valid, cot, vecs, bias, in_weight, w1, w2, w3, w4, out_weight, up_weight,
        spec, tab["window"], tab["tile_back"],
    )

    rows = 256
    count = pixels // rows
    gmiddle, ffn_sent, ffn_kept, ffn_sums, bias_sum = pl.pallas_call(
        ffn_back_kernel,
        grid=(count,),
        in_specs=[
            chunked((rows, width)), chunked((rows, hidden)), chunked((rows, width)), chunked((rows, 1)),
            whole((8, width)), whole((hidden, width)), whole((width, hidden)), whole((hidden, width)),
        ],
        out_specs=[
            chunked((rows, width)), held((hidden, width)), held((hidden, width)), held((8, width)),
            held((8, hidden)),
        ],
        out_shape=[
            shaped((pixels, width), F32), shaped((hidden, width), BF16), shaped((hidden, width), BF16),
            shaped((8, width), F32),
            shaped((8, hidden), F32),
        ],
        scratch_shapes=[pltpu.VMEM((pixels, width), BF16), pltpu.VMEM((pixels, hidden), BF16)],
        compiler_params=params(48),
        cost_estimate=cost(16),
        name="ffn_back",
    )(cot, slope, middle, valid, vecs, down_weight, up_weight, grad_down)

    reducer = Reducer()
    ffn = reducer.open(ffn_sent, ffn_kept)
    ffn.swap()

    gspread, glead, mixer_grads = pl.pallas_call(
        mixer_back_kernel,
        grid=(count,),
        in_specs=[
            chunked((rows, width)), chunked((rows, joined_count)), chunked((rows, joined_count)),
            chunked((rows, 128)), whole((8, width)), whole((128, 128)), whole((128, 128)), whole(w3.shape),
            whole(w4.shape), whole((width, width)),
        ],
        out_specs=[chunked((rows, joined_count)), chunked((rows, 128)), held((896, width))],
        out_shape=[
            shaped((pixels, joined_count), BF16), shaped((pixels, 128), F32), shaped((896, width), BF16),
        ],
        scratch_shapes=[
            pltpu.VMEM((width, width), F32), pltpu.VMEM(w4.shape, F32), pltpu.VMEM(w3.shape, F32),
            pltpu.VMEM((128, 128), F32), pltpu.VMEM((128, 128), F32),
        ],
        compiler_params=params(48),
        cost_estimate=cost(12),
        name="mixer_back",
    )(gmiddle, spread, prods, lead, vecs, w1, w2, w3, w4, out_weight)

    tie = lax.optimization_barrier
    (gspread, ffn.kept, ffn.got) = tie((gspread, ffn.kept, ffn.got))
    block = gspread.reshape(tile_rows, tile_cols, joined_count)
    above, below = rows_around(block)
    grad_kernel = pl.pallas_call(
        kernel_back_kernel,
        grid=(steps,),
        in_specs=[
            chunked((2 * SLOTS * TILES, joined_count)), chunked((chunk, joined_count)),
            whole(tab["tile"].shape), whole(tab["kernel_back"].shape),
        ],
        out_specs=held((112, width)),
        out_shape=shaped((112, width), BF16),
        scratch_shapes=[
            pltpu.VMEM((chunk, joined_count), F32), pltpu.VMEM((2 * SLOTS, LANES * TILES), F32),
            pltpu.VMEM((4 * SLOTS, joined_count), F32),
        ],
        compiler_params=params(48),
        cost_estimate=cost(9),
        name="kernel_back",
    )(xwaves, gspread, tab["tile"], tab["kernel_back"])
    (above, below, grad_kernel, ffn.kept) = tie((above, below, grad_kernel, ffn.kept))
    tall = taller(above, block, below, 0.0)
    sides = tall[:, -HALO:], tall[:, :HALO]
    (sides, ffn.kept) = tie((sides, ffn.kept))
    left, right = cols_around(*sides)
    ffn.combine()
    (left, right, ffn.sent, ffn.kept) = tie((left, right, ffn.sent, ffn.kept))
    ffn.swap()
    gs_ext = wider(left, tall, right, 0.0)

    gjoined = pl.pallas_call(
        gates_back_kernel,
        grid=(steps,),
        in_specs=[
            whole((ext_pixels, joined_count)), chunked((chunk, 128)),
            pl.BlockSpec((3 * SLOTS, joined_count), lambda i: (1, 0), pipeline_mode=pl.Buffered(1)),
            whole(tab["window"].shape), whole(tab["tile_back"].shape),
        ],
        out_specs=chunked((chunk, joined_count)),
        out_shape=shaped((pixels, joined_count), BF16),
        scratch_shapes=[
            pltpu.VMEM((ext_pixels, joined_count), F32), pltpu.VMEM((2 * SLOTS, LANES * TILES), F32),
            pltpu.VMEM((2 * SLOTS, LANES * TILES), BF16), pltpu.VMEM((chunk, joined_count), F32),
        ],
        compiler_params=params(48),
        cost_estimate=cost(11),
        name="gates_back",
    )(gs_ext, glead, spec, tab["window"], tab["tile_back"])
    (gjoined, ffn.got) = tie((gjoined, ffn.got))
    ffn.combine()
    (gjoined, ffn.sent, ffn.kept) = tie((gjoined, ffn.sent, ffn.kept))
    ffn.swap()

    ginput, rest_sent, rest_kept = pl.pallas_call(
        in_back_kernel,
        grid=(count,),
        in_specs=[
            chunked((rows, joined_count)), chunked((rows, width)), chunked((rows, width)), chunked((rows, 1)),
            whole((8, width)), whole((width, joined_count)), whole((896, width)), whole((112, width)),
            whole((8, width)), whole((8, hidden)),
        ],
        out_specs=[chunked((rows, width)), held((joined_count, width)), held((joined_count, width))],
        out_shape=[
            shaped((pixels, width), BF16), shaped((joined_count, width), BF16), shaped((joined_count, width), BF16),
        ],
        scratch_shapes=[
            pltpu.VMEM((pixels, width), BF16), pltpu.VMEM((pixels, joined_count), BF16), pltpu.VMEM((8, width), F32),
        ],
        compiler_params=params(48),
        cost_estimate=cost(8),
        name="in_back",
    )(
        gjoined, x_own, gmiddle, valid, vecs, in_weight, mixer_grads, grad_kernel, ffn_sums, bias_sum,
    )
    rest = reducer.open(rest_sent, rest_kept)
    rest.swap()
    (rest.kept, ffn.got) = tie((rest.kept, ffn.got))
    ffn.combine()
    ffn.swap()

    def down(active, before, first, blocks):
        return pl.pallas_call(
            down_kernel,
            grid=(blocks,),
            in_specs=[
                pl.BlockSpec((rows, hidden), lambda i: (i + first, 0)),
                pl.BlockSpec((rows, width), lambda i: (i + first, 0)), whole((8, width)), whole((hidden, width)),
                pl.BlockSpec(memory_space=pl.ANY),
            ],
            out_specs=pl.BlockSpec((rows, width), lambda i: (i + first, 0)),
            out_shape=shaped((pixels, width), BF16),
            input_output_aliases={4: 0} if first else {},
            compiler_params=params(48),
            cost_estimate=cost(4),
            name="down",
        )(active, middle, vecs, down_weight, before)

    (active, rest.sent, ffn.sent) = tie((active, rest.sent, ffn.sent))
    outputs = down(active, jnp.zeros((8, 128), BF16), 0, count // 2)

    def onward(way, *others):
        values = tie((way.kept, way.got) + others)
        way.kept, way.got = values[:2]
        way.combine()
        if not way.done:
            way.swap()
        return values[2:]

    (outputs,) = onward(rest, outputs)
    (rest.kept,) = onward(ffn, rest.kept)
    (outputs, rest.sent, ffn.sent) = tie((outputs, rest.sent, ffn.sent))
    outputs = down(active, outputs, count // 2, count - count // 2)
    (outputs,) = onward(rest, outputs)
    expand_ffn = pl.pallas_call(
        expand_ffn_kernel,
        grid=(hidden // width,),
        in_specs=[
            chunked((width, width)), chunked((width, width)), chunked((width, width)), whole((8, width)),
        ],
        out_specs=[
            chunked((width, width)), pl.BlockSpec((width, width), lambda i: (0, i)), held((1, width)),
        ],
        out_shape=[shaped((hidden, width), F32), shaped((width, hidden), F32), shaped((1, width), F32)],
        compiler_params=params(32),
        cost_estimate=cost(5),
        name="expand_ffn",
    )
    expanded = None
    for who in "frfrfrrfrfr":
        way, other = (ffn, rest) if who == "f" else (rest, ffn)
        if not way.done:
            (other.kept,) = onward(way, other.kept)
        if ffn.done and expanded is None:
            expanded = expand_ffn(ffn.kept, ffn.got, down_weight, vecs)
            (rest.kept, expanded) = tie((rest.kept, expanded))
    while not (ffn.done and rest.done):
        for way in (ffn, rest):
            if not way.done:
                onward(way)
    if expanded is None:
        expanded = expand_ffn(ffn.kept, ffn.got, down_weight, vecs)
    grad_down_weight, grad_up_weight, scale_2 = expanded
    rest_own, rest_got = rest.kept, rest.got
    vector = shaped((1, width), F32)
    whole_block = pl.BlockSpec(memory_space=pltpu.VMEM)
    (
        grad_in_weight, grad_conv, grad_1, grad_2, grad_3, grad_4, grad_out,
        gain_1, shift_1, scale_1, gain_2, shift_2, grad_bias,
    ) = pl.pallas_call(
        expand_rest_kernel,
        in_specs=[whole_block] * 4,
        out_specs=[whole_block] * 13,
        out_shape=[
            shaped(in_weight.shape, F32), shaped(conv_kernel.shape, F32), shaped(mix_first.shape, F32),
            shaped(mix_second.shape, F32), shaped(w3.shape, F32), shaped(w4.shape, F32), shaped((width, width), F32),
            vector, vector, vector, vector, vector, shaped((1, hidden), F32),
        ],
        compiler_params=pltpu.CompilerParams(vmem_limit_bytes=32 * 1024 * 1024),
        cost_estimate=cost(5),
        name="expand_rest",
    )(rest_own, rest_got, out_weight, vecs)
    return (
        outputs.reshape(activations.shape),
        ginput.reshape(activations.shape),
        gain_1.reshape(width),
        shift_1.reshape(width),
        grad_in_weight,
        grad_conv,
        grad_1,
        grad_2,
        grad_3,
        grad_4,
        grad_out,
        scale_1.reshape(width),
        gain_2.reshape(width),
        shift_2.reshape(width),
        grad_up_weight,
        grad_bias.reshape(hidden),
        grad_down_weight,
        scale_2.reshape(width),
    )


def solution(mesh):
    tiles = P("row", "col", None)
    in_specs = (tiles,) + (P(),) * 16 + (P("row", "col"), P(), tiles)
    out_specs = (tiles, tiles) + (P(),) * 16
    return jax.shard_map(on_device, mesh=mesh, in_specs=in_specs, out_specs=out_specs, check_vma=False)
```

time: 605 us -> 233 us (0.39)
  other arithmetic: 168 us -> 19.2 us
  waiting for transfers between devices: 193 us -> 52.9 us
  Pallas kernels: 0 us -> 104 us
  matrix products: 95.8 us -> 2.84 us
  blocking collectives: 51 us -> 0 us
  local copies, waits for them, and re-layouts: 49.1 us -> 6.11 us
  starting transfers between devices: 24.8 us -> 40.4 us
  between operations: 16.4 us -> 6.86 us
    psum x1 -> x0, waiting for transfers between devices: 184 us -> none  [on_device(): lax.psum((grad_gain_first, grad_shift_first, grad_in_weight, grad_kernel,...]
    pallas_call x0 -> x10, Pallas kernels: none -> 104 us  [the longest x1 34.1 us: on_device(): pl.pallas_call(forward_kernel, grid=(steps,), in_specs=[whole((ext_pixels...]
    dot_general x25 -> x1, matrix products: 95.8 us -> 2.84 us  [on_device(): jnp.dot(tab['spectrum'], taps, precision=lax.Precision.HIGHEST, preferred...]
    reduce_sum x6 -> x0, other arithmetic: 58.8 us -> none  [the longest x3 54.6 us: on_device(): jnp.sum(grad_spread * gate_ext[row_off:row_off + tile_rows, col_off:col_o...]
    mul x4 -> x0, other arithmetic: 52.2 us -> none  [the longest x1 40.2 us: depthwise(): return DW_SCALE * summed]
    psum x1 -> x0, blocking collectives: 51 us -> none  [on_device(): lax.psum((grad_gain_first, grad_shift_first, grad_in_weight, grad_kernel,...]
    ppermute x8 -> x26, waiting for transfers between devices: 8.83 us -> 52.9 us  [the longest x18 50.2 us: swap(): return lax.ppermute(block, AXES, self.pairs(step))]
    another operation x1 -> x0, other arithmetic: 39.4 us -> none
  transfers between devices with their start and end apart: 9 -> 26, of which waited for: 5 -> 16; matrix products, arithmetic and copies ran while one was open for 5% -> 7% of each run, Pallas kernels for 0% -> 21%
where the time goes in v1:
time: 233 us; the launch traced here: 232 us
  Pallas kernels  104 us (45%)
  waiting for transfers between devices  52.9 us (23%)
  starting transfers between devices  40.4 us (17%)
  other arithmetic  19.2 us (8%)
  between operations  6.86 us (3%)
  local copies, waits for them, and re-layouts  6.11 us (3%)
  matrix products  2.84 us (1%)
    ppermute x18, waiting for transfers between devices, swap(): return lax.ppermute(block, AXES, self.pairs(step))  50.2 us
    pallas_call x1, Pallas kernels, on_device(): pl.pallas_call(forward_kernel, grid=(steps,), in_specs=[whole((ext_pixels...  34.1 us
    ppermute x18, starting transfers between devices, swap(): return lax.ppermute(block, AXES, self.pairs(step))  22.3 us
    pallas_call x1, Pallas kernels, on_device(): pl.pallas_call(ffn_back_kernel, grid=(count,), in_specs=[chunked((rows, w...  17.7 us
    pallas_call x1, Pallas kernels, on_device(): pl.pallas_call(gates_back_kernel, grid=(steps,), in_specs=[whole((ext_pix...  10 us
    pallas_call x1, Pallas kernels, on_device(): pl.pallas_call(mixer_back_kernel, grid=(count,), in_specs=[chunked((rows,...  9.69 us
    ppermute x2, starting transfers between devices, rows_around(): lax.ppermute(block[-HALO:], 'row', down_pairs)  9.39 us
    pallas_call x1, Pallas kernels, on_device(): pl.pallas_call(kernel_back_kernel, grid=(steps,), in_specs=[chunked((2 *...  9.17 us
  transfers between devices with their start and end apart: 26, of which 16 were waited for; matrix products, arithmetic and copies ran while one was open for 7% of the time, Pallas kernels for 21%

profile of v1, /device:TPU:0, one launch (start us, length us, event | category | flops | bytes accessed | tf_op | source)
XLA Modules:
  0.0 232.0 jit_solution(6326237430316631534)
XLA Ops:
  1.5 1.6 broadcast_select_fusion
  3.2 4.8 %collective-permute-start = (bf16[3,40,512]{2,1,0:T(8,128)(2,1)S(1)}, bf16[3,40,512]{2,1,0:T(8,128)(2,1)S(1)}, u32[]{:S(2)}, u32[]{:S(2)}) collective-permute-start(bf16[3,40,512]{2,1,0:T(8,128)(2,1)S(1)} %get-tuple-element.294), channel_id=1, source_target_pairs={{0,8},{8,16},{16,24},{1,9},{9,17},{17,25},{2,10},{10,18},{18,26},{... | collective-permute-start | bytes 368648 | tf_op jit(solution)/shard_map/ppermute | solution.py:632
  8.0 1.3 collective-permute-start.1
  16.9 1.5 collective-permute-start.2
  18.4 1.3 collective-permute-start.3
  19.7 2.8 %fusion.spec = f32[672,1024]{1,0:T(8,128)} fusion(f32[672,49]{1,0:T(8,128)S(1)} %copy-done.32, bf16[49,992]{1,0:T(8,128)(2,1)S(1)} %reshape.157), kind=kOutput, calls=%fused_computation.51 | convolution fusion | flops 404619264 | bytes 2981440 | tf_op jit(solution)/shard_map/dot_general | solution.py:666
  24.0 1.1 copy.44.valid
  25.3 2.5 %maximum_maximum_fusion.1 = bf16[38,48,512]{2,1,0:T(8,128)(2,1)} fusion(bf16[38,3,512]{2,1,0:T(4,128)(2,1)S(1)} %get-tuple-element.317, bf16[3,40,512]{2,1,0:T(8,128)(2,1)S(1)} %broadcast_select_fusion.19, bf16[32,40,512]{2,1,0:T(8,128)(2,1)S(1)} %broadcast_select_fusion, bf16[3,40,512]{2,1,0:T(8,128)(2,1)S(1)} %broadcast_select_fusion.20, ...), kind=kLoop, calls=%fused_computation.4 | loop fusion | flops 11206656 | bytes 3657824 | tf_op jit(solution)/shard_map/concatenate | solution.py:647
  27.7 34.1 %forward.1 = (bf16[4480,1024]{1,0:T(8,128)(2,1)}, f32[1280,1024]{1,0:T(8,128)}, f32[1280,1024]{1,0:T(8,128)}, f32[1280,128]{1,0:T(8,128)}, f32[1280,512]{1,0:T(8...) custom-call(bf16[1824,512]{1,0:T(8,128)(2,1)} %bitcast.27, ...), custom_call_target="tpu_custom_call" | custom-call | flops 399999991808 | bytes 1200000000 | tf_op jit(solution)/shard_map/forward/pallas_call | solution.py:679
  62.0 17.7 %ffn_back.1 = (f32[1280,512]{1,0:T(8,128)}, bf16[2048,512]{1,0:T(8,128)(2,1)S(1)}, bf16[2048,512]{1,0:T(8,128)(2,1)}, f32[8,512]{1,0:T(8,128)S(1)}, f32[8,2048]{1,0:T(8,128)S(1)}) custom-call(bf16[1280,512]{1,0:T(8,128)(2,1)S(1)} %bitcast.25, bf16[1280,2048]{1,0:T(8,128)(2,1)} %get-tuple-element.175.slope, f32[1280,512]{1,0:T(8,128)} %get-tuple-element.176.middle, ...), custom_call_target="tpu_custom_call" | custom-call | flops 160000000000 | bytes 480000000 | tf_op jit(solution)/shard_map/ffn_back/pallas_call | solution.py:715
  80.3 3.1 %collective-permute-start.4 = (bf16[2048,512]{1,0:T(8,128)(2,1)S(1)}, bf16[2048,512]{1,0:T(8,128)(2,1)S(1)}, u32[]{:S(2)}, u32[]{:S(2)}) collective-permute-start(bf16[2048,512]{1,0:T(8,128)(2,1)S(1)} %get-tuple-element.184), channel_id=1, source_target_pairs={{0,1},{1,0},{2,3},{3,2},{4,5},{5,4},{6,7},{7,6},{8,9},{9,8},{10,11... | collective-permute-start | bytes 6291464 | tf_op jit(solution)/shard_map/ppermute | solution.py:547
  83.5 9.7 %mixer_back.1 = (bf16[1280,1024]{1,0:T(8,128)(2,1)S(1)}, f32[1280,128]{1,0:T(8,128)S(1)}, bf16[896,512]{1,0:T(8,128)(2,1)S(1)}) custom-call(f32[1280,512]{1,0:T(8,128)} %get-tuple-element.178.gmiddle, f32[1280,1024]{1,0:T(8,128)} %get-tuple-element.179.spread, f32[1280,1024]{1,0:T(8,128)} %get-tuple-element.180.prods, f32[1280,128]{1,0:T(8,128)S(1)} %copy-done.22, ...), custom_call_target="tpu_custom_call" | custom-call | flops 120000004096 | bytes 360000000 | tf_op jit(solution)/shard_map/mixer_back/pallas_call | solution.py:741
  93.3 4.5 %collective-permute-start.5 = (bf16[3,40,1024]{2,1,0:T(8,128)(2,1)S(1)}, bf16[3,40,1024]{2,1,0:T(8,128)(2,1)S(1)}, u32[]{:S(2)}, u32[]{:S(2)}) collective-permute-start(bf16[3,40,1024]{2,1,0:T(8,128)(2,1)S(1)} %bitcast.31), channel_id=1, source_target_pairs={{0,8},{8,16},{16,24},{1,9},{9,17},{17,25},{2,10},{10,18},{18,26},{... | collective-permute-start | bytes 737288 | tf_op jit(solution)/shard_map/ppermute | solution.py:632
  97.8 1.3 collective-permute-start.6
  99.1 9.2 %kernel_back.1.grad_kernel = bf16[112,512]{1,0:T(8,128)(2,1)S(1)} custom-call(bf16[4480,1024]{1,0:T(8,128)(2,1)} %get-tuple-element.186.xwaves, bf16[1280,1024]{1,0:T(8,128)(2,1)S(1)} %get-tuple-element.185.gspread, bf16[224,64]{1,0:T(8,128)(2,1)S(1)} %copy-done.16, f32[56,448]{1,0:T(8,128)S(1)} %copy-done.15), custom_call_target="tpu_custom_call" | custom-call | flops 89999998976 | bytes 270000000 | tf_op jit(solution)/shard_map/kernel_back/pallas_call | solution.py:766
  109.0 2.3 collective-permute-done.6
  113.1 2.0 collective-permute-start.7
  115.1 1.3 collective-permute-start.8
  117.0 2.8 %add_convert_fusion = (bf16[1024,512]{1,0:T(8,128)(2,1)S(1)}, bf16[1024,512]{1,0:T(8,128)(2,1)S(1)}) fusion(bf16[2048,512]{1,0:T(8,128)(2,1)} %copy-done.31, s32[]{:T(128)S(6)} %mul.49, bf16[2048,512]{1,0:T(8,128)(2,1)} %get-tuple-element.193, s32[]{:T(128)S(6)} %select_n.220), kind=kLoop, calls=%fused_computation.2 | loop fusion | flops 4194304 | bytes 6291464 | tf_op jit(solution)/shard_map/convert_element_type | solution.py:580
  120.4 1.1 broadcast_select_fusion.7
  122.3 3.9 %maximum_maximum_fusion = bf16[38,48,1024]{2,1,0:T(8,128)(2,1)} fusion(bf16[38,3,1024]{2,1,0:T(4,128)(2,1)S(1)} %broadcast_select_fusion.7, bf16[3,40,1024]{2,1,0:T(8,128)(2,1)S(1)} %copy-done.30, bf16[32,40,1024]{2,1,0:T(8,128)(2,1)S(1)} %bitcast.23, bf16[3,40,1024]{2,1,0:T(8,128)(2,1)S(1)} %copy-done.28, bf16[38,3,1024]{2,1,0:T(4,128)(2,1)S(1)} %broadcast_select_fusion.8, ...), kind=kLoop, calls=%fused_computation | loop fusion | flops 22413312 | bytes 7315552 | tf_op jit(solution)/shard_map/concatenate | solution.py:647
  126.2 10.0 %gates_back.1.gjoined = bf16[1280,1024]{1,0:T(8,128)(2,1)S(1)} custom-call(bf16[1824,1024]{1,0:T(8,128)(2,1)} %bitcast.26, f32[1280,128]{1,0:T(8,128)S(1)} %copy-done.21, f32[672,1024]{1,0:T(8,128)S(1)} %copy-done, bf16[224,224]{1,0:T(8,128)(2,1)S(1)} %copy-done.14, bf16[64,224]{1,0:T(8,128)(2,1)S(1)} %copy-done.17), custom_call_target="tpu_custom_call" | custom-call | flops 109999996928 | bytes 330000000 | tf_op jit(solution)/shard_map/gates_back/pallas_call | solution.py:793
  136.7 2.0 collective-permute-start.10
  138.7 8.7 %in_back.1 = (bf16[1280,512]{1,0:T(8,128)(2,1)}, bf16[1024,512]{1,0:T(8,128)(2,1)S(1)}, bf16[1024,512]{1,0:T(8,128)(2,1)S(1)}) custom-call(bf16[1280,1024]{1,0:T(8,128)(2,1)} %copy-done.19, bf16[1280,512]{1,0:T(8,128)(2,1)} %bitcast.29, f32[1280,512]{1,0:T(8,128)} %get-tuple-element.178.gmiddle, f32[1280,1]{1,0:T(8,128)S(1)} %copy-done.2, ...), custom_call_target="tpu_custom_call" | custom-call | flops 80000000000 | bytes 240000000 | tf_op jit(solution)/shard_map/in_back/pallas_call | solution.py:816
  147.4 7.2 %collective-permute-start.12 = (bf16[1024,512]{1,0:T(8,128)(2,1)S(1)}, bf16[1024,512]{1,0:T(8,128)(2,1)S(1)}, u32[]{:S(2)}, u32[]{:S(2)}) collective-permute-start(bf16[1024,512]{1,0:T(8,128)(2,1)S(1)} %get-tuple-element.212), channel_id=1, source_target_pairs={{0,1},{1,0},{2,3},{3,2},{4,5},{5,4},{6,7},{7,6},{8,9},{9,8},{10,11... | collective-permute-start | bytes 3145736 | tf_op jit(solution)/shard_map/ppermute | solution.py:547
  154.8 1.5 collective-permute-start.11
  156.3 3.4 %down.2.before = bf16[1280,512]{1,0:T(8,128)(2,1)} custom-call(bf16[1280,2048]{1,0:T(8,128)(2,1)} %get-tuple-element.214.active, f32[1280,512]{1,0:T(8,128)S(1)} %copy-done.18, f32[8,512]{1,0:T(8,128)S(1)} %copy-done.6, bf16[2048,512]{1,0:T(8,128)(2,1)S(1)} %copy-done.7, bf16[8,128]{1,0:T(8,128)(2,1)S(1)} %broadcast_in_dim.50.before), custom_call_target="tpu_custom_call" | custom-call | flops 40000000000 | bytes 120000000 | tf_op jit(solution)/shard_map/down/pallas_call | solution.py:844
  160.0 1.3 collective-permute-done.11
  161.3 2.2 collective-permute-start.14
  163.5 4.7 %down.3 = bf16[1280,512]{1,0:T(8,128)(2,1)} custom-call(bf16[1280,2048]{1,0:T(8,128)(2,1)} %get-tuple-element.214.active, f32[1280,512]{1,0:T(8,128)S(1)} %copy-done.18, f32[8,512]{1,0:T(8,128)S(1)} %copy-done.6, bf16[2048,512]{1,0:T(8,128)(2,1)S(1)} %copy-done.7, bf16[1280,512]{1,0:T(8,128)(2,1)} %down.2.before), custom_call_target="tpu_custom_call", output_to_operand_aliasing={{}: (4, {})} | custom-call | flops 40000000000 | bytes 120000000 | tf_op jit(solution)/shard_map/down/pallas_call | solution.py:844
  168.2 2.2 collective-permute-done.13
  170.6 4.7 %collective-permute-done.14 = bf16[256,512]{1,0:T(8,128)(2,1)S(1)} collective-permute-done((bf16[256,512]{1,0:T(8,128)(2,1)S(1)}, bf16[256,512]{1,0:T(8,128)(2,1)S(1)}, u32[]{:S(2)}, u32[]{:S(2)}) %collective-permute-start.14) | collective-permute-done | bytes 262176 | tf_op jit(solution)/shard_map/ppermute | solution.py:547
  175.3 1.7 collective-permute-start.15
  177.2 4.5 %collective-permute-done.15 = bf16[256,512]{1,0:T(8,128)(2,1)S(1)} collective-permute-done((bf16[256,512]{1,0:T(8,128)(2,1)S(1)}, bf16[256,512]{1,0:T(8,128)(2,1)S(1)}, u32[]{:S(2)}, u32[]{:S(2)}) %collective-permute-start.15) | collective-permute-done | bytes 262176 | tf_op jit(solution)/shard_map/ppermute | solution.py:547
  182.4 1.2 collective-permute-done.16
  183.7 1.2 collective-permute-start.18
  185.1 5.4 %collective-permute-done.17 = bf16[128,512]{1,0:T(8,128)(2,1)S(1)} collective-permute-done((bf16[128,512]{1,0:T(8,128)(2,1)}, bf16[128,512]{1,0:T(8,128)(2,1)S(1)}, u32[]{:S(2)}, u32[]{:S(2)}) %collective-permute-start.17) | collective-permute-done | bytes 131104 | tf_op jit(solution)/shard_map/ppermute | solution.py:547
  190.6 2.3 collective-permute-done.18
  193.5 8.9 %collective-permute-done.19 = bf16[128,512]{1,0:T(8,128)(2,1)S(1)} collective-permute-done((bf16[128,512]{1,0:T(8,128)(2,1)S(1)}, bf16[128,512]{1,0:T(8,128)(2,1)S(1)}, u32[]{:S(2)}, u32[]{:S(2)}) %collective-permute-start.19) | collective-permute-done | bytes 131104 | tf_op jit(solution)/shard_map/ppermute | solution.py:547
  202.5 4.9 %collective-permute-done.20 = bf16[128,512]{1,0:T(8,128)(2,1)S(1)} collective-permute-done((bf16[128,512]{1,0:T(8,128)(2,1)S(1)}, bf16[128,512]{1,0:T(8,128)(2,1)S(1)}, u32[]{:S(2)}, u32[]{:S(2)}) %collective-permute-start.20) | collective-permute-done | bytes 131104 | tf_op jit(solution)/shard_map/ppermute | solution.py:547
  207.5 1.9 collective-permute-done.21
  209.4 1.4 broadcast_select_fusion.2
  211.0 1.2 collective-permute-start.22
  212.2 5.3 %collective-permute-done.22 = bf16[256,512]{1,0:T(8,128)(2,1)S(1)} collective-permute-done((bf16[256,512]{1,0:T(8,128)(2,1)S(1)}, bf16[256,512]{1,0:T(8,128)(2,1)S(1)}, u32[]{:S(2)}, u32[]{:S(2)}) %collective-permute-start.22) | collective-permute-done | bytes 262176 | tf_op jit(solution)/shard_map/ppermute | solution.py:547
  218.0 3.9 %expand_ffn.1 = (f32[2048,512]{1,0:T(8,128)}, f32[512,2048]{1,0:T(8,128)}, f32[1,512]{1,0:T(1,128)}) custom-call(bf16[2048,512]{1,0:T(8,128)(2,1)S(1)} %pad_maximum_fusion.own, bf16[2048,512]{1,0:T(8,128)(2,1)S(1)} %collective-permute-done.23.got, bf16[2048,512]{1,0:T(8,128)(2,1)S(1)} %copy-done.7, f32[8,512]{1,0:T(8,128)S(1)} %copy-done.6), custom_call_target="tpu_custom_call" | custom-call | flops 49999998976 | bytes 150000000 | tf_op jit(solution)/shard_map/expand_ffn/pallas_call | solution.py:896
  222.0 4.8 %collective-permute-done.24 = bf16[512,512]{1,0:T(8,128)(2,1)S(1)} collective-permute-done((bf16[512,512]{1,0:T(8,128)(2,1)S(1)}, bf16[512,512]{1,0:T(8,128)(2,1)S(1)}, u32[]{:S(2)}, u32[]{:S(2)}) %collective-permute-start.24) | collective-permute-done | bytes 524320 | tf_op jit(solution)/shard_map/ppermute | solution.py:547
  227.0 2.6 %collective-permute-done.25.got = bf16[1024,512]{1,0:T(8,128)(2,1)S(1)} collective-permute-done((bf16[1024,512]{1,0:T(8,128)(2,1)S(1)}, bf16[1024,512]{1,0:T(8,128)(2,1)S(1)}, u32[]{:S(2)}, u32[]{:S(2)}) %collective-permute-start.25) | collective-permute-done | bytes 1048608 | tf_op jit(solution)/shard_map/ppermute | solution.py:547
  229.7 2.3 expand_rest.1
  (165 shorter events, 13.7 us)
Async XLA Ops:
  0.7 11.9 %copy-start.41 = (bf16[512]{0:T(512)(128)(2,1)S(1)}, bf16[512]{0:T(512)(128)(2,1)}, u32[]{:S(2)}) copy-start(bf16[512]{0:T(512)(128)(2,1)} %param.39) | copy-start | bytes 3076
  0.7 11.9 %copy-start.42 = (bf16[512]{0:T(512)(128)(2,1)S(1)}, bf16[512]{0:T(512)(128)(2,1)}, u32[]{:S(2)}) copy-start(bf16[512]{0:T(512)(128)(2,1)} %param.40) | copy-start | bytes 3076
  0.7 11.9 %copy-start.43 = (bf16[512]{0:T(512)(128)(2,1)S(1)}, bf16[512]{0:T(512)(128)(2,1)}, u32[]{:S(2)}) copy-start(bf16[512]{0:T(512)(128)(2,1)} %param.41) | copy-start | bytes 3076
  0.7 11.9 %copy-start.44 = (bf16[512]{0:T(512)(128)(2,1)S(1)}, bf16[512]{0:T(512)(128)(2,1)}, u32[]{:S(2)}) copy-start(bf16[512]{0:T(512)(128)(2,1)} %param.45) | copy-start | bytes 3076
  0.7 12.6 %copy-start.37 = (bf16[2048]{0:T(1024)(128)(2,1)S(1)}, bf16[2048]{0:T(1024)(128)(2,1)}, u32[]{:S(2)}) copy-start(bf16[2048]{0:T(1024)(128)(2,1)} %param.43) | copy-start | bytes 12292
  1.5 15.4 %copy-start.33 = (bf16[7,7,992]{2,1,0:T(8,128)(2,1)S(1)}, bf16[7,7,992]{2,1,0:T(8,128)(2,1)}, u32[]{:S(2)}) copy-start(bf16[7,7,992]{2,1,0:T(8,128)(2,1)} %param.33) | copy-start | bytes 291652
  1.5 18.2 %copy-start.32 = (f32[672,49]{1,0:T(8,128)S(1)}, f32[672,49]{1,0:T(8,128)}, u32[]{:S(2)}) copy-start(f32[672,49]{1,0:T(8,128)} %constant.124.clone) | copy-start | bytes 395140
  3.2 13.5 %collective-permute-start = (bf16[3,40,512]{2,1,0:T(8,128)(2,1)S(1)}, bf16[3,40,512]{2,1,0:T(8,128)(2,1)S(1)}, u32[]{:S(2)}, u32[]{:S(2)}) collective-permute-start(bf16[3,40,512]{2,1,0:T(8,128)(2,1)S(1)} %get-tuple-element.294), channel_id=1, source_target_pairs={{0,8},{8,16},{16,24},{1,9},{9,17},{17,25},{2,10},{10,18},{18,26},{... | collective-permute-start | bytes 368648 | tf_op jit(solution)/shard_map/ppermute | solution.py:632
  8.0 8.6 %collective-permute-start.1 = (bf16[3,40,512]{2,1,0:T(8,128)(2,1)S(1)}, bf16[3,40,512]{2,1,0:T(8,128)(2,1)S(1)}, u32[]{:S(2)}, u32[]{:S(2)}) collective-permute-start(bf16[3,40,512]{2,1,0:T(8,128)(2,1)S(1)} %get-tuple-element.295), channel_id=1, source_target_pairs={{8,0},{16,8},{24,16},{9,1},{17,9},{25,17},{10,2},{18,10},{26,18},{... | collective-permute-start | bytes 368648 | tf_op jit(solution)/shard_map/ppermute | solution.py:632
  16.9 7.0 %collective-permute-start.2 = (bf16[38,3,512]{2,1,0:T(4,128)(2,1)S(1)}, bf16[38,3,512]{2,1,0:T(4,128)(2,1)S(1)}, u32[]{:S(2)}, u32[]{:S(2)}) collective-permute-start(bf16[38,3,512]{2,1,0:T(4,128)(2,1)S(1)} %get-tuple-element.161), channel_id=1, source_target_pairs={{0,1},{1,2},{2,3},{3,4},{4,5},{5,6},{6,7},{8,9},{9,10},{10,11},{11... | collective-permute-start | bytes 350216 | tf_op jit(solution)/shard_map/ppermute | solution.py:640
  18.4 5.6 %collective-permute-start.3 = (bf16[38,3,512]{2,1,0:T(4,128)(2,1)S(1)}, bf16[38,3,512]{2,1,0:T(4,128)(2,1)S(1)}, u32[]{:S(2)}, u32[]{:S(2)}) collective-permute-start(bf16[38,3,512]{2,1,0:T(4,128)(2,1)S(1)} %get-tuple-element.162), channel_id=1, source_target_pairs={{1,0},{2,1},{3,2},{4,3},{5,4},{6,5},{7,6},{9,8},{10,9},{11,10},{12... | collective-permute-start | bytes 350216 | tf_op jit(solution)/shard_map/ppermute | solution.py:640
  27.7 34.1 %copy-start.1 = (f32[1280,1]{1,0:T(8,128)S(1)}, f32[1280,1]{1,0:T(8,128)}, u32[]{:S(2)}) copy-start(f32[1280,1]{1,0:T(8,128)} %copy.44.valid) | copy-start | bytes 15364
  27.7 34.1 %copy-start.5 = (f32[8,512]{1,0:T(8,128)S(1)}, f32[8,512]{1,0:T(8,128)}, u32[]{:S(2)}) copy-start(f32[8,512]{1,0:T(8,128)} %convert_element_type.173.vecs) | copy-start | bytes 49156
  27.7 34.1 %copy-start.8 = (bf16[32,40,512]{2,1,0:T(8,128)(2,1)S(1)}, bf16[32,40,512]{2,1,0:T(8,128)(2,1)}, u32[]{:S(2)}) copy-start(bf16[32,40,512]{2,1,0:T(8,128)(2,1)} %param.48) | copy-start | bytes 3932164
  61.9 21.6 %copy-start.3 = (bf16[128,128]{1,0:T(8,128)(2,1)S(1)}, bf16[128,128]{1,0:T(8,128)(2,1)}, u32[]{:S(2)}) copy-start(bf16[128,128]{1,0:T(8,128)(2,1)} %scatter.9.w2) | copy-start | bytes 98308
  61.9 21.5 %copy-start.4 = (bf16[128,128]{1,0:T(8,128)(2,1)S(1)}, bf16[128,128]{1,0:T(8,128)(2,1)}, u32[]{:S(2)}) copy-start(bf16[128,128]{1,0:T(8,128)(2,1)} %scatter.6.w1) | copy-start | bytes 98308
  61.9 21.5 %copy-start.10 = (bf16[512,512]{1,0:T(8,128)(2,1)S(1)}, bf16[512,512]{1,0:T(8,128)(2,1)}, u32[]{:S(2)}) copy-start(bf16[512,512]{1,0:T(8,128)(2,1)} %out_w.5) | copy-start | bytes 1572868
  61.9 21.5 %copy-start.12 = (bf16[256,512]{1,0:T(8,128)(2,1)S(1)}, bf16[256,512]{1,0:T(8,128)(2,1)}, u32[]{:S(2)}) copy-start(bf16[256,512]{1,0:T(8,128)(2,1)} %w4.3) | copy-start | bytes 786436
  61.9 21.5 %copy-start.13 = (bf16[128,256]{1,0:T(8,128)(2,1)S(1)}, bf16[128,256]{1,0:T(8,128)(2,1)}, u32[]{:S(2)}) copy-start(bf16[128,256]{1,0:T(8,128)(2,1)} %w3.3) | copy-start | bytes 196612
  61.9 21.5 %copy-start.22 = (f32[1280,128]{1,0:T(8,128)S(1)}, f32[1280,128]{1,0:T(8,128)}, u32[]{:S(2)}) copy-start(f32[1280,128]{1,0:T(8,128)} %get-tuple-element.181.lead) | copy-start | bytes 1966084
  80.3 12.9 %collective-permute-start.4 = (bf16[2048,512]{1,0:T(8,128)(2,1)S(1)}, bf16[2048,512]{1,0:T(8,128)(2,1)S(1)}, u32[]{:S(2)}, u32[]{:S(2)}) collective-permute-start(bf16[2048,512]{1,0:T(8,128)(2,1)S(1)} %get-tuple-element.184), channel_id=1, source_target_pairs={{0,1},{1,0},{2,3},{3,2},{4,5},{5,4},{6,7},{7,6},{8,9},{9,8},{10,11... | collective-permute-start | bytes 6291464 | tf_op jit(solution)/shard_map/ppermute | solution.py:547
  83.5 15.7 %copy-start.15 = (f32[56,448]{1,0:T(8,128)S(1)}, f32[56,448]{1,0:T(8,128)}, u32[]{:S(2)}) copy-start(f32[56,448]{1,0:T(8,128)} %constant.128.clone.td) | copy-start | bytes 301060
  83.5 15.6 %copy-start.16 = (bf16[224,64]{1,0:T(8,128)(2,1)S(1)}, bf16[224,64]{1,0:T(8,128)(2,1)}, u32[]{:S(2)}) copy-start(bf16[224,64]{1,0:T(8,128)(2,1)} %constant.127.clone.tg) | copy-start | bytes 86020
  93.2 15.1 %copy-start.20 = (f32[1280,128]{1,0:T(8,128)}, f32[1280,128]{1,0:T(8,128)S(1)}, u32[]{:S(2)}) copy-start(f32[1280,128]{1,0:T(8,128)S(1)} %get-tuple-element.197.glead) | copy-start | bytes 1966084
  93.2 15.1 %copy-start.31 = (bf16[2048,512]{1,0:T(8,128)(2,1)}, bf16[2048,512]{1,0:T(8,128)(2,1)S(1)}, u32[]{:S(2)}) copy-start(bf16[2048,512]{1,0:T(8,128)(2,1)S(1)} %collective-permute-done.4) | copy-start | bytes 6291460
  93.3 15.7 %collective-permute-start.5 = (bf16[3,40,1024]{2,1,0:T(8,128)(2,1)S(1)}, bf16[3,40,1024]{2,1,0:T(8,128)(2,1)S(1)}, u32[]{:S(2)}, u32[]{:S(2)}) collective-permute-start(bf16[3,40,1024]{2,1,0:T(8,128)(2,1)S(1)} %bitcast.31), channel_id=1, source_target_pairs={{0,8},{8,16},{16,24},{1,9},{9,17},{17,25},{2,10},{10,18},{18,26},{... | collective-permute-start | bytes 737288 | tf_op jit(solution)/shard_map/ppermute | solution.py:632
  97.8 13.5 %collective-permute-start.6 = (bf16[3,40,1024]{2,1,0:T(8,128)(2,1)S(1)}, bf16[3,40,1024]{2,1,0:T(8,128)(2,1)S(1)}, u32[]{:S(2)}, u32[]{:S(2)}) collective-permute-start(bf16[3,40,1024]{2,1,0:T(8,128)(2,1)S(1)} %bitcast.30), channel_id=1, source_target_pairs={{8,0},{16,8},{24,16},{9,1},{17,9},{25,17},{10,2},{18,10},{26,18},{... | collective-permute-start | bytes 737288 | tf_op jit(solution)/shard_map/ppermute | solution.py:632
  113.1 6.8 %collective-permute-start.7 = (bf16[38,3,1024]{2,1,0:T(4,128)(2,1)}, bf16[38,3,1024]{2,1,0:T(4,128)(2,1)}, u32[]{:S(2)}, u32[]{:S(2)}) collective-permute-start(bf16[38,3,1024]{2,1,0:T(4,128)(2,1)} %get-tuple-element.191), channel_id=1, source_target_pairs={{0,1},{1,2},{2,3},{3,4},{4,5},{5,6},{6,7},{8,9},{9,10},{10,11},{11... | collective-permute-start | bytes 700424 | tf_op jit(solution)/shard_map/ppermute | solution.py:640
  115.1 5.2 %collective-permute-start.8 = (bf16[38,3,1024]{2,1,0:T(4,128)(2,1)}, bf16[38,3,1024]{2,1,0:T(4,128)(2,1)}, u32[]{:S(2)}, u32[]{:S(2)}) collective-permute-start(bf16[38,3,1024]{2,1,0:T(4,128)(2,1)} %get-tuple-element.192), channel_id=1, source_target_pairs={{1,0},{2,1},{3,2},{4,3},{5,4},{6,5},{7,6},{9,8},{10,9},{11,10},{12... | collective-permute-start | bytes 700424 | tf_op jit(solution)/shard_map/ppermute | solution.py:640
  121.5 14.9 %collective-permute-start.9 = (bf16[1024,512]{1,0:T(8,128)(2,1)S(1)}, bf16[1024,512]{1,0:T(8,128)(2,1)S(1)}, u32[]{:S(2)}, u32[]{:S(2)}) collective-permute-start(bf16[1024,512]{1,0:T(8,128)(2,1)S(1)} %get-tuple-element.198), channel_id=1, source_target_pairs={{0,8},{1,17},{2,10},{3,19},{4,12},{5,21},{6,14},{7,23},{8,0},{9,25... | collective-permute-start | bytes 3145736 | tf_op jit(solution)/shard_map/ppermute | solution.py:547
  136.7 18.0 %collective-permute-start.10 = (bf16[512,512]{1,0:T(8,128)(2,1)S(1)}, bf16[512,512]{1,0:T(8,128)(2,1)S(1)}, u32[]{:S(2)}, u32[]{:S(2)}) collective-permute-start(bf16[512,512]{1,0:T(8,128)(2,1)S(1)} %get-tuple-element.209), channel_id=1, source_target_pairs={{0,16},{1,3},{2,18},{3,1},{4,20},{5,7},{6,22},{7,5},{8,24},{9,11},... | collective-permute-start | bytes 1572872 | tf_op jit(solution)/shard_map/ppermute | solution.py:547
  138.7 17.6 %copy-start.7 = (bf16[2048,512]{1,0:T(8,128)(2,1)S(1)}, bf16[2048,512]{1,0:T(8,128)(2,1)}, u32[]{:S(2)}) copy-start(bf16[2048,512]{1,0:T(8,128)(2,1)} %down_w.7) | copy-start | bytes 6291460
  138.7 17.5 %copy-start.18 = (f32[1280,512]{1,0:T(8,128)S(1)}, f32[1280,512]{1,0:T(8,128)}, u32[]{:S(2)}) copy-start(f32[1280,512]{1,0:T(8,128)} %get-tuple-element.176.middle) | copy-start | bytes 7864324
  147.4 12.2 %collective-permute-start.12 = (bf16[1024,512]{1,0:T(8,128)(2,1)S(1)}, bf16[1024,512]{1,0:T(8,128)(2,1)S(1)}, u32[]{:S(2)}, u32[]{:S(2)}) collective-permute-start(bf16[1024,512]{1,0:T(8,128)(2,1)S(1)} %get-tuple-element.212), channel_id=1, source_target_pairs={{0,1},{1,0},{2,3},{3,2},{4,5},{5,4},{6,7},{7,6},{8,9},{9,8},{10,11... | collective-permute-start | bytes 3145736 | tf_op jit(solution)/shard_map/ppermute | solution.py:547
  154.8 6.4 %collective-permute-start.11 = (bf16[256,512]{1,0:T(8,128)(2,1)S(1)}, bf16[256,512]{1,0:T(8,128)(2,1)S(1)}, u32[]{:S(2)}, u32[]{:S(2)}) collective-permute-start(bf16[256,512]{1,0:T(8,128)(2,1)S(1)} %get-tuple-element.302), channel_id=1, source_target_pairs={{0,2},{1,9},{2,0},{3,11},{4,6},{5,13},{6,4},{7,15},{8,10},{9,1},{1... | collective-permute-start | bytes 786440 | tf_op jit(solution)/shard_map/ppermute | solution.py:547
  161.2 9.2 %collective-permute-start.13 = (bf16[512,512]{1,0:T(8,128)(2,1)S(1)}, bf16[512,512]{1,0:T(8,128)(2,1)S(1)}, u32[]{:S(2)}, u32[]{:S(2)}) collective-permute-start(bf16[512,512]{1,0:T(8,128)(2,1)S(1)} %get-tuple-element.288), channel_id=1, source_target_pairs={{0,8},{1,17},{2,10},{3,19},{4,12},{5,21},{6,14},{7,23},{8,0},{9,25... | collective-permute-start | bytes 1572872 | tf_op jit(solution)/shard_map/ppermute | solution.py:547
  161.3 14.0 %collective-permute-start.14 = (bf16[256,512]{1,0:T(8,128)(2,1)S(1)}, bf16[256,512]{1,0:T(8,128)(2,1)S(1)}, u32[]{:S(2)}, u32[]{:S(2)}) collective-permute-start(bf16[256,512]{1,0:T(8,128)(2,1)S(1)} %add_convert_fusion.9), channel_id=1, source_target_pairs={{0,4},{1,5},{2,6},{3,7},{4,0},{5,1},{6,2},{7,3},{8,12},{9,13},{10,... | collective-permute-start | bytes 786440 | tf_op jit(solution)/shard_map/ppermute | solution.py:547
  175.3 6.4 %collective-permute-start.15 = (bf16[256,512]{1,0:T(8,128)(2,1)S(1)}, bf16[256,512]{1,0:T(8,128)(2,1)S(1)}, u32[]{:S(2)}, u32[]{:S(2)}) collective-permute-start(bf16[256,512]{1,0:T(8,128)(2,1)S(1)} %get-tuple-element.300), channel_id=1, source_target_pairs={{0,16},{1,3},{2,18},{3,1},{4,20},{5,7},{6,22},{7,5},{8,24},{9,11},... | collective-permute-start | bytes 786440 | tf_op jit(solution)/shard_map/ppermute | solution.py:547
  177.1 6.5 %collective-permute-start.16 = (bf16[256,512]{1,0:T(8,128)(2,1)S(1)}, bf16[256,512]{1,0:T(8,128)(2,1)S(1)}, u32[]{:S(2)}, u32[]{:S(2)}) collective-permute-start(bf16[256,512]{1,0:T(8,128)(2,1)S(1)} %add_convert_fusion.6), channel_id=1, source_target_pairs={{0,2},{1,9},{2,0},{3,11},{4,6},{5,13},{6,4},{7,15},{8,10},{9,1},{1... | collective-permute-start | bytes 786440 | tf_op jit(solution)/shard_map/ppermute | solution.py:547
  183.7 9.2 %collective-permute-start.18 = (bf16[512,512]{1,0:T(8,128)(2,1)S(1)}, bf16[512,512]{1,0:T(8,128)(2,1)S(1)}, u32[]{:S(2)}, u32[]{:S(2)}) collective-permute-start(bf16[512,512]{1,0:T(8,128)(2,1)S(1)} %pad_maximum_fusion.3), channel_id=1, source_target_pairs={{0,16},{1,3},{2,18},{3,1},{4,20},{5,7},{6,22},{7,5},{8,24},{9,11},... | collective-permute-start | bytes 1572872 | tf_op jit(solution)/shard_map/ppermute | solution.py:547
  184.8 5.7 %collective-permute-start.17 = (bf16[128,512]{1,0:T(8,128)(2,1)}, bf16[128,512]{1,0:T(8,128)(2,1)S(1)}, u32[]{:S(2)}, u32[]{:S(2)}) collective-permute-start(bf16[128,512]{1,0:T(8,128)(2,1)} %get-tuple-element.308), channel_id=1, source_target_pairs={{0,2},{1,9},{2,0},{3,11},{4,6},{5,13},{6,4},{7,15},{8,10},{9,1},{1... | collective-permute-start | bytes 393224 | tf_op jit(solution)/shard_map/ppermute | solution.py:547
  193.1 16.4 %collective-permute-start.21 = (bf16[1024,512]{1,0:T(8,128)(2,1)S(1)}, bf16[1024,512]{1,0:T(8,128)(2,1)}, u32[]{:S(2)}, u32[]{:S(2)}) collective-permute-start(bf16[1024,512]{1,0:T(8,128)(2,1)S(1)} %pad_maximum_fusion.1), channel_id=1, source_target_pairs={{0,8},{1,17},{2,10},{3,19},{4,12},{5,21},{6,14},{7,23},{8,0},{9,25... | collective-permute-start | bytes 3145736 | tf_op jit(solution)/shard_map/ppermute | solution.py:547
  193.5 8.9 %collective-permute-start.19 = (bf16[128,512]{1,0:T(8,128)(2,1)S(1)}, bf16[128,512]{1,0:T(8,128)(2,1)S(1)}, u32[]{:S(2)}, u32[]{:S(2)}) collective-permute-start(bf16[128,512]{1,0:T(8,128)(2,1)S(1)} %add_convert_fusion.13), channel_id=1, source_target_pairs={{0,4},{1,5},{2,6},{3,7},{4,0},{5,1},{6,2},{7,3},{8,12},{9,13},{10,... | collective-permute-start | bytes 393224 | tf_op jit(solution)/shard_map/ppermute | solution.py:547
  202.4 5.0 %collective-permute-start.20 = (bf16[128,512]{1,0:T(8,128)(2,1)S(1)}, bf16[128,512]{1,0:T(8,128)(2,1)S(1)}, u32[]{:S(2)}, u32[]{:S(2)}) collective-permute-start(bf16[128,512]{1,0:T(8,128)(2,1)S(1)} %add_convert_fusion.12), channel_id=1, source_target_pairs={{0,2},{1,9},{2,0},{3,11},{4,6},{5,13},{6,4},{7,15},{8,10},{9,1},{1... | collective-permute-start | bytes 393224 | tf_op jit(solution)/shard_map/ppermute | solution.py:547
  210.9 7.1 %collective-permute-start.23 = (bf16[2048,512]{1,0:T(8,128)(2,1)S(1)}, bf16[2048,512]{1,0:T(8,128)(2,1)S(1)}, u32[]{:S(2)}, u32[]{:S(2)}) collective-permute-start(bf16[2048,512]{1,0:T(8,128)(2,1)S(1)} %pad_maximum_fusion.own), channel_id=1, source_target_pairs={{0,1},{1,0},{2,3},{3,2},{4,5},{5,4},{6,7},{7,6},{8,9},{9,8},{10,11... | collective-permute-start | bytes 6291464 | tf_op jit(solution)/shard_map/ppermute | solution.py:547
  211.0 6.4 %collective-permute-start.22 = (bf16[256,512]{1,0:T(8,128)(2,1)S(1)}, bf16[256,512]{1,0:T(8,128)(2,1)S(1)}, u32[]{:S(2)}, u32[]{:S(2)}) collective-permute-start(bf16[256,512]{1,0:T(8,128)(2,1)S(1)} %pad_maximum_fusion.8), channel_id=1, source_target_pairs={{0,16},{1,3},{2,18},{3,1},{4,20},{5,7},{6,22},{7,5},{8,24},{9,11},... | collective-permute-start | bytes 786440 | tf_op jit(solution)/shard_map/ppermute | solution.py:547
  217.5 9.2 %collective-permute-start.24 = (bf16[512,512]{1,0:T(8,128)(2,1)S(1)}, bf16[512,512]{1,0:T(8,128)(2,1)S(1)}, u32[]{:S(2)}, u32[]{:S(2)}) collective-permute-start(bf16[512,512]{1,0:T(8,128)(2,1)S(1)} %pad_maximum_fusion.4), channel_id=1, source_target_pairs={{0,8},{1,17},{2,10},{3,19},{4,12},{5,21},{6,14},{7,23},{8,0},{9,25... | collective-permute-start | bytes 1572872 | tf_op jit(solution)/shard_map/ppermute | solution.py:547
  226.9 2.7 %collective-permute-start.25 = (bf16[1024,512]{1,0:T(8,128)(2,1)S(1)}, bf16[1024,512]{1,0:T(8,128)(2,1)S(1)}, u32[]{:S(2)}, u32[]{:S(2)}) collective-permute-start(bf16[1024,512]{1,0:T(8,128)(2,1)S(1)} %pad_maximum_fusion.2.own), channel_id=1, source_target_pairs={{0,1},{1,0},{2,3},{3,2},{4,5},{5,4},{6,7},{7,6},{8,9},{9,8},{10,11... | collective-permute-start | bytes 3145736 | tf_op jit(solution)/shard_map/ppermute | solution.py:547
  (24 other events, 112.9 us)

commit v2 on v1

--- a/solution.py
+++ b/solution.py
@@ -122,6 +122,27 @@
     cumulative = 0.5 + 0.5 * lax.erf(x * math.sqrt(0.5))
     density = jnp.exp(-0.5 * x * x) * (1.0 / math.sqrt(2.0 * math.pi))
     return x * cumulative, cumulative + x * density
+
+
+UP, DOWN, LEFT, RIGHT = range(4)
+
+
+def fill(source, near, outside, above, own, below):
+    edge, body = above.shape[0], own.shape[0]
+    source[0:edge, :] = jnp.where(near[UP] != 0, above[...].astype(F32), outside)
+    source[edge : edge + body, :] = own[...].astype(F32)
+    source[edge + body : 2 * edge + body, :] = jnp.where(near[DOWN] != 0, below[...].astype(F32), outside)
+
+
+def widen(ext, lanes, near, outside, source, left, right, first_row, rows):
+    for r in range(rows):
+        row = first_row + r
+        line = source[pl.ds(pl.multiple_of(row * 40, 8), 40), :]
+        depth = line.shape[1]
+        before = jnp.where(near[LEFT] != 0, left[row].astype(F32), outside)
+        after = jnp.where(near[RIGHT] != 0, right[row].astype(F32), outside)
+        pieces = [before, line, after, jnp.full((2, depth), outside, F32)]
+        ext[pl.ds(pl.multiple_of(row * 48, 8), 48), lanes] = jnp.concatenate(pieces, axis=0)
 
 
 def depthwise(ext, first_row, spec, tx, ty, waves, mixed_waves, result_ref, kept=None):
@@ -169,20 +190,73 @@
 GAIN_1, SHIFT_1, SCALE_1, GAIN_2, SHIFT_2, SCALE_2 = range(6)
 
 
+def copies(pairs, sems):
+    return [pltpu.make_async_copy(src, dst, sems.at[k]) for k, (src, dst) in enumerate(pairs)]
+
+
+class Sender:
+    def __init__(self, hbm, slots, sems, step):
+        self.hbm, self.slots, self.sems, self.step = hbm, slots, sems, step
+        self.rows = slots.shape[1]
+        self.slot = lax.rem(step, 2)
+        self.ref = slots.at[self.slot]
+
+    def copy(self, step, slot):
+        at = pl.ds(pl.multiple_of(step * self.rows, 16), self.rows)
+        return pltpu.make_async_copy(self.slots.at[slot], self.hbm.at[at, :], self.sems.at[slot])
+
+    def free(self):
+        pl.when(self.step >= 2)(lambda: self.copy(self.step - 2, self.slot).wait())
+
+    def start(self):
+        self.copy(self.step, self.slot).start()
+
+    def finish(self):
+        self.copy(self.step - 1, 1 - self.slot).wait()
+        self.copy(self.step, self.slot).wait()
+
+
 def forward_kernel(
-    x_ext, x_own, valid, cot, vecs, up_bias, in_w, w1, w2, w3, w4, out_w, up_w, spec, tx, ty,
-    waves_out, spread, prods, lead_out, middle_out, active_out, slope_out, grad_down,
+    near, x_own, valid, cot, vecs, up_bias, w1, w2, w3, tx, ty,
+    x_above, x_marked, x_below, x_left, x_right, in_hbm, spec_hbm, w4_hbm, out_hbm, up_hbm,
+    waves_hbm, spread_hbm, prods_hbm, lead_out, middle_out, active_hbm, slope_hbm, down_hbm,
     ext, waves, mixed_waves, active_all, gdown_all,
+    x_source, x_ext, in_w, spec, w4, out_w, up_w, waves_slots, spread_slots, prods_slots, slope_slots, grad_down,
+    in_sems, waves_sems, spread_sems, prods_sems, slope_sems, active_sems, down_sems,
 ):
     step = pl.program_id(0)
+    last = pl.num_programs(0) - 1
     span = 48
-    chunk = spread.shape[0]
+    chunk = lead_out.shape[0]
     gain = vecs[GAIN_1 : GAIN_1 + 1, :]
     shift = vecs[SHIFT_1 : SHIFT_1 + 1, :]
+    loads = copies(
+        [(in_hbm, in_w), (spec_hbm.at[: 3 * SLOTS, :], spec), (w4_hbm, w4), (out_hbm, out_w), (up_hbm, up_w)],
+        in_sems,
+    )
+
+    def begin():
+        for load in loads:
+            load.start()
+
+    pl.when(step == 0)(begin)
+
+    def arrived(*which):
+        def wait():
+            for k in which:
+                loads[k].wait()
+
+        pl.when(step == 0)(wait)
+
+    waves_to = Sender(waves_hbm, waves_slots, waves_sems, step)
+    spread_to = Sender(spread_hbm, spread_slots, spread_sems, step)
+    prods_to = Sender(prods_hbm, prods_slots, prods_sems, step)
+    slope_to = Sender(slope_hbm, slope_slots, slope_sems, step)
+    spread, prods = spread_to.ref, prods_to.ref
 
     def project(start, rows):
         at = pl.ds(start, rows)
-        values = x_ext[at, :].astype(F32)
+        values = x_ext[at, :]
         normal, _ = normalize(values)
         normed = jnp.where(values[:, :1] < 0.5 * OUTSIDE, normal * gain + shift, 0.0).astype(BF16)
         for block in range(2):
@@ -193,13 +267,24 @@
             low = joined.astype(BF16)
             ext[at, lanes] = low.astype(F32)
 
+    arrived(0)
+
     @pl.when(step == 0)
     def _():
+        fill(x_source, near, OUTSIDE, x_above, x_marked, x_below)
+        widen(x_ext, slice(0, 512), near, OUTSIDE, x_source, x_left, x_right, 0, 6)
         project(0, 6 * span)
 
+    widen(x_ext, slice(0, 512), near, OUTSIDE, x_source, x_left, x_right, OUT * step + 6, OUT)
+
     project(pl.multiple_of((OUT * step + 6) * span, 16), OUT * span)
 
-    depthwise(ext, OUT * step, spec, tx, ty, waves, mixed_waves, spread, waves_out)
+    arrived(1)
+    waves_to.free()
+    spread_to.free()
+    depthwise(ext, OUT * step, spec, tx, ty, waves, mixed_waves, spread, waves_to.ref)
+    waves_to.start()
+    spread_to.start()
 
     lead = jnp.concatenate(
         [
@@ -211,10 +296,13 @@
     lead = pltpu.roll(lead, 32, 1)
     lead_out[...] = lead
     mixed = lead * spread[:, :128]
+    arrived(2, 3)
+    prods_to.free()
     for weight, lo, hi in ((w1, 0, 128), (w2, 128, 256), (w3, 256, 512), (w4, 512, 1024)):
         produced = dot(mixed.astype(BF16), weight[...])
         prods[:, lo:hi] = produced
         mixed = produced * spread[:, lo:hi]
+    prods_to.start()
     branch = dot(mixed.astype(BF16), out_w[...])
     middle = x_own[...].astype(F32) + vecs[SCALE_1 : SCALE_1 + 1, :] * branch
     middle_out[...] = middle
@@ -223,21 +311,39 @@
         (normal * vecs[GAIN_2 : GAIN_2 + 1, :] + vecs[SHIFT_2 : SHIFT_2 + 1, :]) * valid[...]
     ).astype(BF16)
     rows = pl.ds(pl.multiple_of(step * chunk, 16), chunk)
+    arrived(4)
+    slope_to.free()
     for block in range(4):
         lanes = slice(512 * block, 512 * block + 512)
         pre = dot(normed, up_w[:, lanes]) + up_bias[:, lanes]
         active, slope = gelu_pair(pre)
-        active = active.astype(BF16)
-        active_out[:, lanes] = active
-        active_all[rows, lanes] = active
-        slope_out[:, lanes] = slope.astype(BF16)
+        active_all[rows, lanes] = active.astype(BF16)
+        slope_to.ref[:, lanes] = slope.astype(BF16)
+    slope_to.start()
     gdown_all[rows, :] = (cot[...].astype(F32) * vecs[SCALE_2 : SCALE_2 + 1, :]).astype(BF16)
 
-    @pl.when(step == pl.num_programs(0) - 1)
-    def _():
+    def active_copy(number):
+        at = pl.ds(pl.multiple_of(number * chunk, 16), chunk)
+        return pltpu.make_async_copy(active_all.at[at, :], active_hbm.at[at, :], active_sems.at[number])
+
+    active_copy(step).start()
+
+    @pl.when(step == last)
+    def _():
+        parts = []
         for block in range(4):
             lanes = slice(512 * block, 512 * block + 512)
             grad_down[lanes, :] = dot_left(gdown_all[...], active_all[:, lanes]).astype(BF16)
+            parts.append(
+                pltpu.make_async_copy(grad_down.at[lanes, :], down_hbm.at[lanes, :], down_sems.at[block])
+            )
+            parts[-1].start()
+        for sender in (waves_to, spread_to, prods_to, slope_to):
+            sender.finish()
+        for number in range(active_sems.shape[0]):
+            active_copy(number).wait()
+        for part in parts:
+            part.wait()
 
 
 def ffn_back_kernel(
@@ -279,7 +385,7 @@
             for block in range(4):
                 lanes = slice(512 * block, 512 * block + 512)
                 for_up[lanes, :] = dot_left(normed_all[...], gpre_all[:, lanes]).astype(BF16)
-            for_down[...] = grad_down[...]
+            for_down[: grad_down.shape[0], :] = grad_down[...]
 
         even = lax.axis_index("col") % 2 == 0
         pl.when(even)(lambda: finish(sent, kept))
@@ -287,9 +393,9 @@
 
 
 def mixer_back_kernel(
-    gmiddle, spread, prods, lead, vecs, w1, w2, w3, w4, out_w,
-    gspread, glead, grads,
-    d_out, d_4, d_3, d_2, d_1,
+    gmiddle, spread, prods, lead, vecs, w1, w2, w3, w4, out_w, sent_before, kept_before,
+    gspread, glead, sent, kept,
+    d_out, d_4, d_3, d_2, d_1, grads, sems,
 ):
     step = pl.program_id(0)
 
@@ -320,11 +426,32 @@
 
     @pl.when(step == pl.num_programs(0) - 1)
     def _():
-        grads[0:512, :] = d_out[...].astype(BF16)
-        grads[512:768, :] = d_4[...].astype(BF16)
-        grads[768:896, 0:256] = d_3[...].astype(BF16)
-        grads[768:896, 256:384] = d_2[...].astype(BF16)
-        grads[768:896, 384:512] = d_1[...].astype(BF16)
+        grads[0:448, :] = d_out[0:448, :].astype(BF16)
+        grads[448:512, :] = jnp.zeros((64, 512), BF16)
+        grads[512:576, :] = d_out[448:512, :].astype(BF16)
+        grads[576:832, :] = d_4[...].astype(BF16)
+        grads[832:960, 0:256] = d_3[...].astype(BF16)
+        grads[832:960, 256:384] = d_2[...].astype(BF16)
+        grads[832:960, 384:512] = d_1[...].astype(BF16)
+        grads[960:1024, :] = jnp.zeros((64, 512), BF16)
+        start = sent.shape[0] - 512
+
+        def finish(first, second):
+            parts = copies(
+                [
+                    (grads.at[0:512, :], first.at[start : start + 512, :]),
+                    (grads.at[512:1024, :], second.at[start : start + 512, :]),
+                ],
+                sems,
+            )
+            for part in parts:
+                part.start()
+            for part in parts:
+                part.wait()
+
+        even = lax.axis_index("col") % 2 == 0
+        pl.when(even)(lambda: finish(kept, sent))
+        pl.when(jnp.logical_not(even))(lambda: finish(sent, kept))
 
 
 def down_kernel(active, middle, vecs, down_w, before, outputs):
@@ -379,26 +506,24 @@
         out[...] = jnp.concatenate([taps[:, :512], taps[:, 512:]], axis=0).astype(BF16)
 
 
-def gates_back_kernel(gs_ext, glead, spec, tx, ty, gjoined, ext, waves, mixed_waves, ggates):
+def gates_back_kernel(
+    near, above, own, below, left, right, glead, spec, tx, ty, gjoined, source, ext, waves, mixed_waves, ggates
+):
     step = pl.program_id(0)
-    span = 48
-
-    def widen(start, count):
-        at = pl.ds(start, count)
-        ext[at, :] = gs_ext[at, :].astype(F32)
 
     @pl.when(step == 0)
     def _():
-        widen(0, 6 * span)
-
-    widen(pl.multiple_of((OUT * step + 6) * span, 16), OUT * span)
+        fill(source, near, 0.0, above, own, below)
+        widen(ext, slice(0, 1024), near, 0.0, source, left, right, 0, 6)
+
+    widen(ext, slice(0, 1024), near, 0.0, source, left, right, OUT * step + 6, OUT)
     depthwise(ext, OUT * step, spec, tx, ty, waves, mixed_waves, ggates)
     gjoined[:, :128] = (ggates[:, :128] + glead[...]).astype(BF16)
     gjoined[:, 128:] = ggates[:, 128:].astype(BF16)
 
 
 def in_back_kernel(
-    gjoined, x_own, gmiddle, valid, vecs, in_w, mixer_grads, grad_kernel, ffn_sums, bias_sum,
+    gjoined, x_own, gmiddle, valid, vecs, in_w, grad_kernel, ffn_sums, bias_sum,
     ginput, sent, kept,
     normed_all, gjoined_all, vec_sums,
 ):
@@ -423,61 +548,64 @@
 
     @pl.when(step == pl.num_programs(0) - 1)
     def _():
-        def finish(for_in, for_others):
-            for block in range(2):
-                lanes = slice(512 * block, 512 * block + 512)
-                for_in[lanes, :] = dot_left(normed_all[...], gjoined_all[:, lanes]).astype(BF16)
-            for_others[0:896, :] = mixer_grads[...]
-            for_others[896:1008, :] = grad_kernel[...]
+        def finish(first, second):
+            first[0:512, :] = dot_left(normed_all[...], gjoined_all[:, 0:512]).astype(BF16)
+            block = dot_left(normed_all[...], gjoined_all[:, 512:1024]).astype(BF16)
+            first[512:576, :] = block[0:64, :]
+            second[0:448, :] = block[64:512, :]
+            second[448:560, :] = grad_kernel[...]
             pieces = [vec_sums[0:2, :], ffn_sums[0:2, :]]
             pieces += [bias_sum[0:1, 512 * k : 512 * k + 512] for k in range(4)]
             pieces.append(jnp.zeros((8, 512), F32))
-            for_others[1008:1024, :] = jnp.concatenate(pieces, axis=0).astype(BF16)
+            second[560:576, :] = jnp.concatenate(pieces, axis=0).astype(BF16)
 
         even = lax.axis_index("col") % 2 == 0
         pl.when(even)(lambda: finish(kept, sent))
         pl.when(jnp.logical_not(even))(lambda: finish(sent, kept))
 
 
-def expand_ffn_kernel(own, got, down_w, vecs, grad_down, grad_up, grad_scale):
+def expand_early_kernel(
+    own, got, down_w, out_w, vecs,
+    grad_down, grad_up, scale_2, grad_out, grad_4, grad_3, grad_2, grad_1, scale_1,
+):
     step = pl.program_id(0)
 
     @pl.when(step == 0)
     def _():
-        grad_scale[...] = jnp.zeros_like(grad_scale)
-
-    def expand(down, up):
-        block = down[...].astype(F32).T
-        grad_down[...] = block
-        grad_up[...] = up[...].astype(F32)
-        grad_scale[...] += jnp.sum(block * down_w[...].astype(F32), axis=0, keepdims=True)
+        scale_2[...] = jnp.zeros_like(scale_2)
+
+    def expand(first, second):
+        @pl.when(step < 4)
+        def _():
+            block = first[...].astype(F32).T
+            grad_down[...] = block
+            grad_up[...] = second[...].astype(F32)
+            scale_2[...] += jnp.sum(block * down_w[...].astype(F32), axis=0, keepdims=True)
+
+        @pl.when(step == 4)
+        def _():
+            scale_2[...] = scale_2[...] / vecs[SCALE_2 : SCALE_2 + 1, :]
+            grad_out[0:448, :] = first[0:448, :].astype(F32)
+            grad_out[448:512, :] = second[0:64, :].astype(F32)
+            grad_4[...] = second[64:320, :].astype(F32)
+            square = second[320:448, :].astype(F32)
+            grad_3[...] = square[:, 0:256]
+            grad_2[...] = square[64:128, 256:384]
+            grad_1[...] = square[32:64, 384 + 64 : 512]
+            summed = jnp.sum(grad_out[...] * out_w[...].astype(F32), axis=0, keepdims=True)
+            scale_1[...] = summed / vecs[SCALE_1 : SCALE_1 + 1, :]
 
     even = lax.axis_index("col") % 2 == 0
     pl.when(even)(lambda: expand(own, got))
     pl.when(jnp.logical_not(even))(lambda: expand(got, own))
 
-    @pl.when(step == pl.num_programs(0) - 1)
-    def _():
-        grad_scale[...] = grad_scale[...] / vecs[SCALE_2 : SCALE_2 + 1, :]
-
-
-def expand_rest_kernel(
-    own, got, out_w, vecs, grad_in, grad_conv, grad_1, grad_2, grad_3, grad_4, grad_out,
-    gain_1, shift_1, scale_1, gain_2, shift_2, grad_bias,
-):
-    def expand(first, other):
+
+def expand_late_kernel(own, got, grad_in, grad_conv, gain_1, shift_1, gain_2, shift_2, grad_bias):
+    def expand(first, second):
         grad_in[:, :512] = first[:512, :].astype(F32)
-        grad_in[:, 512:] = first[512:, :].astype(F32)
-        block = other[:512, :].astype(F32)
-        grad_out[...] = block
-        scaled = jnp.sum(block * out_w[...].astype(F32), axis=0, keepdims=True)
-        scale_1[...] = scaled / vecs[SCALE_1 : SCALE_1 + 1, :]
-        grad_4[...] = other[512:768, :].astype(F32)
-        square = other[768:896, :].astype(F32)
-        grad_3[...] = square[:, 0:256]
-        grad_2[...] = square[64:128, 256:384]
-        grad_1[...] = square[32:64, 384 + 64 : 512]
-        tail = other[896:1024, :].astype(F32)
+        grad_in[0:64, 512:] = first[512:576, :].astype(F32)
+        grad_in[64:512, 512:] = second[0:448, :].astype(F32)
+        tail = second[448:576, :].astype(F32)
         taps = jnp.concatenate([tail[:56], tail[56:112]], axis=1)[:, 32:]
         for row in range(TAPS):
             grad_conv[row] = taps[TAPS * row : TAPS * row + TAPS]
@@ -631,29 +759,31 @@
     def rows_around(block):
         return lax.ppermute(block[-HALO:], "row", down_pairs), lax.ppermute(block[:HALO], "row", up_pairs)
 
-    def taller(above, block, below, outside):
-        blank = jnp.asarray(outside, BF16)
-        above, below = jnp.where(same_up, above, blank), jnp.where(same_down, below, blank)
-        return jnp.concatenate([above, block, below], axis=0)
-
-    def cols_around(from_left, from_right):
-        return lax.ppermute(from_left, "col", right_pairs), lax.ppermute(from_right, "col", left_pairs)
-
-    def wider(left, tall, right, outside):
-        depth = tall.shape[-1]
-        blank = jnp.asarray(outside, BF16)
-        left, right = jnp.where(same_left, left, blank), jnp.where(same_right, right, blank)
-        filler = jnp.full((ext_rows, span - tile_cols - 2 * HALO, depth), blank)
-        return jnp.concatenate([left, tall, right, filler], axis=1).reshape(ext_pixels, depth)
+    def cols_around(above, below, block):
+        def side(cols):
+            return jnp.concatenate([above[:, cols], block[:, cols], below[:, cols]], axis=0)
+
+        last, first = slice(tile_cols - HALO, tile_cols), slice(0, HALO)
+        return lax.ppermute(side(last), "col", right_pairs), lax.ppermute(side(first), "col", left_pairs)
+
+    near = jnp.stack([same_up, same_down, same_left, same_right]).astype(jnp.int32)
+
+    def masked(pair, marks, outside):
+        return tuple(jnp.where(mark, block, jnp.asarray(outside, BF16)) for block, mark in zip(pair, marks))
+
+    def flat(block):
+        return block.reshape(block.shape[0] * block.shape[1], block.shape[2])
 
     marked = jnp.where(valid_pixels[..., None] != 0, activations, jnp.asarray(OUTSIDE, BF16))
+    taps = jnp.pad(conv_kernel.astype(F32).reshape(TAPS * TAPS, gate_count), ((0, 0), (lead_count, 0)))
+    spec = jnp.dot(tab["spectrum"], taps, precision=lax.Precision.HIGHEST, preferred_element_type=F32)
+    w1 = jnp.zeros((128, 128), BF16).at[32:64, 64:128].set(mix_first)
+    w2 = jnp.zeros((128, 128), BF16).at[64:128, :].set(mix_second)
     above, below = rows_around(marked)
-    tall = taller(above, marked, below, OUTSIDE)
-    sides = tall[:, -HALO:], tall[:, :HALO]
-    (sides, conv_kernel, mix_first, mix_second, valid_pixels) = lax.optimization_barrier(
-        (sides, conv_kernel, mix_first, mix_second, valid_pixels)
+    (above, below, spec, w1, w2, valid_pixels) = lax.optimization_barrier(
+        (above, below, spec, w1, w2, valid_pixels)
     )
-    left, right = cols_around(*sides)
+    left, right = cols_around(*masked((above, below), (same_up, same_down), OUTSIDE), marked)
 
     x_own = activations.reshape(pixels, width)
     cot = cotangent.reshape(pixels, width)
@@ -662,34 +792,29 @@
         [gain_first, shift_first, scale_mixer, gain_second, shift_second, scale_mlp, scale_mlp, scale_mlp]
     ).astype(F32)
     bias = up_bias.astype(F32).reshape(1, hidden)
-    taps = jnp.pad(conv_kernel.astype(F32).reshape(TAPS * TAPS, gate_count), ((0, 0), (lead_count, 0)))
-    spec = jnp.dot(tab["spectrum"], taps, precision=lax.Precision.HIGHEST, preferred_element_type=F32)
-    w1 = jnp.zeros((128, 128), BF16).at[32:64, 64:128].set(mix_first)
-    w2 = jnp.zeros((128, 128), BF16).at[64:128, :].set(mix_second)
     w3, w4 = mix_third, mix_fourth
-    (left, right, spec, w1, w2, valid, vecs, bias) = lax.optimization_barrier(
-        (left, right, spec, w1, w2, valid, vecs, bias)
-    )
-    x_ext = wider(left, tall, right, OUTSIDE)
+    (left, right, valid, vecs, bias) = lax.optimization_barrier((left, right, valid, vecs, bias))
+    x_source = flat(above), flat(marked), flat(below), left, right
 
     chunk = OUT * tile_cols
     steps = tile_rows // OUT
+    anywhere = pl.BlockSpec(memory_space=pl.ANY)
+    in_smem = pl.BlockSpec(memory_space=pltpu.SMEM)
     (
         xwaves, spread, prods, lead, middle, active, slope, grad_down,
     ) = pl.pallas_call(
         forward_kernel,
         grid=(steps,),
         in_specs=[
-            whole((ext_pixels, width)), chunked((chunk, width)), chunked((chunk, 1)),
-            chunked((chunk, width)), whole((8, width)), whole((1, hidden)), whole((width, joined_count)),
-            whole((128, 128)), whole((128, 128)), whole(w3.shape), whole(w4.shape), whole((width, width)),
-            whole((width, hidden)), whole((3 * SLOTS, joined_count)), whole(tab["window"].shape),
+            in_smem,
+            chunked((chunk, width)), chunked((chunk, 1)), chunked((chunk, width)), whole((8, width)),
+            whole((1, hidden)), whole((128, 128)), whole((128, 128)), whole(w3.shape), whole(tab["window"].shape),
             whole(tab["tile_back"].shape),
-        ],
+            whole((HALO * tile_cols, width)), whole((pixels, width)), whole((HALO * tile_cols, width)),
+            whole((ext_rows, HALO, width)), whole((ext_rows, HALO, width)),
+        ] + [anywhere] * 5,
         out_specs=[
-            chunked((2 * SLOTS * TILES, joined_count)), chunked((chunk, joined_count)),
-            chunked((chunk, joined_count)), chunked((chunk, 128)), chunked((chunk, width)), chunked((chunk, hidden)),
-            chunked((chunk, hidden)), held((hidden, width)),
+            anywhere, anywhere, anywhere, chunked((chunk, 128)), chunked((chunk, width)), anywhere, anywhere, anywhere,
         ],
         out_shape=[
             shaped((steps * 2 * SLOTS * TILES, joined_count), BF16), shaped((pixels, joined_count), F32),
@@ -701,30 +826,43 @@
             pltpu.VMEM((ext_pixels, joined_count + 128), F32),
             pltpu.VMEM((2 * SLOTS, LANES * TILES), F32), pltpu.VMEM((2 * SLOTS, LANES * TILES), BF16),
             pltpu.VMEM((pixels, hidden), BF16), pltpu.VMEM((pixels, width), BF16),
+            pltpu.VMEM((ext_rows * tile_cols, width), F32), pltpu.VMEM((ext_pixels, width), F32),
+            pltpu.VMEM((width, joined_count), BF16),
+            pltpu.VMEM((3 * SLOTS, joined_count), F32), pltpu.VMEM(w4.shape, BF16), pltpu.VMEM((width, width), BF16),
+            pltpu.VMEM((width, hidden), BF16), pltpu.VMEM((2, 2 * SLOTS * TILES, joined_count), BF16),
+            pltpu.VMEM((2, chunk, joined_count), F32), pltpu.VMEM((2, chunk, joined_count), F32),
+            pltpu.VMEM((2, chunk, hidden), BF16), pltpu.VMEM((hidden, width), BF16),
+            pltpu.SemaphoreType.DMA((5,)), pltpu.SemaphoreType.DMA((2,)), pltpu.SemaphoreType.DMA((2,)),
+            pltpu.SemaphoreType.DMA((2,)), pltpu.SemaphoreType.DMA((2,)), pltpu.SemaphoreType.DMA((steps,)),
+            pltpu.SemaphoreType.DMA((4,)),
         ],
         compiler_params=params(58),
-        cost_estimate=cost(40),
+        cost_estimate=cost(30),
         name="forward",
     )(
-        x_ext, x_own, valid, cot, vecs, bias, in_weight, w1, w2, w3, w4, out_weight, up_weight,
-        spec, tab["window"], tab["tile_back"],
+        near, x_own, valid, cot, vecs, bias, w1, w2, w3, tab["window"], tab["tile_back"],
+        *x_source, in_weight, spec, w4, out_weight, up_weight,
     )
 
     rows = 256
     count = pixels // rows
+    wide = 640
+    few = pixels // wide
+    early = hidden + width
+    late = 576
     gmiddle, ffn_sent, ffn_kept, ffn_sums, bias_sum = pl.pallas_call(
         ffn_back_kernel,
-        grid=(count,),
+        grid=(few,),
         in_specs=[
-            chunked((rows, width)), chunked((rows, hidden)), chunked((rows, width)), chunked((rows, 1)),
+            chunked((wide, width)), chunked((wide, hidden)), chunked((wide, width)), chunked((wide, 1)),
             whole((8, width)), whole((hidden, width)), whole((width, hidden)), whole((hidden, width)),
         ],
         out_specs=[
-            chunked((rows, width)), held((hidden, width)), held((hidden, width)), held((8, width)),
+            chunked((wide, width)), held((early, width)), held((early, width)), held((8, width)),
             held((8, hidden)),
         ],
         out_shape=[
-            shaped((pixels, width), F32), shaped((hidden, width), BF16), shaped((hidden, width), BF16),
+            shaped((pixels, width), F32), shaped((early, width), BF16), shaped((early, width), BF16),
             shaped((8, width), F32),
             shaped((8, hidden), F32),
         ],
@@ -734,33 +872,34 @@
         name="ffn_back",
     )(cot, slope, middle, valid, vecs, down_weight, up_weight, grad_down)
 
+    gspread, glead, ffn_sent, ffn_kept = pl.pallas_call(
+        mixer_back_kernel,
+        grid=(few,),
+        in_specs=[
+            chunked((wide, width)), chunked((wide, joined_count)), chunked((wide, joined_count)),
+            chunked((wide, 128)), whole((8, width)), whole((128, 128)), whole((128, 128)), whole(w3.shape),
+            whole(w4.shape), whole((width, width)), anywhere, anywhere,
+        ],
+        out_specs=[chunked((wide, joined_count)), chunked((wide, 128)), anywhere, anywhere],
+        out_shape=[
+            shaped((pixels, joined_count), BF16), shaped((pixels, 128), F32), shaped((early, width), BF16),
+            shaped((early, width), BF16),
+        ],
+        input_output_aliases={10: 2, 11: 3},
+        scratch_shapes=[
+            pltpu.VMEM((width, width), F32), pltpu.VMEM(w4.shape, F32), pltpu.VMEM(w3.shape, F32),
+            pltpu.VMEM((128, 128), F32), pltpu.VMEM((128, 128), F32), pltpu.VMEM((2 * width, width), BF16),
+            pltpu.SemaphoreType.DMA((2,)),
+        ],
+        compiler_params=params(48),
+        cost_estimate=cost(9),
+        name="mixer_back",
+    )(gmiddle, spread, prods, lead, vecs, w1, w2, w3, w4, out_weight, ffn_sent, ffn_kept)
+
     reducer = Reducer()
     ffn = reducer.open(ffn_sent, ffn_kept)
     ffn.swap()
-
-    gspread, glead, mixer_grads = pl.pallas_call(
-        mixer_back_kernel,
-        grid=(count,),
-        in_specs=[
-            chunked((rows, width)), chunked((rows, joined_count)), chunked((rows, joined_count)),
-            chunked((rows, 128)), whole((8, width)), whole((128, 128)), whole((128, 128)), whole(w3.shape),
-            whole(w4.shape), whole((width, width)),
-        ],
-        out_specs=[chunked((rows, joined_count)), chunked((rows, 128)), held((896, width))],
-        out_shape=[
-            shaped((pixels, joined_count), BF16), shaped((pixels, 128), F32), shaped((896, width), BF16),
-        ],
-        scratch_shapes=[
-            pltpu.VMEM((width, width), F32), pltpu.VMEM(w4.shape, F32), pltpu.VMEM(w3.shape, F32),
-            pltpu.VMEM((128, 128), F32), pltpu.VMEM((128, 128), F32),
-        ],
-        compiler_params=params(48),
-        cost_estimate=cost(12),
-        name="mixer_back",
-    )(gmiddle, spread, prods, lead, vecs, w1, w2, w3, w4, out_weight)
-
     tie = lax.optimization_barrier
-    (gspread, ffn.kept, ffn.got) = tie((gspread, ffn.kept, ffn.got))
     block = gspread.reshape(tile_rows, tile_cols, joined_count)
     above, below = rows_around(block)
     grad_kernel = pl.pallas_call(
@@ -780,34 +919,34 @@
         cost_estimate=cost(9),
         name="kernel_back",
     )(xwaves, gspread, tab["tile"], tab["kernel_back"])
-    (above, below, grad_kernel, ffn.kept) = tie((above, below, grad_kernel, ffn.kept))
-    tall = taller(above, block, below, 0.0)
-    sides = tall[:, -HALO:], tall[:, :HALO]
-    (sides, ffn.kept) = tie((sides, ffn.kept))
-    left, right = cols_around(*sides)
+    (above, below, grad_kernel, ffn.kept, ffn.got) = tie((above, below, grad_kernel, ffn.kept, ffn.got))
+    left, right = cols_around(*masked((above, below), (same_up, same_down), 0.0), block)
     ffn.combine()
     (left, right, ffn.sent, ffn.kept) = tie((left, right, ffn.sent, ffn.kept))
     ffn.swap()
-    gs_ext = wider(left, tall, right, 0.0)
+    above, below = flat(above), flat(below)
 
     gjoined = pl.pallas_call(
         gates_back_kernel,
         grid=(steps,),
         in_specs=[
-            whole((ext_pixels, joined_count)), chunked((chunk, 128)),
+            in_smem,
+            whole((HALO * tile_cols, joined_count)), whole((pixels, joined_count)),
+            whole((HALO * tile_cols, joined_count)), whole((ext_rows, HALO, joined_count)),
+            whole((ext_rows, HALO, joined_count)), chunked((chunk, 128)),
             pl.BlockSpec((3 * SLOTS, joined_count), lambda i: (1, 0), pipeline_mode=pl.Buffered(1)),
             whole(tab["window"].shape), whole(tab["tile_back"].shape),
         ],
         out_specs=chunked((chunk, joined_count)),
         out_shape=shaped((pixels, joined_count), BF16),
         scratch_shapes=[
-            pltpu.VMEM((ext_pixels, joined_count), F32), pltpu.VMEM((2 * SLOTS, LANES * TILES), F32),
+            pltpu.VMEM((ext_rows * tile_cols, joined_count), F32), pltpu.VMEM((ext_pixels, joined_count), F32), pltpu.VMEM((2 * SLOTS, LANES * TILES), F32),
             pltpu.VMEM((2 * SLOTS, LANES * TILES), BF16), pltpu.VMEM((chunk, joined_count), F32),
         ],
         compiler_params=params(48),
         cost_estimate=cost(11),
         name="gates_back",
-    )(gs_ext, glead, spec, tab["window"], tab["tile_back"])
+    )(near, above, gspread, below, left, right, glead, spec, tab["window"], tab["tile_back"])
     (gjoined, ffn.got) = tie((gjoined, ffn.got))
     ffn.combine()
     (gjoined, ffn.sent, ffn.kept) = tie((gjoined, ffn.sent, ffn.kept))
@@ -815,15 +954,15 @@
 
     ginput, rest_sent, rest_kept = pl.pallas_call(
         in_back_kernel,
-        grid=(count,),
+        grid=(few,),
         in_specs=[
-            chunked((rows, joined_count)), chunked((rows, width)), chunked((rows, width)), chunked((rows, 1)),
-            whole((8, width)), whole((width, joined_count)), whole((896, width)), whole((112, width)),
+            chunked((wide, joined_count)), chunked((wide, width)), chunked((wide, width)), chunked((wide, 1)),
+            whole((8, width)), whole((width, joined_count)), whole((112, width)),
             whole((8, width)), whole((8, hidden)),
         ],
-        out_specs=[chunked((rows, width)), held((joined_count, width)), held((joined_count, width))],
+        out_specs=[chunked((wide, width)), held((late, width)), held((late, width))],
         out_shape=[
-            shaped((pixels, width), BF16), shaped((joined_count, width), BF16), shaped((joined_count, width), BF16),
+            shaped((pixels, width), BF16), shaped((late, width), BF16), shaped((late, width), BF16),
         ],
         scratch_shapes=[
             pltpu.VMEM((pixels, width), BF16), pltpu.VMEM((pixels, joined_count), BF16), pltpu.VMEM((8, width), F32),
@@ -832,7 +971,7 @@
         cost_estimate=cost(8),
         name="in_back",
     )(
-        gjoined, x_own, gmiddle, valid, vecs, in_weight, mixer_grads, grad_kernel, ffn_sums, bias_sum,
+        gjoined, x_own, gmiddle, valid, vecs, in_weight, grad_kernel, ffn_sums, bias_sum,
     )
     rest = reducer.open(rest_sent, rest_kept)
     rest.swap()
@@ -873,54 +1012,56 @@
     (outputs, rest.sent, ffn.sent) = tie((outputs, rest.sent, ffn.sent))
     outputs = down(active, outputs, count // 2, count - count // 2)
     (outputs,) = onward(rest, outputs)
-    expand_ffn = pl.pallas_call(
-        expand_ffn_kernel,
-        grid=(hidden // width,),
+    vector = shaped((1, width), F32)
+    block_at = lambda i: (jnp.minimum(i, 3), 0)
+    expand_early = pl.pallas_call(
+        expand_early_kernel,
+        grid=(5,),
         in_specs=[
-            chunked((width, width)), chunked((width, width)), chunked((width, width)), whole((8, width)),
+            chunked((width, width)), chunked((width, width)), pl.BlockSpec((width, width), block_at),
+            whole((width, width)), whole((8, width)),
         ],
         out_specs=[
-            chunked((width, width)), pl.BlockSpec((width, width), lambda i: (0, i)), held((1, width)),
-        ],
-        out_shape=[shaped((hidden, width), F32), shaped((width, hidden), F32), shaped((1, width), F32)],
+            pl.BlockSpec((width, width), block_at), pl.BlockSpec((width, width), lambda i: (0, jnp.minimum(i, 3))),
+            held((1, width)), held((width, width)), held(w4.shape), held(w3.shape), held(mix_second.shape),
+            held(mix_first.shape), held((1, width)),
+        ],
+        out_shape=[
+            shaped((hidden, width), F32), shaped((width, hidden), F32), vector, shaped((width, width), F32),
+            shaped(w4.shape, F32), shaped(w3.shape, F32), shaped(mix_second.shape, F32),
+            shaped(mix_first.shape, F32), vector,
+        ],
         compiler_params=params(32),
         cost_estimate=cost(5),
-        name="expand_ffn",
+        name="expand_early",
     )
     expanded = None
-    for who in "frfrfrrfrfr":
+    for who in "frfrrfrrfrfr":
         way, other = (ffn, rest) if who == "f" else (rest, ffn)
         if not way.done:
             (other.kept,) = onward(way, other.kept)
         if ffn.done and expanded is None:
-            expanded = expand_ffn(ffn.kept, ffn.got, down_weight, vecs)
+            expanded = expand_early(ffn.kept, ffn.got, down_weight, out_weight, vecs)
             (rest.kept, expanded) = tie((rest.kept, expanded))
     while not (ffn.done and rest.done):
         for way in (ffn, rest):
             if not way.done:
                 onward(way)
     if expanded is None:
-        expanded = expand_ffn(ffn.kept, ffn.got, down_weight, vecs)
-    grad_down_weight, grad_up_weight, scale_2 = expanded
-    rest_own, rest_got = rest.kept, rest.got
-    vector = shaped((1, width), F32)
-    whole_block = pl.BlockSpec(memory_space=pltpu.VMEM)
-    (
-        grad_in_weight, grad_conv, grad_1, grad_2, grad_3, grad_4, grad_out,
-        gain_1, shift_1, scale_1, gain_2, shift_2, grad_bias,
-    ) = pl.pallas_call(
-        expand_rest_kernel,
-        in_specs=[whole_block] * 4,
-        out_specs=[whole_block] * 13,
+        expanded = expand_early(ffn.kept, ffn.got, down_weight, out_weight, vecs)
+    (grad_down_weight, grad_up_weight, scale_2, grad_out, grad_4, grad_3, grad_2, grad_1, scale_1) = expanded
+    grad_in_weight, grad_conv, gain_1, shift_1, gain_2, shift_2, grad_bias = pl.pallas_call(
+        expand_late_kernel,
+        in_specs=[pl.BlockSpec(memory_space=pltpu.VMEM)] * 2,
+        out_specs=[pl.BlockSpec(memory_space=pltpu.VMEM)] * 7,
         out_shape=[
-            shaped(in_weight.shape, F32), shaped(conv_kernel.shape, F32), shaped(mix_first.shape, F32),
-            shaped(mix_second.shape, F32), shaped(w3.shape, F32), shaped(w4.shape, F32), shaped((width, width), F32),
-            vector, vector, vector, vector, vector, shaped((1, hidden), F32),
+            shaped(in_weight.shape, F32), shaped(conv_kernel.shape, F32), vector, vector, vector, vector,
+            shaped((1, hidden), F32),
         ],
         compiler_params=pltpu.CompilerParams(vmem_limit_bytes=32 * 1024 * 1024),
-        cost_estimate=cost(5),
-        name="expand_rest",
-    )(rest_own, rest_got, out_weight, vecs)
+        cost_estimate=cost(3),
+        name="expand_late",
+    )(rest.kept, rest.got)
     return (
         outputs.reshape(activations.shape),
         ginput.reshape(activations.shape),

time: 233 us -> 220 us (0.944)
  other arithmetic: 19.2 us -> 8.51 us
  starting transfers between devices: 40.4 us -> 46.1 us
  waiting for transfers between devices: 52.9 us -> 48.9 us
  Pallas kernels: 104 us -> 101 us
    concatenate x4, other arithmetic: 7.61 us -> 0.68 us  [side(): jnp.concatenate([above[:, cols], block[:, cols], below[:, cols]], axis=0)]
    ppermute x18, waiting for transfers between devices: 50.2 us -> 46.2 us  [swap(): return lax.ppermute(block, AXES, self.pairs(step))]
    ppermute x18, starting transfers between devices: 22.3 us -> 25.3 us  [swap(): return lax.ppermute(block, AXES, self.pairs(step))]
    ppermute x4, starting transfers between devices: 6.04 us -> 8.8 us  [the longest x2 6.22 us: cols_around(): lax.ppermute(side(last), 'col', right_pairs)]
    pallas_call x7, Pallas kernels: 86.4 us -> 83.8 us  [the longest x1 31.9 us: on_device(): pl.pallas_call(forward_kernel, grid=(steps,), in_specs=[in_smem, chunked(...]
  transfers between devices with their start and end apart: 26 -> 26, of which waited for: 16 -> 12; matrix products, arithmetic and copies ran while one was open for 7% -> 5% of each run, Pallas kernels for 21% -> 19%
where the time goes in v2:
time: 220 us
  Pallas kernels  101 us (46%)
  waiting for transfers between devices  48.9 us (22%)
  starting transfers between devices  46.1 us (21%)
  other arithmetic  8.51 us (4%)
  between operations  6.85 us (3%)
  local copies, waits for them, and re-layouts  5.41 us (2%)
  matrix products  2.84 us (1%)
    ppermute x18, waiting for transfers between devices, swap(): return lax.ppermute(block, AXES, self.pairs(step))  46.2 us
    pallas_call x1, Pallas kernels, on_device(): pl.pallas_call(forward_kernel, grid=(steps,), in_specs=[in_smem, chunked(...  31.9 us
    ppermute x18, starting transfers between devices, swap(): return lax.ppermute(block, AXES, self.pairs(step))  25.3 us
    pallas_call x1, Pallas kernels, on_device(): pl.pallas_call(ffn_back_kernel, grid=(few,), in_specs=[chunked((wide, wid...  16.9 us
    pallas_call x1, Pallas kernels, on_device(): pl.pallas_call(gates_back_kernel, grid=(steps,), in_specs=[in_smem, whole...  11.4 us
    ppermute x2, starting transfers between devices, rows_around(): lax.ppermute(block[-HALO:], 'row', down_pairs)  9.41 us
    pallas_call x1, Pallas kernels, on_device(): pl.pallas_call(kernel_back_kernel, grid=(steps,), in_specs=[chunked((2 *...  9.17 us
    pallas_call x1, Pallas kernels, on_device(): pl.pallas_call(mixer_back_kernel, grid=(few,), in_specs=[chunked((wide, w...  9.04 us
  transfers between devices with their start and end apart: 26, of which 12 were waited for; matrix products, arithmetic and copies ran while one was open for 5% of the time, Pallas kernels for 19%

profile of v2, /device:TPU:0, one launch (start us, length us, event | category | flops | bytes accessed | tf_op | source)
XLA Modules:
  0.0 219.6 jit_solution(3099307933457993191)
XLA Ops:
  0.7 0.7 broadcast_compare_fusion
  1.4 1.6 broadcast_select_fusion.2
  3.1 4.8 %collective-permute-start = (bf16[3,40,512]{2,1,0:T(8,128)(2,1)S(1)}, bf16[3,40,512]{2,1,0:T(8,128)(2,1)S(1)}, u32[]{:S(2)}, u32[]{:S(2)}) collective-permute-start(bf16[3,40,512]{2,1,0:T(8,128)(2,1)S(1)} %get-tuple-element.297), channel_id=1, source_target_pairs={{0,8},{8,16},{16,24},{1,9},{9,17},{17,25},{2,10},{10,18},{18,26},{... | collective-permute-start | bytes 368648 | tf_op jit(solution)/shard_map/ppermute | solution.py:760
  8.0 1.3 collective-permute-start.1
  9.3 0.6 fusion.11
  12.6 0.7 scatter.6.w1
  13.9 2.8 %fusion.spec_hbm.spec = f32[672,1024]{1,0:T(8,128)} fusion(f32[672,49]{1,0:T(8,128)S(1)} %copy-done.25, bf16[49,992]{1,0:T(8,128)(2,1)S(1)} %reshape.167), kind=kOutput, calls=%fused_computation.41 | convolution fusion | flops 404619264 | bytes 2981440 | tf_op jit(solution)/shard_map/dot_general | solution.py:779
  17.2 1.3 collective-permute-start.3
  18.6 3.0 %collective-permute-start.2 = (bf16[38,3,512]{2,1,0:T(4,128)(2,1)S(1)}, bf16[38,3,512]{2,1,0:T(4,128)(2,1)S(1)}, u32[]{:S(2)}, u32[]{:S(2)}) collective-permute-start(bf16[38,3,512]{2,1,0:T(4,128)(2,1)S(1)} %pad_maximum_fusion.7), channel_id=1, source_target_pairs={{0,1},{1,2},{2,3},{3,4},{4,5},{5,6},{6,7},{8,9},{9,10},{10,11},{11... | collective-permute-start | bytes 350216 | tf_op jit(solution)/shard_map/ppermute | solution.py:767
  26.4 1.1 copy.46.valid
  27.6 31.9 %forward.1 = (bf16[4480,1024]{1,0:T(8,128)(2,1)}, f32[1280,1024]{1,0:T(8,128)}, f32[1280,1024]{1,0:T(8,128)}, f32[1280,128]{1,0:T(8,128)}, f32[1280,512]{1,0:T(8...) custom-call(s32[4]{0:T(128)} %add_convert_fusion.16.near, ...), custom_call_target="tpu_custom_call" | custom-call | flops 299999985664 | bytes 900000000 | tf_op jit(solution)/shard_map/forward/pallas_call | solution.py:805
  59.6 16.9 %ffn_back.1 = (f32[1280,512]{1,0:T(8,128)}, bf16[2560,512]{1,0:T(8,128)(2,1)}, bf16[2560,512]{1,0:T(8,128)(2,1)}, f32[8,512]{1,0:T(8,128)S(1)}, f32[8,2048]{1,0:T(8,128)S(1)}) custom-call(bf16[1280,512]{1,0:T(8,128)(2,1)S(1)} %bitcast.35, bf16[1280,2048]{1,0:T(8,128)(2,1)} %get-tuple-element.172.slope, f32[1280,512]{1,0:T(8,128)} %get-tuple-element.173.middle, ...), custom_call_target="tpu_custom_call" | custom-call | flops 160000000000 | bytes 480000000 | tf_op jit(solution)/shard_map/ffn_back/pallas_call | solution.py:853
  76.6 9.0 %mixer_back.1 = (bf16[1280,1024]{1,0:T(8,128)(2,1)S(1)}, f32[1280,128]{1,0:T(8,128)S(1)}, bf16[2560,512]{1,0:T(8,128)(2,1)}, bf16[2560,512]{1,0:T(8,128)(2,1)}) custom-call(f32[1280,512]{1,0:T(8,128)} %get-tuple-element.175.gmiddle, f32[1280,1024]{1,0:T(8,128)} %get-tuple-element.176.spread, ...), custom_call_target="tpu_custom_call", output_to_operand_aliasing={{2}: (10, {}), {3}: (11, {})} | custom-call | flops 89999998976 | bytes 270000000 | tf_op jit(solution)/shard_map/mixer_back/pallas_call | solution.py:875
  85.6 1.3 collective-permute-start.6
  86.9 4.6 %collective-permute-start.4 = (bf16[3,40,1024]{2,1,0:T(8,128)(2,1)S(1)}, bf16[3,40,1024]{2,1,0:T(8,128)(2,1)S(1)}, u32[]{:S(2)}, u32[]{:S(2)}) collective-permute-start(bf16[3,40,1024]{2,1,0:T(8,128)(2,1)S(1)} %bitcast.38), channel_id=1, source_target_pairs={{0,8},{8,16},{16,24},{1,9},{9,17},{17,25},{2,10},{10,18},{18,26},{... | collective-permute-start | bytes 737288 | tf_op jit(solution)/shard_map/ppermute | solution.py:760
  91.5 1.3 collective-permute-start.5
  92.8 9.2 %kernel_back.1.grad_kernel = bf16[112,512]{1,0:T(8,128)(2,1)S(1)} custom-call(bf16[4480,1024]{1,0:T(8,128)(2,1)} %get-tuple-element.182.xwaves, bf16[1280,1024]{1,0:T(8,128)(2,1)S(1)} %get-tuple-element.181.gspread.own, bf16[224,64]{1,0:T(8,128)(2,1)S(1)} %copy-done.18, f32[56,448]{1,0:T(8,128)S(1)} %copy-done.17), custom_call_target="tpu_custom_call" | custom-call | flops 89999998976 | bytes 270000000 | tf_op jit(solution)/shard_map/kernel_back/pallas_call | solution.py:905
  102.2 2.7 %collective-permute-done.5 = bf16[3,40,1024]{2,1,0:T(8,128)(2,1)S(1)} collective-permute-done((bf16[3,40,1024]{2,1,0:T(8,128)(2,1)S(1)}, bf16[3,40,1024]{2,1,0:T(8,128)(2,1)S(1)}, u32[]{:S(2)}, u32[]{:S(2)}) %collective-permute-start.5) | collective-permute-done | bytes 245792 | tf_op jit(solution)/shard_map/ppermute | solution.py:760
  105.3 1.3 collective-permute-start.8
  106.9 3.2 %collective-permute-start.7 = (bf16[38,3,1024]{2,1,0:T(4,128)(2,1)S(1)}, bf16[38,3,1024]{2,1,0:T(4,128)(2,1)S(1)}, u32[]{:S(2)}, u32[]{:S(2)}) collective-permute-start(bf16[38,3,1024]{2,1,0:T(4,128)(2,1)S(1)} %pad_maximum_fusion.4), channel_id=1, source_target_pairs={{0,1},{1,2},{2,3},{3,4},{4,5},{5,6},{6,7},{8,9},{9,10},{10,11},{11... | collective-permute-start | bytes 700424 | tf_op jit(solution)/shard_map/ppermute | solution.py:767
  110.1 1.8 add_convert_fusion
  112.5 11.4 %gates_back.1.gjoined = bf16[1280,1024]{1,0:T(8,128)(2,1)S(1)} custom-call(s32[4]{0:T(128)S(1)} %copy-done.7, bf16[120,1024]{1,0:T(8,128)(2,1)S(1)} %bitcast.32, bf16[1280,1024]{1,0:T(8,128)(2,1)} %copy-done.2, bf16[120,1024]{1,0:T(8,128)(2,1)S(1)} %bitcast.33, bf16[38,3,1024]{2,1,0:T(4,128)(2,1)S(1)} %collective-permute-done.7.left, ...), custom_call_target="tpu_custom_call" | custom-call | flops 109999996928 | bytes 330000000 | tf_op jit(solution)/shard_map/gates_back/pallas_call | solution.py:929
  123.9 1.5 copy-done.21
  125.4 4.3 %collective-permute-done.9 = bf16[1280,512]{1,0:T(8,128)(2,1)S(1)} collective-permute-done((bf16[1280,512]{1,0:T(8,128)(2,1)}, bf16[1280,512]{1,0:T(8,128)(2,1)S(1)}, u32[]{:S(2)}, u32[]{:S(2)}) %collective-permute-start.9) | collective-permute-done | bytes 1310752 | tf_op jit(solution)/shard_map/ppermute | solution.py:675
  130.1 1.9 collective-permute-start.10
  132.1 7.5 %in_back.1 = (bf16[1280,512]{1,0:T(8,128)(2,1)}, bf16[576,512]{1,0:T(8,128)(2,1)S(1)}, bf16[576,512]{1,0:T(8,128)(2,1)S(1)}) custom-call(bf16[1280,1024]{1,0:T(8,128)(2,1)} %copy-done.21, bf16[1280,512]{1,0:T(8,128)(2,1)S(1)} %bitcast.30, f32[1280,512]{1,0:T(8,128)} %get-tuple-element.175.gmiddle, f32[1280,1]{1,0:T(8,128)S(1)} %copy-done.1, ...), custom_call_target="tpu_custom_call" | custom-call | flops 80000000000 | bytes 240000000 | tf_op jit(solution)/shard_map/in_back/pallas_call | solution.py:955
  139.6 1.9 collective-permute-start.12
  141.6 4.9 %collective-permute-start.11 = (bf16[320,512]{1,0:T(8,128)(2,1)S(1)}, bf16[320,512]{1,0:T(8,128)(2,1)S(1)}, u32[]{:S(2)}, u32[]{:S(2)}) collective-permute-start(bf16[320,512]{1,0:T(8,128)(2,1)S(1)} %get-tuple-element.292), channel_id=1, source_target_pairs={{0,2},{1,9},{2,0},{3,11},{4,6},{5,13},{6,4},{7,15},{8,10},{9,1},{1... | collective-permute-start | bytes 983048 | tf_op jit(solution)/shard_map/ppermute | solution.py:675
  146.5 3.4 %down.2.before = bf16[1280,512]{1,0:T(8,128)(2,1)} custom-call(bf16[1280,2048]{1,0:T(8,128)(2,1)} %get-tuple-element.207.active, f32[1280,512]{1,0:T(8,128)S(1)} %copy-done.20, f32[8,512]{1,0:T(8,128)S(1)} %copy-done.5, bf16[2048,512]{1,0:T(8,128)(2,1)S(1)} %copy-done.8, bf16[8,128]{1,0:T(8,128)(2,1)S(1)} %broadcast_in_dim.30.before), custom_call_target="tpu_custom_call" | custom-call | flops 40000000000 | bytes 120000000 | tf_op jit(solution)/shard_map/down/pallas_call | solution.py:983
  150.1 0.7 collective-permute-start.13
  150.7 0.9 collective-permute-done.11
  151.7 3.1 %collective-permute-start.14 = (bf16[320,512]{1,0:T(8,128)(2,1)S(1)}, bf16[320,512]{1,0:T(8,128)(2,1)S(1)}, u32[]{:S(2)}, u32[]{:S(2)}) collective-permute-start(bf16[320,512]{1,0:T(8,128)(2,1)S(1)} %add_convert_fusion.5), channel_id=1, source_target_pairs={{0,4},{1,5},{2,6},{3,7},{4,0},{5,1},{6,2},{7,3},{8,12},{9,13},{10,... | collective-permute-start | bytes 983048 | tf_op jit(solution)/shard_map/ppermute | solution.py:675
  154.8 4.7 %down.3 = bf16[1280,512]{1,0:T(8,128)(2,1)} custom-call(bf16[1280,2048]{1,0:T(8,128)(2,1)} %get-tuple-element.207.active, f32[1280,512]{1,0:T(8,128)S(1)} %copy-done.20, f32[8,512]{1,0:T(8,128)S(1)} %copy-done.5, bf16[2048,512]{1,0:T(8,128)(2,1)S(1)} %copy-done.8, bf16[1280,512]{1,0:T(8,128)(2,1)} %down.2.before), custom_call_target="tpu_custom_call", output_to_operand_aliasing={{}: (4, {})} | custom-call | flops 40000000000 | bytes 120000000 | tf_op jit(solution)/shard_map/down/pallas_call | solution.py:983
  159.5 8.6 %collective-permute-done.14 = bf16[320,512]{1,0:T(8,128)(2,1)S(1)} collective-permute-done((bf16[320,512]{1,0:T(8,128)(2,1)S(1)}, bf16[320,512]{1,0:T(8,128)(2,1)S(1)}, u32[]{:S(2)}, u32[]{:S(2)}) %collective-permute-start.14) | collective-permute-done | bytes 327712 | tf_op jit(solution)/shard_map/ppermute | solution.py:675
  168.7 5.1 %collective-permute-done.15 = bf16[144,512]{1,0:T(8,128)(2,1)S(1)} collective-permute-done((bf16[144,512]{1,0:T(8,128)(2,1)S(1)}, bf16[144,512]{1,0:T(8,128)(2,1)S(1)}, u32[]{:S(2)}, u32[]{:S(2)}) %collective-permute-start.15) | collective-permute-done | bytes 147488 | tf_op jit(solution)/shard_map/ppermute | solution.py:675
  173.8 1.6 collective-permute-done.16
  175.7 1.0 collective-permute-start.17
  176.6 4.3 %collective-permute-done.17 = bf16[72,512]{1,0:T(8,128)(2,1)S(1)} collective-permute-done((bf16[72,512]{1,0:T(8,128)(2,1)S(1)}, bf16[72,512]{1,0:T(8,128)(2,1)S(1)}, u32[]{:S(2)}, u32[]{:S(2)}) %collective-permute-start.17) | collective-permute-done | bytes 73760 | tf_op jit(solution)/shard_map/ppermute | solution.py:675
  180.9 2.7 %collective-permute-start.18 = (bf16[72,512]{1,0:T(8,128)(2,1)S(1)}, bf16[72,512]{1,0:T(8,128)(2,1)S(1)}, u32[]{:S(2)}, u32[]{:S(2)}) collective-permute-start(bf16[72,512]{1,0:T(8,128)(2,1)S(1)} %add_convert_fusion.13), channel_id=1, source_target_pairs={{0,4},{1,5},{2,6},{3,7},{4,0},{5,1},{6,2},{7,3},{8,12},{9,13},{10,... | collective-permute-start | bytes 221192 | tf_op jit(solution)/shard_map/ppermute | solution.py:675
  183.5 3.5 %collective-permute-done.18 = bf16[72,512]{1,0:T(8,128)(2,1)S(1)} collective-permute-done((bf16[72,512]{1,0:T(8,128)(2,1)S(1)}, bf16[72,512]{1,0:T(8,128)(2,1)S(1)}, u32[]{:S(2)}, u32[]{:S(2)}) %collective-permute-start.18) | collective-permute-done | bytes 73760 | tf_op jit(solution)/shard_map/ppermute | solution.py:675
  187.7 2.2 %collective-permute-start.20 = (bf16[72,512]{1,0:T(8,128)(2,1)S(1)}, bf16[72,512]{1,0:T(8,128)(2,1)S(1)}, u32[]{:S(2)}, u32[]{:S(2)}) collective-permute-start(bf16[72,512]{1,0:T(8,128)(2,1)S(1)} %add_convert_fusion.12), channel_id=1, source_target_pairs={{0,2},{1,9},{2,0},{3,11},{4,6},{5,13},{6,4},{7,15},{8,10},{9,1},{1... | collective-permute-start | bytes 221192 | tf_op jit(solution)/shard_map/ppermute | solution.py:675
  189.9 2.8 %collective-permute-done.20 = bf16[72,512]{1,0:T(8,128)(2,1)S(1)} collective-permute-done((bf16[72,512]{1,0:T(8,128)(2,1)S(1)}, bf16[72,512]{1,0:T(8,128)(2,1)S(1)}, u32[]{:S(2)}, u32[]{:S(2)}) %collective-permute-start.20) | collective-permute-done | bytes 73760 | tf_op jit(solution)/shard_map/ppermute | solution.py:675
  192.8 3.2 %collective-permute-start.21 = (bf16[144,512]{1,0:T(8,128)(2,1)S(1)}, bf16[144,512]{1,0:T(8,128)(2,1)S(1)}, u32[]{:S(2)}, u32[]{:S(2)}) collective-permute-start(bf16[144,512]{1,0:T(8,128)(2,1)S(1)} %pad_maximum_fusion.9), channel_id=1, source_target_pairs={{0,16},{1,3},{2,18},{3,1},{4,20},{5,7},{6,22},{7,5},{8,24},{9,11},... | collective-permute-start | bytes 442376 | tf_op jit(solution)/shard_map/ppermute | solution.py:675
  196.0 4.8 %collective-permute-done.21 = bf16[144,512]{1,0:T(8,128)(2,1)S(1)} collective-permute-done((bf16[144,512]{1,0:T(8,128)(2,1)S(1)}, bf16[144,512]{1,0:T(8,128)(2,1)S(1)}, u32[]{:S(2)}, u32[]{:S(2)}) %collective-permute-start.21) | collective-permute-done | bytes 147488 | tf_op jit(solution)/shard_map/ppermute | solution.py:675
  200.8 4.1 %collective-permute-done.22 = bf16[1280,512]{1,0:T(8,128)(2,1)S(1)} collective-permute-done((bf16[1280,512]{1,0:T(8,128)(2,1)S(1)}, bf16[1280,512]{1,0:T(8,128)(2,1)S(1)}, u32[]{:S(2)}, u32[]{:S(2)}) %collective-permute-start.22) | collective-permute-done | bytes 1310752 | tf_op jit(solution)/shard_map/ppermute | solution.py:675
  205.8 6.3 %collective-permute-done.23 = bf16[288,512]{1,0:T(8,128)(2,1)S(1)} collective-permute-done((bf16[288,512]{1,0:T(8,128)(2,1)S(1)}, bf16[288,512]{1,0:T(8,128)(2,1)S(1)}, u32[]{:S(2)}, u32[]{:S(2)}) %collective-permute-start.23) | collective-permute-done | bytes 294944 | tf_op jit(solution)/shard_map/ppermute | solution.py:675
  212.6 5.4 %expand_early.1 = (f32[2048,512]{1,0:T(8,128)}, f32[512,2048]{1,0:T(8,128)}, f32[1,512]{1,0:T(1,128)}, f32[512,512]{1,0:T(8,128)}, f32[256,512]{1,0:T(8,128)}, /...) custom-call(bf16[2560,512]{1,0:T(8,128)(2,1)S(1)} %pad_maximum_fusion.own, ...), custom_call_target="tpu_custom_call" | custom-call | flops 49999998976 | bytes 150000000 | tf_op jit(solution)/shard_map/expand_early/pallas_call | solution.py:1044
  218.0 1.6 expand_late.1
  (156 shorter events, 8.4 us)
Async XLA Ops:
  1.4 11.1 %copy-start.28 = (bf16[7,7,992]{2,1,0:T(8,128)(2,1)S(1)}, bf16[7,7,992]{2,1,0:T(8,128)(2,1)}, u32[]{:S(2)}) copy-start(bf16[7,7,992]{2,1,0:T(8,128)(2,1)} %param.33) | copy-start | bytes 291652
  1.4 11.2 %copy-start.31 = (bf16[32,64]{1,0:T(8,128)(2,1)S(1)}, bf16[32,64]{1,0:T(8,128)(2,1)}, u32[]{:S(2)}) copy-start(bf16[32,64]{1,0:T(8,128)(2,1)} %param.34) | copy-start | bytes 12292
  1.4 11.9 %copy-start.30 = (bf16[64,128]{1,0:T(8,128)(2,1)S(1)}, bf16[64,128]{1,0:T(8,128)(2,1)}, u32[]{:S(2)}) copy-start(bf16[64,128]{1,0:T(8,128)(2,1)} %param.35) | copy-start | bytes 49156
  1.4 12.5 %copy-start.25 = (f32[672,49]{1,0:T(8,128)S(1)}, f32[672,49]{1,0:T(8,128)}, u32[]{:S(2)}) copy-start(f32[672,49]{1,0:T(8,128)} %constant.128.clone) | copy-start | bytes 395140
  3.1 13.7 %copy-start.24 = (bf16[32,40,512]{2,1,0:T(8,128)(2,1)}, bf16[32,40,512]{2,1,0:T(8,128)(2,1)S(1)}, u32[]{:S(2)}) copy-start(bf16[32,40,512]{2,1,0:T(8,128)(2,1)S(1)} %broadcast_select_fusion.2) | copy-start | bytes 3932164
  3.1 13.8 %collective-permute-start = (bf16[3,40,512]{2,1,0:T(8,128)(2,1)S(1)}, bf16[3,40,512]{2,1,0:T(8,128)(2,1)S(1)}, u32[]{:S(2)}, u32[]{:S(2)}) collective-permute-start(bf16[3,40,512]{2,1,0:T(8,128)(2,1)S(1)} %get-tuple-element.297), channel_id=1, source_target_pairs={{0,8},{8,16},{16,24},{1,9},{9,17},{17,25},{2,10},{10,18},{18,26},{... | collective-permute-start | bytes 368648 | tf_op jit(solution)/shard_map/ppermute | solution.py:760
  8.0 9.0 %collective-permute-start.1 = (bf16[3,40,512]{2,1,0:T(8,128)(2,1)S(1)}, bf16[3,40,512]{2,1,0:T(8,128)(2,1)S(1)}, u32[]{:S(2)}, u32[]{:S(2)}) collective-permute-start(bf16[3,40,512]{2,1,0:T(8,128)(2,1)S(1)} %get-tuple-element.296), channel_id=1, source_target_pairs={{8,0},{16,8},{24,16},{9,1},{17,9},{25,17},{10,2},{18,10},{26,18},{... | collective-permute-start | bytes 368648 | tf_op jit(solution)/shard_map/ppermute | solution.py:760
  16.8 9.5 %copy-start.29 = (s32[32,40]{1,0:T(8,128)S(1)}, s32[32,40]{1,0:T(8,128)}, u32[]{:S(2)}) copy-start(s32[32,40]{1,0:T(8,128)} %param.46) | copy-start | bytes 15364
  16.9 10.6 %copy-start.26 = (bf16[3,40,512]{2,1,0:T(8,128)(2,1)}, bf16[3,40,512]{2,1,0:T(8,128)(2,1)S(1)}, u32[]{:S(2)}) copy-start(bf16[3,40,512]{2,1,0:T(8,128)(2,1)S(1)} %collective-permute-done) | copy-start | bytes 368644
  16.9 10.6 %copy-start.27 = (bf16[3,40,512]{2,1,0:T(8,128)(2,1)}, bf16[3,40,512]{2,1,0:T(8,128)(2,1)S(1)}, u32[]{:S(2)}) copy-start(bf16[3,40,512]{2,1,0:T(8,128)(2,1)S(1)} %collective-permute-done.1) | copy-start | bytes 368644
  17.2 9.2 %collective-permute-start.3 = (bf16[38,3,512]{2,1,0:T(4,128)(2,1)S(1)}, bf16[38,3,512]{2,1,0:T(4,128)(2,1)S(1)}, u32[]{:S(2)}, u32[]{:S(2)}) collective-permute-start(bf16[38,3,512]{2,1,0:T(4,128)(2,1)S(1)} %pad_maximum_fusion.8), channel_id=1, source_target_pairs={{1,0},{2,1},{3,2},{4,3},{5,4},{6,5},{7,6},{9,8},{10,9},{11,10},{12... | collective-permute-start | bytes 350216 | tf_op jit(solution)/shard_map/ppermute | solution.py:767
  18.6 7.8 %collective-permute-start.2 = (bf16[38,3,512]{2,1,0:T(4,128)(2,1)S(1)}, bf16[38,3,512]{2,1,0:T(4,128)(2,1)S(1)}, u32[]{:S(2)}, u32[]{:S(2)}) collective-permute-start(bf16[38,3,512]{2,1,0:T(4,128)(2,1)S(1)} %pad_maximum_fusion.7), channel_id=1, source_target_pairs={{0,1},{1,2},{2,3},{3,4},{4,5},{5,6},{6,7},{8,9},{9,10},{10,11},{11... | collective-permute-start | bytes 350216 | tf_op jit(solution)/shard_map/ppermute | solution.py:767
  27.5 31.9 %copy-start.1 = (f32[1280,1]{1,0:T(8,128)S(1)}, f32[1280,1]{1,0:T(8,128)}, u32[]{:S(2)}) copy-start(f32[1280,1]{1,0:T(8,128)} %copy.46.valid) | copy-start | bytes 15364
  27.5 31.9 %copy-start.5 = (f32[8,512]{1,0:T(8,128)S(1)}, f32[8,512]{1,0:T(8,128)}, u32[]{:S(2)}) copy-start(f32[8,512]{1,0:T(8,128)} %convert_element_type.177.vecs) | copy-start | bytes 49156
  27.5 31.9 %copy-start.8 = (bf16[2048,512]{1,0:T(8,128)(2,1)S(1)}, bf16[2048,512]{1,0:T(8,128)(2,1)}, u32[]{:S(2)}) copy-start(bf16[2048,512]{1,0:T(8,128)(2,1)} %down_w.7) | copy-start | bytes 6291460
  27.5 31.9 %copy-start.10 = (bf16[32,40,512]{2,1,0:T(8,128)(2,1)S(1)}, bf16[32,40,512]{2,1,0:T(8,128)(2,1)}, u32[]{:S(2)}) copy-start(bf16[32,40,512]{2,1,0:T(8,128)(2,1)} %param.48) | copy-start | bytes 3932164
  59.5 17.0 %copy-start.3 = (bf16[128,128]{1,0:T(8,128)(2,1)S(1)}, bf16[128,128]{1,0:T(8,128)(2,1)}, u32[]{:S(2)}) copy-start(bf16[128,128]{1,0:T(8,128)(2,1)} %scatter.9.w2) | copy-start | bytes 98308
  59.5 17.0 %copy-start.4 = (bf16[128,128]{1,0:T(8,128)(2,1)S(1)}, bf16[128,128]{1,0:T(8,128)(2,1)}, u32[]{:S(2)}) copy-start(bf16[128,128]{1,0:T(8,128)(2,1)} %scatter.6.w1) | copy-start | bytes 98308
  59.5 17.0 %copy-start.12 = (bf16[512,512]{1,0:T(8,128)(2,1)S(1)}, bf16[512,512]{1,0:T(8,128)(2,1)}, u32[]{:S(2)}) copy-start(bf16[512,512]{1,0:T(8,128)(2,1)} %out_w.3) | copy-start | bytes 1572868
  59.5 17.0 %copy-start.14 = (bf16[256,512]{1,0:T(8,128)(2,1)S(1)}, bf16[256,512]{1,0:T(8,128)(2,1)}, u32[]{:S(2)}) copy-start(bf16[256,512]{1,0:T(8,128)(2,1)} %w4.1) | copy-start | bytes 786436
  59.5 17.0 %copy-start.15 = (bf16[128,256]{1,0:T(8,128)(2,1)S(1)}, bf16[128,256]{1,0:T(8,128)(2,1)}, u32[]{:S(2)}) copy-start(bf16[128,256]{1,0:T(8,128)(2,1)} %w3.3) | copy-start | bytes 196612
  59.5 17.0 %copy-start.22 = (f32[1280,128]{1,0:T(8,128)S(1)}, f32[1280,128]{1,0:T(8,128)}, u32[]{:S(2)}) copy-start(f32[1280,128]{1,0:T(8,128)} %get-tuple-element.178.lead) | copy-start | bytes 1966084
  76.6 16.2 %copy-start.17 = (f32[56,448]{1,0:T(8,128)S(1)}, f32[56,448]{1,0:T(8,128)}, u32[]{:S(2)}) copy-start(f32[56,448]{1,0:T(8,128)} %constant.132.clone.td) | copy-start | bytes 301060
  76.6 16.2 %copy-start.18 = (bf16[224,64]{1,0:T(8,128)(2,1)S(1)}, bf16[224,64]{1,0:T(8,128)(2,1)}, u32[]{:S(2)}) copy-start(bf16[224,64]{1,0:T(8,128)(2,1)} %constant.131.clone.tg) | copy-start | bytes 86020
  85.6 16.4 %copy-start.2 = (bf16[1280,1024]{1,0:T(8,128)(2,1)}, bf16[1280,1024]{1,0:T(8,128)(2,1)S(1)}, u32[]{:S(2)}) copy-start(bf16[1280,1024]{1,0:T(8,128)(2,1)S(1)} %get-tuple-element.181.gspread.own) | copy-start | bytes 7864324
  85.6 19.3 %collective-permute-start.6 = (bf16[2560,512]{1,0:T(8,128)(2,1)}, bf16[2560,512]{1,0:T(8,128)(2,1)S(1)}, u32[]{:S(2)}, u32[]{:S(2)}) collective-permute-start(bf16[2560,512]{1,0:T(8,128)(2,1)} %get-tuple-element.184), channel_id=1, source_target_pairs={{0,1},{1,0},{2,3},{3,2},{4,5},{5,4},{6,7},{7,6},{8,9},{9,8},{10,11... | collective-permute-start | bytes 7864328 | tf_op jit(solution)/shard_map/ppermute | solution.py:675
  86.9 15.3 %collective-permute-start.4 = (bf16[3,40,1024]{2,1,0:T(8,128)(2,1)S(1)}, bf16[3,40,1024]{2,1,0:T(8,128)(2,1)S(1)}, u32[]{:S(2)}, u32[]{:S(2)}) collective-permute-start(bf16[3,40,1024]{2,1,0:T(8,128)(2,1)S(1)} %bitcast.38), channel_id=1, source_target_pairs={{0,8},{8,16},{16,24},{1,9},{9,17},{17,25},{2,10},{10,18},{18,26},{... | collective-permute-start | bytes 737288 | tf_op jit(solution)/shard_map/ppermute | solution.py:760
  91.5 13.5 %collective-permute-start.5 = (bf16[3,40,1024]{2,1,0:T(8,128)(2,1)S(1)}, bf16[3,40,1024]{2,1,0:T(8,128)(2,1)S(1)}, u32[]{:S(2)}, u32[]{:S(2)}) collective-permute-start(bf16[3,40,1024]{2,1,0:T(8,128)(2,1)S(1)} %bitcast.37), channel_id=1, source_target_pairs={{8,0},{16,8},{24,16},{9,1},{17,9},{25,17},{10,2},{18,10},{26,18},{... | collective-permute-start | bytes 737288 | tf_op jit(solution)/shard_map/ppermute | solution.py:760
  105.3 6.6 %collective-permute-start.8 = (bf16[38,3,1024]{2,1,0:T(4,128)(2,1)S(1)}, bf16[38,3,1024]{2,1,0:T(4,128)(2,1)S(1)}, u32[]{:S(2)}, u32[]{:S(2)}) collective-permute-start(bf16[38,3,1024]{2,1,0:T(4,128)(2,1)S(1)} %pad_maximum_fusion.5), channel_id=1, source_target_pairs={{1,0},{2,1},{3,2},{4,3},{5,4},{6,5},{7,6},{9,8},{10,9},{11,10},{12... | collective-permute-start | bytes 700424 | tf_op jit(solution)/shard_map/ppermute | solution.py:767
  106.9 5.0 %collective-permute-start.7 = (bf16[38,3,1024]{2,1,0:T(4,128)(2,1)S(1)}, bf16[38,3,1024]{2,1,0:T(4,128)(2,1)S(1)}, u32[]{:S(2)}, u32[]{:S(2)}) collective-permute-start(bf16[38,3,1024]{2,1,0:T(4,128)(2,1)S(1)} %pad_maximum_fusion.4), channel_id=1, source_target_pairs={{0,1},{1,2},{2,3},{3,4},{4,5},{5,6},{6,7},{8,9},{9,10},{10,11},{11... | collective-permute-start | bytes 700424 | tf_op jit(solution)/shard_map/ppermute | solution.py:767
  111.9 17.8 %collective-permute-start.9 = (bf16[1280,512]{1,0:T(8,128)(2,1)}, bf16[1280,512]{1,0:T(8,128)(2,1)S(1)}, u32[]{:S(2)}, u32[]{:S(2)}) collective-permute-start(bf16[1280,512]{1,0:T(8,128)(2,1)} %get-tuple-element.192), channel_id=1, source_target_pairs={{0,8},{1,17},{2,10},{3,19},{4,12},{5,21},{6,14},{7,23},{8,0},{9,25... | collective-permute-start | bytes 3932168 | tf_op jit(solution)/shard_map/ppermute | solution.py:675
  130.1 11.3 %collective-permute-start.10 = (bf16[640,512]{1,0:T(8,128)(2,1)S(1)}, bf16[640,512]{1,0:T(8,128)(2,1)S(1)}, u32[]{:S(2)}, u32[]{:S(2)}) collective-permute-start(bf16[640,512]{1,0:T(8,128)(2,1)S(1)} %get-tuple-element.202), channel_id=1, source_target_pairs={{0,16},{1,3},{2,18},{3,1},{4,20},{5,7},{6,22},{7,5},{8,24},{9,11},... | collective-permute-start | bytes 1966088 | tf_op jit(solution)/shard_map/ppermute | solution.py:675
  132.1 14.5 %copy-start.20 = (f32[1280,512]{1,0:T(8,128)S(1)}, f32[1280,512]{1,0:T(8,128)}, u32[]{:S(2)}) copy-start(f32[1280,512]{1,0:T(8,128)} %get-tuple-element.173.middle) | copy-start | bytes 7864324
  139.6 10.3 %collective-permute-start.12 = (bf16[576,512]{1,0:T(8,128)(2,1)S(1)}, bf16[576,512]{1,0:T(8,128)(2,1)S(1)}, u32[]{:S(2)}, u32[]{:S(2)}) collective-permute-start(bf16[576,512]{1,0:T(8,128)(2,1)S(1)} %get-tuple-element.205), channel_id=1, source_target_pairs={{0,1},{1,0},{2,3},{3,2},{4,5},{5,4},{6,7},{7,6},{8,9},{9,8},{10,11... | collective-permute-start | bytes 1769480 | tf_op jit(solution)/shard_map/ppermute | solution.py:675
  141.6 10.0 %collective-permute-start.11 = (bf16[320,512]{1,0:T(8,128)(2,1)S(1)}, bf16[320,512]{1,0:T(8,128)(2,1)S(1)}, u32[]{:S(2)}, u32[]{:S(2)}) collective-permute-start(bf16[320,512]{1,0:T(8,128)(2,1)S(1)} %get-tuple-element.292), channel_id=1, source_target_pairs={{0,2},{1,9},{2,0},{3,11},{4,6},{5,13},{6,4},{7,15},{8,10},{9,1},{1... | collective-permute-start | bytes 983048 | tf_op jit(solution)/shard_map/ppermute | solution.py:675
  150.1 9.4 %collective-permute-start.13 = (bf16[288,512]{1,0:T(8,128)(2,1)S(1)}, bf16[288,512]{1,0:T(8,128)(2,1)S(1)}, u32[]{:S(2)}, u32[]{:S(2)}) collective-permute-start(bf16[288,512]{1,0:T(8,128)(2,1)S(1)} %get-tuple-element.298), channel_id=1, source_target_pairs={{0,8},{1,17},{2,10},{3,19},{4,12},{5,21},{6,14},{7,23},{8,0},{9,25... | collective-permute-start | bytes 884744 | tf_op jit(solution)/shard_map/ppermute | solution.py:675
  151.7 16.5 %collective-permute-start.14 = (bf16[320,512]{1,0:T(8,128)(2,1)S(1)}, bf16[320,512]{1,0:T(8,128)(2,1)S(1)}, u32[]{:S(2)}, u32[]{:S(2)}) collective-permute-start(bf16[320,512]{1,0:T(8,128)(2,1)S(1)} %add_convert_fusion.5), channel_id=1, source_target_pairs={{0,4},{1,5},{2,6},{3,7},{4,0},{5,1},{6,2},{7,3},{8,12},{9,13},{10,... | collective-permute-start | bytes 983048 | tf_op jit(solution)/shard_map/ppermute | solution.py:675
  168.2 7.1 %collective-permute-start.16 = (bf16[320,512]{1,0:T(8,128)(2,1)S(1)}, bf16[320,512]{1,0:T(8,128)(2,1)S(1)}, u32[]{:S(2)}, u32[]{:S(2)}) collective-permute-start(bf16[320,512]{1,0:T(8,128)(2,1)S(1)} %add_convert_fusion.4), channel_id=1, source_target_pairs={{0,2},{1,9},{2,0},{3,11},{4,6},{5,13},{6,4},{7,15},{8,10},{9,1},{1... | collective-permute-start | bytes 983048 | tf_op jit(solution)/shard_map/ppermute | solution.py:675
  168.6 5.1 %collective-permute-start.15 = (bf16[144,512]{1,0:T(8,128)(2,1)S(1)}, bf16[144,512]{1,0:T(8,128)(2,1)S(1)}, u32[]{:S(2)}, u32[]{:S(2)}) collective-permute-start(bf16[144,512]{1,0:T(8,128)(2,1)S(1)} %get-tuple-element.304), channel_id=1, source_target_pairs={{0,16},{1,3},{2,18},{3,1},{4,20},{5,7},{6,22},{7,5},{8,24},{9,11},... | collective-permute-start | bytes 442376 | tf_op jit(solution)/shard_map/ppermute | solution.py:675
  175.5 11.6 %collective-permute-start.19 = (bf16[640,512]{1,0:T(8,128)(2,1)S(1)}, bf16[640,512]{1,0:T(8,128)(2,1)S(1)}, u32[]{:S(2)}, u32[]{:S(2)}) collective-permute-start(bf16[640,512]{1,0:T(8,128)(2,1)S(1)} %pad_maximum_fusion.2), channel_id=1, source_target_pairs={{0,16},{1,3},{2,18},{3,1},{4,20},{5,7},{6,22},{7,5},{8,24},{9,11},... | collective-permute-start | bytes 1966088 | tf_op jit(solution)/shard_map/ppermute | solution.py:675
  175.7 5.2 %collective-permute-start.17 = (bf16[72,512]{1,0:T(8,128)(2,1)S(1)}, bf16[72,512]{1,0:T(8,128)(2,1)S(1)}, u32[]{:S(2)}, u32[]{:S(2)}) collective-permute-start(bf16[72,512]{1,0:T(8,128)(2,1)S(1)} %get-tuple-element.308), channel_id=1, source_target_pairs={{0,2},{1,9},{2,0},{3,11},{4,6},{5,13},{6,4},{7,15},{8,10},{9,1},{1... | collective-permute-start | bytes 221192 | tf_op jit(solution)/shard_map/ppermute | solution.py:675
  180.9 6.1 %collective-permute-start.18 = (bf16[72,512]{1,0:T(8,128)(2,1)S(1)}, bf16[72,512]{1,0:T(8,128)(2,1)S(1)}, u32[]{:S(2)}, u32[]{:S(2)}) collective-permute-start(bf16[72,512]{1,0:T(8,128)(2,1)S(1)} %add_convert_fusion.13), channel_id=1, source_target_pairs={{0,4},{1,5},{2,6},{3,7},{4,0},{5,1},{6,2},{7,3},{8,12},{9,13},{10,... | collective-permute-start | bytes 221192 | tf_op jit(solution)/shard_map/ppermute | solution.py:675
  187.2 17.7 %collective-permute-start.22 = (bf16[1280,512]{1,0:T(8,128)(2,1)S(1)}, bf16[1280,512]{1,0:T(8,128)(2,1)S(1)}, u32[]{:S(2)}, u32[]{:S(2)}) collective-permute-start(bf16[1280,512]{1,0:T(8,128)(2,1)S(1)} %pad_maximum_fusion.1), channel_id=1, source_target_pairs={{0,8},{1,17},{2,10},{3,19},{4,12},{5,21},{6,14},{7,23},{8,0},{9,25... | collective-permute-start | bytes 3932168 | tf_op jit(solution)/shard_map/ppermute | solution.py:675
  187.7 5.1 %collective-permute-start.20 = (bf16[72,512]{1,0:T(8,128)(2,1)S(1)}, bf16[72,512]{1,0:T(8,128)(2,1)S(1)}, u32[]{:S(2)}, u32[]{:S(2)}) collective-permute-start(bf16[72,512]{1,0:T(8,128)(2,1)S(1)} %add_convert_fusion.12), channel_id=1, source_target_pairs={{0,2},{1,9},{2,0},{3,11},{4,6},{5,13},{6,4},{7,15},{8,10},{9,1},{1... | collective-permute-start | bytes 221192 | tf_op jit(solution)/shard_map/ppermute | solution.py:675
  192.8 8.0 %collective-permute-start.21 = (bf16[144,512]{1,0:T(8,128)(2,1)S(1)}, bf16[144,512]{1,0:T(8,128)(2,1)S(1)}, u32[]{:S(2)}, u32[]{:S(2)}) collective-permute-start(bf16[144,512]{1,0:T(8,128)(2,1)S(1)} %pad_maximum_fusion.9), channel_id=1, source_target_pairs={{0,16},{1,3},{2,18},{3,1},{4,20},{5,7},{6,22},{7,5},{8,24},{9,11},... | collective-permute-start | bytes 442376 | tf_op jit(solution)/shard_map/ppermute | solution.py:675
  205.3 7.2 %collective-permute-start.24 = (bf16[2560,512]{1,0:T(8,128)(2,1)S(1)}, bf16[2560,512]{1,0:T(8,128)(2,1)S(1)}, u32[]{:S(2)}, u32[]{:S(2)}) collective-permute-start(bf16[2560,512]{1,0:T(8,128)(2,1)S(1)} %pad_maximum_fusion.own), channel_id=1, source_target_pairs={{0,1},{1,0},{2,3},{3,2},{4,5},{5,4},{6,7},{7,6},{8,9},{9,8},{10,11... | collective-permute-start | bytes 7864328 | tf_op jit(solution)/shard_map/ppermute | solution.py:675
  205.4 6.8 %collective-permute-start.23 = (bf16[288,512]{1,0:T(8,128)(2,1)S(1)}, bf16[288,512]{1,0:T(8,128)(2,1)S(1)}, u32[]{:S(2)}, u32[]{:S(2)}) collective-permute-start(bf16[288,512]{1,0:T(8,128)(2,1)S(1)} %pad_maximum_fusion.6), channel_id=1, source_target_pairs={{0,8},{1,17},{2,10},{3,19},{4,12},{5,21},{6,14},{7,23},{8,0},{9,25... | collective-permute-start | bytes 884744 | tf_op jit(solution)/shard_map/ppermute | solution.py:675
  212.3 5.8 %collective-permute-start.25 = (bf16[576,512]{1,0:T(8,128)(2,1)S(1)}, bf16[576,512]{1,0:T(8,128)(2,1)S(1)}, u32[]{:S(2)}, u32[]{:S(2)}) collective-permute-start(bf16[576,512]{1,0:T(8,128)(2,1)S(1)} %pad_maximum_fusion.3.own), channel_id=1, source_target_pairs={{0,1},{1,0},{2,3},{3,2},{4,5},{5,4},{6,7},{7,6},{8,9},{9,8},{10,11... | collective-permute-start | bytes 1769480 | tf_op jit(solution)/shard_map/ppermute | solution.py:675
  (20 other events, 107.6 us)

commit v3 on v2

--- a/solution.py
+++ b/solution.py
@@ -195,34 +195,40 @@
 
 
 class Sender:
-    def __init__(self, hbm, slots, sems, step):
-        self.hbm, self.slots, self.sems, self.step = hbm, slots, sems, step
-        self.rows = slots.shape[1]
-        self.slot = lax.rem(step, 2)
-        self.ref = slots.at[self.slot]
-
-    def copy(self, step, slot):
-        at = pl.ds(pl.multiple_of(step * self.rows, 16), self.rows)
-        return pltpu.make_async_copy(self.slots.at[slot], self.hbm.at[at, :], self.sems.at[slot])
+    def __init__(self, hbm, held, sems, step, rows):
+        self.hbm, self.held, self.sems, self.step, self.rows = hbm, held, sems, step, rows
+        self.own = held.shape[0] > rows
+        self.ref = held.at[self.at(step), :] if self.own else held
+
+    def at(self, step):
+        return pl.ds(pl.multiple_of(step * self.rows, 16), self.rows)
+
+    def copy(self, step):
+        source = self.held.at[self.at(step), :] if self.own else self.held
+        return pltpu.make_async_copy(source, self.hbm.at[self.at(step), :], self.sems.at[step])
 
     def free(self):
-        pl.when(self.step >= 2)(lambda: self.copy(self.step - 2, self.slot).wait())
+        if not self.own:
+            pl.when(self.step > 0)(lambda: self.copy(self.step - 1).wait())
 
     def start(self):
-        self.copy(self.step, self.slot).start()
+        self.copy(self.step).start()
 
     def finish(self):
-        self.copy(self.step - 1, 1 - self.slot).wait()
-        self.copy(self.step, self.slot).wait()
+        if self.own:
+            for step in range(self.sems.shape[0]):
+                self.copy(step).wait()
+        else:
+            self.copy(self.step).wait()
 
 
 def forward_kernel(
     near, x_own, valid, cot, vecs, up_bias, w1, w2, w3, tx, ty,
-    x_above, x_marked, x_below, x_left, x_right, in_hbm, spec_hbm, w4_hbm, out_hbm, up_hbm,
-    waves_hbm, spread_hbm, prods_hbm, lead_out, middle_out, active_hbm, slope_hbm, down_hbm,
-    ext, waves, mixed_waves, active_all, gdown_all,
-    x_source, x_ext, in_w, spec, w4, out_w, up_w, waves_slots, spread_slots, prods_slots, slope_slots, grad_down,
-    in_sems, waves_sems, spread_sems, prods_sems, slope_sems, active_sems, down_sems,
+    x_above, x_marked, x_below, x_left, x_right, in_hbm, spec_hbm, w4_hbm, out_hbm, up_hbm, down_hbm,
+    waves_hbm, spread_hbm, prods_hbm, lead_out, middle_hbm, active_hbm, gmiddle_hbm, sent, kept, vec_sums, bias_sum,
+    ext, waves, mixed_waves, active_all, gdown_all, normed_all, slope_all, middle_all,
+    x_source, x_ext, in_w, spec, w4, out_w, up_w, down_w, waves_held, spread_held, prods_held, grad_down, grad_up,
+    in_sems, waves_sems, spread_sems, prods_sems, middle_sems, active_sems, gmiddle_sems, down_sems, up_sems,
 ):
     step = pl.program_id(0)
     last = pl.num_programs(0) - 1
@@ -231,7 +237,7 @@
     gain = vecs[GAIN_1 : GAIN_1 + 1, :]
     shift = vecs[SHIFT_1 : SHIFT_1 + 1, :]
     loads = copies(
-        [(in_hbm, in_w), (spec_hbm.at[: 3 * SLOTS, :], spec), (w4_hbm, w4), (out_hbm, out_w), (up_hbm, up_w)],
+        [(in_hbm, in_w), (spec_hbm.at[: 3 * SLOTS, :], spec), (w4_hbm, w4), (out_hbm, out_w), (up_hbm, up_w), (down_hbm, down_w)],
         in_sems,
     )
 
@@ -248,11 +254,13 @@
 
         pl.when(step == 0)(wait)
 
-    waves_to = Sender(waves_hbm, waves_slots, waves_sems, step)
-    spread_to = Sender(spread_hbm, spread_slots, spread_sems, step)
-    prods_to = Sender(prods_hbm, prods_slots, prods_sems, step)
-    slope_to = Sender(slope_hbm, slope_slots, slope_sems, step)
-    spread, prods = spread_to.ref, prods_to.ref
+    waves_to = Sender(waves_hbm, waves_held, waves_sems, step, waves_held.shape[0])
+    spread_to = Sender(spread_hbm, spread_held, spread_sems, step, chunk)
+    prods_to = Sender(prods_hbm, prods_held, prods_sems, step, chunk)
+    middle_to = Sender(middle_hbm, middle_all, middle_sems, step, chunk)
+    active_to = Sender(active_hbm, active_all, active_sems, step, chunk)
+    spread, prods = spread_held, prods_held
+    rows = pl.ds(pl.multiple_of(step * chunk, 16), chunk)
 
     def project(start, rows):
         at = pl.ds(start, rows)
@@ -282,7 +290,7 @@
     arrived(1)
     waves_to.free()
     spread_to.free()
-    depthwise(ext, OUT * step, spec, tx, ty, waves, mixed_waves, spread, waves_to.ref)
+    depthwise(ext, OUT * step, spec, tx, ty, waves, mixed_waves, spread, waves_held)
     waves_to.start()
     spread_to.start()
 
@@ -305,91 +313,81 @@
     prods_to.start()
     branch = dot(mixed.astype(BF16), out_w[...])
     middle = x_own[...].astype(F32) + vecs[SCALE_1 : SCALE_1 + 1, :] * branch
-    middle_out[...] = middle
+    middle_all[rows, :] = middle
+    middle_to.start()
     normal, _ = normalize(middle)
-    normed = (
-        (normal * vecs[GAIN_2 : GAIN_2 + 1, :] + vecs[SHIFT_2 : SHIFT_2 + 1, :]) * valid[...]
-    ).astype(BF16)
-    rows = pl.ds(pl.multiple_of(step * chunk, 16), chunk)
-    arrived(4)
-    slope_to.free()
+    gain_2 = vecs[GAIN_2 : GAIN_2 + 1, :]
+    normed = ((normal * gain_2 + vecs[SHIFT_2 : SHIFT_2 + 1, :]) * valid[rows, :]).astype(BF16)
+    normed_all[rows, :] = normed
+    arrived(4, 5)
     for block in range(4):
         lanes = slice(512 * block, 512 * block + 512)
         pre = dot(normed, up_w[:, lanes]) + up_bias[:, lanes]
         active, slope = gelu_pair(pre)
         active_all[rows, lanes] = active.astype(BF16)
-        slope_to.ref[:, lanes] = slope.astype(BF16)
-    slope_to.start()
-    gdown_all[rows, :] = (cot[...].astype(F32) * vecs[SCALE_2 : SCALE_2 + 1, :]).astype(BF16)
-
-    def active_copy(number):
-        at = pl.ds(pl.multiple_of(number * chunk, 16), chunk)
-        return pltpu.make_async_copy(active_all.at[at, :], active_hbm.at[at, :], active_sems.at[number])
-
-    active_copy(step).start()
+        slope_all[rows, lanes] = slope.astype(BF16)
+    active_to.start()
+    gdown_all[rows, :] = (cot[rows, :].astype(F32) * vecs[SCALE_2 : SCALE_2 + 1, :]).astype(BF16)
 
     @pl.when(step == last)
     def _():
-        parts = []
+        even = lax.axis_index("col") % 2 == 0
+
+        def part(source, to, block, sems):
+            lanes = slice(512 * block, 512 * block + 512)
+            return pltpu.make_async_copy(source.at[lanes, :], to.at[lanes, :], sems.at[block])
+
+        def both(act):
+            pl.when(even)(lambda: act(sent, kept))
+            pl.when(jnp.logical_not(even))(lambda: act(kept, sent))
+
         for block in range(4):
             lanes = slice(512 * block, 512 * block + 512)
             grad_down[lanes, :] = dot_left(gdown_all[...], active_all[:, lanes]).astype(BF16)
-            parts.append(
-                pltpu.make_async_copy(grad_down.at[lanes, :], down_hbm.at[lanes, :], down_sems.at[block])
-            )
-            parts[-1].start()
-        for sender in (waves_to, spread_to, prods_to, slope_to):
-            sender.finish()
-        for number in range(active_sems.shape[0]):
-            active_copy(number).wait()
-        for part in parts:
-            part.wait()
-
-
-def ffn_back_kernel(
-    cot, slope, middle, valid, vecs, down_w, up_w, grad_down,
-    gmiddle, sent, kept, vec_sums, bias_sum,
-    normed_all, gpre_all,
-):
-    step = pl.program_id(0)
-    chunk = cot.shape[0]
-    rows = pl.ds(pl.multiple_of(step * chunk, 16), chunk)
-
-    @pl.when(step == 0)
-    def _():
+
+        def send_down(for_up, for_down):
+            for block in range(4):
+                part(grad_down, for_down, block, down_sems).start()
+
+        both(send_down)
+
+        gmiddle = x_source
         vec_sums[...] = jnp.zeros_like(vec_sums)
         bias_sum[...] = jnp.zeros_like(bias_sum)
-
-    grad = cot[...].astype(F32)
-    gdown = (grad * vecs[SCALE_2 : SCALE_2 + 1, :]).astype(BF16)
-    gnormed = jnp.zeros((chunk, 512), F32)
-    for block in range(4):
-        lanes = slice(512 * block, 512 * block + 512)
-        gactive = dot_right(gdown, down_w[lanes, :])
-        gpre = (gactive * slope[:, lanes].astype(F32)).astype(BF16)
-        gpre_all[rows, lanes] = gpre
-        bias_sum[0:1, lanes] += jnp.sum(gpre.astype(F32), axis=0, keepdims=True)
-        gnormed = gnormed + dot_right(gpre, up_w[:, lanes])
-    normal, inverse = normalize(middle[...])
-    gain = vecs[GAIN_2 : GAIN_2 + 1, :]
-    mask = valid[...]
-    normed_all[rows, :] = ((normal * gain + vecs[SHIFT_2 : SHIFT_2 + 1, :]) * mask).astype(BF16)
-    masked = gnormed * mask
-    vec_sums[0:1, :] += jnp.sum(masked * normal, axis=0, keepdims=True)
-    vec_sums[1:2, :] += jnp.sum(masked, axis=0, keepdims=True)
-    gmiddle[...] = grad + norm_back(masked, normal, inverse, gain)
-
-    @pl.when(step == pl.num_programs(0) - 1)
-    def _():
+        pixels = gdown_all.shape[0]
+        half = pixels // 2
+        for k in range(2):
+            here = slice(half * k, half * k + half)
+            gnormed = jnp.zeros((half, 512), F32)
+            for block in range(4):
+                lanes = slice(512 * block, 512 * block + 512)
+                gactive = dot_right(gdown_all[here, :], down_w[lanes, :])
+                gpre = (gactive * slope_all[here, lanes].astype(F32)).astype(BF16)
+                slope_all[here, lanes] = gpre
+                bias_sum[0:1, lanes] += jnp.sum(gpre.astype(F32), axis=0, keepdims=True)
+                gnormed = gnormed + dot_right(gpre, up_w[:, lanes])
+            normal, inverse = normalize(middle_all[here, :])
+            masked = gnormed * valid[here, :]
+            vec_sums[0:1, :] += jnp.sum(masked * normal, axis=0, keepdims=True)
+            vec_sums[1:2, :] += jnp.sum(masked, axis=0, keepdims=True)
+            gmiddle[here, :] = cot[here, :].astype(F32) + norm_back(masked, normal, inverse, gain_2)
+            pltpu.make_async_copy(gmiddle.at[here, :], gmiddle_hbm.at[here, :], gmiddle_sems.at[k]).start()
+        for block in range(4):
+            lanes = slice(512 * block, 512 * block + 512)
+            grad_up[lanes, :] = dot_left(normed_all[...], slope_all[:, lanes]).astype(BF16)
+            both(lambda for_up, for_down, block=block: part(grad_up, for_up, block, up_sems).start())
+        for sender in (waves_to, spread_to, prods_to, middle_to, active_to):
+            sender.finish()
+        for k in range(2):
+            here = slice(half * k, half * k + half)
+            pltpu.make_async_copy(gmiddle.at[here, :], gmiddle_hbm.at[here, :], gmiddle_sems.at[k]).wait()
+
         def finish(for_up, for_down):
             for block in range(4):
-                lanes = slice(512 * block, 512 * block + 512)
-                for_up[lanes, :] = dot_left(normed_all[...], gpre_all[:, lanes]).astype(BF16)
-            for_down[: grad_down.shape[0], :] = grad_down[...]
-
-        even = lax.axis_index("col") % 2 == 0
-        pl.when(even)(lambda: finish(sent, kept))
-        pl.when(jnp.logical_not(even))(lambda: finish(kept, sent))
+                part(grad_down, for_down, block, down_sems).wait()
+                part(grad_up, for_up, block, up_sems).wait()
+
+        both(finish)
 
 
 def mixer_back_kernel(
@@ -800,77 +798,58 @@
     steps = tile_rows // OUT
     anywhere = pl.BlockSpec(memory_space=pl.ANY)
     in_smem = pl.BlockSpec(memory_space=pltpu.SMEM)
-    (
-        xwaves, spread, prods, lead, middle, active, slope, grad_down,
-    ) = pl.pallas_call(
-        forward_kernel,
-        grid=(steps,),
-        in_specs=[
-            in_smem,
-            chunked((chunk, width)), chunked((chunk, 1)), chunked((chunk, width)), whole((8, width)),
-            whole((1, hidden)), whole((128, 128)), whole((128, 128)), whole(w3.shape), whole(tab["window"].shape),
-            whole(tab["tile_back"].shape),
-            whole((HALO * tile_cols, width)), whole((pixels, width)), whole((HALO * tile_cols, width)),
-            whole((ext_rows, HALO, width)), whole((ext_rows, HALO, width)),
-        ] + [anywhere] * 5,
-        out_specs=[
-            anywhere, anywhere, anywhere, chunked((chunk, 128)), chunked((chunk, width)), anywhere, anywhere, anywhere,
-        ],
-        out_shape=[
-            shaped((steps * 2 * SLOTS * TILES, joined_count), BF16), shaped((pixels, joined_count), F32),
-            shaped((pixels, joined_count), F32), shaped((pixels, 128), F32),
-            shaped((pixels, width), F32), shaped((pixels, hidden), BF16), shaped((pixels, hidden), BF16),
-            shaped((hidden, width), BF16),
-        ],
-        scratch_shapes=[
-            pltpu.VMEM((ext_pixels, joined_count + 128), F32),
-            pltpu.VMEM((2 * SLOTS, LANES * TILES), F32), pltpu.VMEM((2 * SLOTS, LANES * TILES), BF16),
-            pltpu.VMEM((pixels, hidden), BF16), pltpu.VMEM((pixels, width), BF16),
-            pltpu.VMEM((ext_rows * tile_cols, width), F32), pltpu.VMEM((ext_pixels, width), F32),
-            pltpu.VMEM((width, joined_count), BF16),
-            pltpu.VMEM((3 * SLOTS, joined_count), F32), pltpu.VMEM(w4.shape, BF16), pltpu.VMEM((width, width), BF16),
-            pltpu.VMEM((width, hidden), BF16), pltpu.VMEM((2, 2 * SLOTS * TILES, joined_count), BF16),
-            pltpu.VMEM((2, chunk, joined_count), F32), pltpu.VMEM((2, chunk, joined_count), F32),
-            pltpu.VMEM((2, chunk, hidden), BF16), pltpu.VMEM((hidden, width), BF16),
-            pltpu.SemaphoreType.DMA((5,)), pltpu.SemaphoreType.DMA((2,)), pltpu.SemaphoreType.DMA((2,)),
-            pltpu.SemaphoreType.DMA((2,)), pltpu.SemaphoreType.DMA((2,)), pltpu.SemaphoreType.DMA((steps,)),
-            pltpu.SemaphoreType.DMA((4,)),
-        ],
-        compiler_params=params(58),
-        cost_estimate=cost(30),
-        name="forward",
-    )(
-        near, x_own, valid, cot, vecs, bias, w1, w2, w3, tab["window"], tab["tile_back"],
-        *x_source, in_weight, spec, w4, out_weight, up_weight,
-    )
-
     rows = 256
     count = pixels // rows
     wide = 640
     few = pixels // wide
     early = hidden + width
     late = 576
-    gmiddle, ffn_sent, ffn_kept, ffn_sums, bias_sum = pl.pallas_call(
-        ffn_back_kernel,
-        grid=(few,),
+    dma = pltpu.SemaphoreType.DMA
+    (
+        xwaves, spread, prods, lead, middle, active, gmiddle, ffn_sent, ffn_kept, ffn_sums, bias_sum,
+    ) = pl.pallas_call(
+        forward_kernel,
+        grid=(steps,),
         in_specs=[
-            chunked((wide, width)), chunked((wide, hidden)), chunked((wide, width)), chunked((wide, 1)),
-            whole((8, width)), whole((hidden, width)), whole((width, hidden)), whole((hidden, width)),
-        ],
-        out_specs=[
-            chunked((wide, width)), held((early, width)), held((early, width)), held((8, width)),
-            held((8, hidden)),
+            in_smem,
+            chunked((chunk, width)), whole((pixels, 1)), whole((pixels, width)), whole((8, width)),
+            whole((1, hidden)), whole((128, 128)), whole((128, 128)), whole(w3.shape), whole(tab["window"].shape),
+            whole(tab["tile_back"].shape),
+            whole((HALO * tile_cols, width)), whole((pixels, width)), whole((HALO * tile_cols, width)),
+            whole((ext_rows, HALO, width)), whole((ext_rows, HALO, width)),
+        ] + [anywhere] * 6,
+        out_specs=[anywhere, anywhere, anywhere, chunked((chunk, 128))] + [anywhere] * 5 + [
+            held((8, width)), held((8, hidden)),
         ],
         out_shape=[
-            shaped((pixels, width), F32), shaped((early, width), BF16), shaped((early, width), BF16),
-            shaped((8, width), F32),
+            shaped((steps * 2 * SLOTS * TILES, joined_count), BF16), shaped((pixels, joined_count), F32),
+            shaped((pixels, joined_count), F32), shaped((pixels, 128), F32),
+            shaped((pixels, width), F32), shaped((pixels, hidden), BF16), shaped((pixels, width), F32),
+            shaped((early, width), BF16), shaped((early, width), BF16), shaped((8, width), F32),
             shaped((8, hidden), F32),
         ],
-        scratch_shapes=[pltpu.VMEM((pixels, width), BF16), pltpu.VMEM((pixels, hidden), BF16)],
-        compiler_params=params(48),
-        cost_estimate=cost(16),
-        name="ffn_back",
-    )(cot, slope, middle, valid, vecs, down_weight, up_weight, grad_down)
+        scratch_shapes=[
+            pltpu.VMEM((ext_pixels, joined_count + 128), F32),
+            pltpu.VMEM((2 * SLOTS, LANES * TILES), F32), pltpu.VMEM((2 * SLOTS, LANES * TILES), BF16),
+            pltpu.VMEM((pixels, hidden), BF16), pltpu.VMEM((pixels, width), BF16), pltpu.VMEM((pixels, width), BF16),
+            pltpu.VMEM((pixels, hidden), BF16), pltpu.VMEM((pixels, width), F32),
+            pltpu.VMEM((ext_rows * tile_cols, width), F32), pltpu.VMEM((ext_pixels, width), F32),
+            pltpu.VMEM((width, joined_count), BF16),
+            pltpu.VMEM((3 * SLOTS, joined_count), F32), pltpu.VMEM(w4.shape, BF16), pltpu.VMEM((width, width), BF16),
+            pltpu.VMEM((width, hidden), BF16), pltpu.VMEM((hidden, width), BF16),
+            pltpu.VMEM((2 * SLOTS * TILES, joined_count), BF16),
+            pltpu.VMEM((chunk, joined_count), F32), pltpu.VMEM((chunk, joined_count), F32),
+            pltpu.VMEM((hidden, width), BF16), pltpu.VMEM((hidden, width), BF16),
+            dma((6,)), dma((steps,)), dma((steps,)), dma((steps,)), dma((steps,)), dma((steps,)), dma((2,)),
+            dma((4,)), dma((4,)),
+        ],
+        compiler_params=params(62),
+        cost_estimate=cost(45),
+        name="forward",
+    )(
+        near, x_own, valid, cot, vecs, bias, w1, w2, w3, tab["window"], tab["tile_back"],
+        *x_source, in_weight, spec, w4, out_weight, up_weight, down_weight,
+    )
 
     gspread, glead, ffn_sent, ffn_kept = pl.pallas_call(
         mixer_back_kernel,
@@ -902,6 +881,8 @@
     tie = lax.optimization_barrier
     block = gspread.reshape(tile_rows, tile_cols, joined_count)
     above, below = rows_around(block)
+    ffn.combine()
+    (gspread, ffn.sent, ffn.kept) = tie((gspread, ffn.sent, ffn.kept))
     grad_kernel = pl.pallas_call(
         kernel_back_kernel,
         grid=(steps,),
@@ -919,11 +900,9 @@
         cost_estimate=cost(9),
         name="kernel_back",
     )(xwaves, gspread, tab["tile"], tab["kernel_back"])
-    (above, below, grad_kernel, ffn.kept, ffn.got) = tie((above, below, grad_kernel, ffn.kept, ffn.got))
+    (above, below, grad_kernel, ffn.sent) = tie((above, below, grad_kernel, ffn.sent))
+    ffn.swap()
     left, right = cols_around(*masked((above, below), (same_up, same_down), 0.0), block)
-    ffn.combine()
-    (left, right, ffn.sent, ffn.kept) = tie((left, right, ffn.sent, ffn.kept))
-    ffn.swap()
     above, below = flat(above), flat(below)
 
     gjoined = pl.pallas_call(
@@ -967,7 +946,7 @@
         scratch_shapes=[
             pltpu.VMEM((pixels, width), BF16), pltpu.VMEM((pixels, joined_count), BF16), pltpu.VMEM((8, width), F32),
         ],
-        compiler_params=params(48),
+        compiler_params=params(24),
         cost_estimate=cost(8),
         name="in_back",
     )(
@@ -991,7 +970,7 @@
             out_specs=pl.BlockSpec((rows, width), lambda i: (i + first, 0)),
             out_shape=shaped((pixels, width), BF16),
             input_output_aliases={4: 0} if first else {},
-            compiler_params=params(48),
+            compiler_params=params(12),
             cost_estimate=cost(4),
             name="down",
         )(active, middle, vecs, down_weight, before)
@@ -1036,7 +1015,7 @@
         name="expand_early",
     )
     expanded = None
-    for who in "frfrrfrrfrfr":
+    for who in "frfrfrrrfrfr":
         way, other = (ffn, rest) if who == "f" else (rest, ffn)
         if not way.done:
             (other.kept,) = onward(way, other.kept)

time: 220 us -> 215 us (0.977)
  Pallas kernels: 101 us -> 88.8 us
  other arithmetic: 8.51 us -> 16 us
  starting transfers between devices: 46.1 us -> 43.5 us
    pallas_call x1 -> x0, Pallas kernels: 16.9 us -> none  [on_device(): pl.pallas_call(ffn_back_kernel, grid=(few,), in_specs=[chunked((wide, wid...]
    pallas_call x1, Pallas kernels: 31.9 us -> 41.3 us  [on_device(): pl.pallas_call(forward_kernel, grid=(steps,), in_specs=[in_smem, chunked(...]
    ppermute x18, waiting for transfers between devices: 46.2 us -> 50.5 us  [swap(): return lax.ppermute(block, AXES, self.pairs(step))]
    convert_element_type x6, other arithmetic: 2.62 us -> 6.28 us  [summed(): return (pieces[0] + pieces[1]).astype(BF16)]
    pallas_call x2, Pallas kernels: 8.04 us -> 4.99 us  [down(): pl.pallas_call(down_kernel, grid=(blocks,), in_specs=[pl.BlockSpec((rows,...]
    ppermute x2, waiting for transfers between devices: 2.73 us -> 0.01 us  [rows_around(): lax.ppermute(block[:HALO], 'row', up_pairs)]
    ppermute x18, starting transfers between devices: 25.3 us -> 22.8 us  [swap(): return lax.ppermute(block, AXES, self.pairs(step))]
    select_n x6, other arithmetic: 0.39 us -> 2.69 us  [combine(): jnp.where(bit, got, kept)]
  transfers between devices with their start and end apart: 26 -> 26, of which waited for: 12 -> 12; matrix products, arithmetic and copies ran while one was open for 5% -> 8% of each run, Pallas kernels for 19% -> 17%
where the time goes in v3:
time: 215 us; the launch traced here: 214 us
  Pallas kernels  88.8 us (41%)
  waiting for transfers between devices  50.6 us (24%)
  starting transfers between devices  43.5 us (20%)
  other arithmetic  16 us (7%)
  between operations  6.94 us (3%)
  local copies, waits for them, and re-layouts  5.87 us (3%)
  matrix products  2.84 us (1%)
    ppermute x18, waiting for transfers between devices, swap(): return lax.ppermute(block, AXES, self.pairs(step))  50.5 us
    pallas_call x1, Pallas kernels, on_device(): pl.pallas_call(forward_kernel, grid=(steps,), in_specs=[in_smem, chunked(...  41.3 us
    ppermute x18, starting transfers between devices, swap(): return lax.ppermute(block, AXES, self.pairs(step))  22.8 us
    pallas_call x1, Pallas kernels, on_device(): pl.pallas_call(gates_back_kernel, grid=(steps,), in_specs=[in_smem, whole...  11.5 us
    ppermute x2, starting transfers between devices, rows_around(): lax.ppermute(block[-HALO:], 'row', down_pairs)  9.41 us
    pallas_call x1, Pallas kernels, on_device(): pl.pallas_call(kernel_back_kernel, grid=(steps,), in_specs=[chunked((2 *...  9.17 us
    pallas_call x1, Pallas kernels, on_device(): pl.pallas_call(mixer_back_kernel, grid=(few,), in_specs=[chunked((wide, w...  9 us
    convert_element_type x6, other arithmetic, summed(): return (pieces[0] + pieces[1]).astype(BF16)  6.28 us
  transfers between devices with their start and end apart: 26, of which 12 were waited for; matrix products, arithmetic and copies ran while one was open for 8% of the time, Pallas kernels for 17%

profile of v3, /device:TPU:0, one launch (start us, length us, event | category | flops | bytes accessed | tf_op | source)
XLA Modules:
  0.0 214.5 jit_solution(8198525292880323571)
XLA Ops:
  1.4 1.6 broadcast_select_fusion.2
  3.1 4.8 %collective-permute-start = (bf16[3,40,512]{2,1,0:T(8,128)(2,1)S(1)}, bf16[3,40,512]{2,1,0:T(8,128)(2,1)S(1)}, u32[]{:S(2)}, u32[]{:S(2)}) collective-permute-start(bf16[3,40,512]{2,1,0:T(8,128)(2,1)S(1)} %get-tuple-element.289), channel_id=1, source_target_pairs={{0,8},{8,16},{16,24},{1,9},{9,17},{17,25},{2,10},{10,18},{18,26},{... | collective-permute-start | bytes 368648 | tf_op jit(solution)/shard_map/ppermute | solution.py:758
  8.0 1.3 collective-permute-start.1
  13.9 2.8 %fusion.spec_hbm.spec = f32[672,1024]{1,0:T(8,128)} fusion(f32[672,49]{1,0:T(8,128)S(1)} %copy-done.27, bf16[49,992]{1,0:T(8,128)(2,1)S(1)} %reshape.166), kind=kOutput, calls=%fused_computation.41 | convolution fusion | flops 404619264 | bytes 2981440 | tf_op jit(solution)/shard_map/dot_general | solution.py:777
  17.2 1.3 collective-permute-start.3
  18.6 3.0 %collective-permute-start.2 = (bf16[38,3,512]{2,1,0:T(4,128)(2,1)S(1)}, bf16[38,3,512]{2,1,0:T(4,128)(2,1)S(1)}, u32[]{:S(2)}, u32[]{:S(2)}) collective-permute-start(bf16[38,3,512]{2,1,0:T(4,128)(2,1)S(1)} %pad_maximum_fusion.7), channel_id=1, source_target_pairs={{0,1},{1,2},{2,3},{3,4},{4,5},{5,6},{6,7},{8,9},{9,10},{10,11},{11... | collective-permute-start | bytes 350216 | tf_op jit(solution)/shard_map/ppermute | solution.py:765
  26.4 1.1 copy.46.valid
  27.6 41.3 %forward.1 = (bf16[4480,1024]{1,0:T(8,128)(2,1)}, f32[1280,1024]{1,0:T(8,128)}, f32[1280,1024]{1,0:T(8,128)}, f32[1280,128]{1,0:T(8,128)}, f32[1280,512]{1,0:T(8...) custom-call(s32[4]{0:T(128)} %add_convert_fusion.16.near, ...), custom_call_target="tpu_custom_call" | custom-call | flops 449999994880 | bytes 1350000000 | tf_op jit(solution)/shard_map/forward/pallas_call | solution.py:810
  68.9 1.1 copy-done.22
  70.0 9.0 %mixer_back.1 = (bf16[1280,1024]{1,0:T(8,128)(2,1)S(1)}, f32[1280,128]{1,0:T(8,128)S(1)}, bf16[2560,512]{1,0:T(8,128)(2,1)}, bf16[2560,512]{1,0:T(8,128)(2,1)}) custom-call(f32[1280,512]{1,0:T(8,128)} %get-tuple-element.168.gmiddle, f32[1280,1024]{1,0:T(8,128)} %get-tuple-element.169.spread, ...), custom_call_target="tpu_custom_call", output_to_operand_aliasing={{2}: (10, {}), {3}: (11, {})} | custom-call | flops 89999998976 | bytes 270000000 | tf_op jit(solution)/shard_map/mixer_back/pallas_call | solution.py:854
  79.0 0.8 copy-done.20
  79.8 1.2 collective-permute-start.6
  81.1 4.6 %collective-permute-start.4 = (bf16[3,40,1024]{2,1,0:T(8,128)(2,1)S(1)}, bf16[3,40,1024]{2,1,0:T(8,128)(2,1)S(1)}, u32[]{:S(2)}, u32[]{:S(2)}) collective-permute-start(bf16[3,40,1024]{2,1,0:T(8,128)(2,1)S(1)} %bitcast.38), channel_id=1, source_target_pairs={{0,8},{8,16},{16,24},{1,9},{9,17},{17,25},{2,10},{10,18},{18,26},{... | collective-permute-start | bytes 737288 | tf_op jit(solution)/shard_map/ppermute | solution.py:758
  85.6 1.3 collective-permute-start.5
  87.2 4.8 %add_convert_fusion = (bf16[1280,512]{1,0:T(8,128)(2,1)}, bf16[1280,512]{1,0:T(8,128)(2,1)}) fusion(bf16[2560,512]{1,0:T(8,128)(2,1)} %collective-permute-done.6, s32[]{:T(128)S(6)} %mul.49, bf16[2560,512]{1,0:T(8,128)(2,1)} %get-tuple-element.176, s32[]{:T(128)S(6)} %select_n.187), kind=kLoop, calls=%fused_computation.1 | loop fusion | flops 5242880 | bytes 7864328 | tf_op jit(solution)/shard_map/convert_element_type | solution.py:706
  92.0 9.2 %kernel_back.1.grad_kernel = bf16[112,512]{1,0:T(8,128)(2,1)S(1)} custom-call(bf16[4480,1024]{1,0:T(8,128)(2,1)} %get-tuple-element.175.xwaves, bf16[1280,1024]{1,0:T(8,128)(2,1)S(1)} %get-tuple-element.178.gspread.own, bf16[224,64]{1,0:T(8,128)(2,1)S(1)} %copy-done.16, f32[56,448]{1,0:T(8,128)S(1)} %copy-done.15), custom_call_target="tpu_custom_call" | custom-call | flops 89999998976 | bytes 270000000 | tf_op jit(solution)/shard_map/kernel_back/pallas_call | solution.py:886
  101.6 1.3 collective-permute-start.8
  103.1 3.0 %collective-permute-start.7 = (bf16[38,3,1024]{2,1,0:T(4,128)(2,1)S(1)}, bf16[38,3,1024]{2,1,0:T(4,128)(2,1)S(1)}, u32[]{:S(2)}, u32[]{:S(2)}) collective-permute-start(bf16[38,3,1024]{2,1,0:T(4,128)(2,1)S(1)} %pad_maximum_fusion.4), channel_id=1, source_target_pairs={{0,1},{1,2},{2,3},{3,4},{4,5},{5,6},{6,7},{8,9},{9,10},{10,11},{11... | collective-permute-start | bytes 700424 | tf_op jit(solution)/shard_map/ppermute | solution.py:765
  106.2 3.1 %collective-permute-start.9 = (bf16[1280,512]{1,0:T(8,128)(2,1)}, bf16[1280,512]{1,0:T(8,128)(2,1)S(1)}, u32[]{:S(2)}, u32[]{:S(2)}) collective-permute-start(bf16[1280,512]{1,0:T(8,128)(2,1)} %get-tuple-element.183), channel_id=1, source_target_pairs={{0,8},{1,17},{2,10},{3,19},{4,12},{5,21},{6,14},{7,23},{8,0},{9,25... | collective-permute-start | bytes 3932168 | tf_op jit(solution)/shard_map/ppermute | solution.py:673
  109.4 11.5 %gates_back.1.gjoined = bf16[1280,1024]{1,0:T(8,128)(2,1)S(1)} custom-call(s32[4]{0:T(128)S(1)} %copy-done.7, bf16[120,1024]{1,0:T(8,128)(2,1)S(1)} %bitcast.32, bf16[1280,1024]{1,0:T(8,128)(2,1)} %copy-done.2, bf16[120,1024]{1,0:T(8,128)(2,1)S(1)} %bitcast.33, bf16[38,3,1024]{2,1,0:T(4,128)(2,1)S(1)} %collective-permute-done.7.left, ...), custom_call_target="tpu_custom_call" | custom-call | flops 109999996928 | bytes 330000000 | tf_op jit(solution)/shard_map/gates_back/pallas_call | solution.py:908
  120.9 4.2 %collective-permute-done.9 = bf16[1280,512]{1,0:T(8,128)(2,1)S(1)} collective-permute-done((bf16[1280,512]{1,0:T(8,128)(2,1)}, bf16[1280,512]{1,0:T(8,128)(2,1)S(1)}, u32[]{:S(2)}, u32[]{:S(2)}) %collective-permute-start.9) | collective-permute-done | bytes 1310752 | tf_op jit(solution)/shard_map/ppermute | solution.py:673
  125.5 3.5 %collective-permute-start.10 = (bf16[640,512]{1,0:T(8,128)(2,1)S(1)}, bf16[640,512]{1,0:T(8,128)(2,1)S(1)}, u32[]{:S(2)}, u32[]{:S(2)}) collective-permute-start(bf16[640,512]{1,0:T(8,128)(2,1)S(1)} %get-tuple-element.193), channel_id=1, source_target_pairs={{0,16},{1,3},{2,18},{3,1},{4,20},{5,7},{6,22},{7,5},{8,24},{9,11},... | collective-permute-start | bytes 1966088 | tf_op jit(solution)/shard_map/ppermute | solution.py:673
  129.1 5.8 %in_back.1 = (bf16[1280,512]{1,0:T(8,128)(2,1)}, bf16[576,512]{1,0:T(8,128)(2,1)S(1)}, bf16[576,512]{1,0:T(8,128)(2,1)S(1)}) custom-call(bf16[1280,1024]{1,0:T(8,128)(2,1)S(1)} %gates_back.1.gjoined, bf16[1280,512]{1,0:T(8,128)(2,1)S(1)} %bitcast.30, f32[1280,512]{1,0:T(8,128)S(1)} %copy-done.19, f32[1280,1]{1,0:T(8,128)S(1)} %copy-done.1, ...), custom_call_target="tpu_custom_call" | custom-call | flops 80000000000 | bytes 240000000 | tf_op jit(solution)/shard_map/in_back/pallas_call | solution.py:934
  135.0 2.6 %collective-permute-done.10 = bf16[640,512]{1,0:T(8,128)(2,1)S(1)} collective-permute-done((bf16[640,512]{1,0:T(8,128)(2,1)S(1)}, bf16[640,512]{1,0:T(8,128)(2,1)S(1)}, u32[]{:S(2)}, u32[]{:S(2)}) %collective-permute-start.10) | collective-permute-done | bytes 655392 | tf_op jit(solution)/shard_map/ppermute | solution.py:673
  137.8 1.6 collective-permute-start.11
  139.5 2.1 %down.2.before = bf16[1280,512]{1,0:T(8,128)(2,1)} custom-call(bf16[1280,2048]{1,0:T(8,128)(2,1)S(1)} %bitcast.35, f32[1280,512]{1,0:T(8,128)S(1)} %copy-done.18, f32[8,512]{1,0:T(8,128)S(1)} %copy-done.6, bf16[2048,512]{1,0:T(8,128)(2,1)S(1)} %copy-done.8, bf16[8,128]{1,0:T(8,128)(2,1)S(1)} %broadcast_in_dim.30.before), custom_call_target="tpu_custom_call" | custom-call | flops 40000000000 | bytes 120000000 | tf_op jit(solution)/shard_map/down/pallas_call | solution.py:962
  142.4 2.5 %collective-permute-done.11 = bf16[320,512]{1,0:T(8,128)(2,1)S(1)} collective-permute-done((bf16[320,512]{1,0:T(8,128)(2,1)S(1)}, bf16[320,512]{1,0:T(8,128)(2,1)S(1)}, u32[]{:S(2)}, u32[]{:S(2)}) %collective-permute-start.11) | collective-permute-done | bytes 327712 | tf_op jit(solution)/shard_map/ppermute | solution.py:673
  145.0 2.6 %collective-permute-start.14 = (bf16[320,512]{1,0:T(8,128)(2,1)S(1)}, bf16[320,512]{1,0:T(8,128)(2,1)S(1)}, u32[]{:S(2)}, u32[]{:S(2)}) collective-permute-start(bf16[320,512]{1,0:T(8,128)(2,1)S(1)} %add_convert_fusion.5), channel_id=1, source_target_pairs={{0,4},{1,5},{2,6},{3,7},{4,0},{5,1},{6,2},{7,3},{8,12},{9,13},{10,... | collective-permute-start | bytes 983048 | tf_op jit(solution)/shard_map/ppermute | solution.py:673
  147.7 2.8 %down.3 = bf16[1280,512]{1,0:T(8,128)(2,1)} custom-call(bf16[1280,2048]{1,0:T(8,128)(2,1)S(1)} %bitcast.35, f32[1280,512]{1,0:T(8,128)S(1)} %copy-done.18, f32[8,512]{1,0:T(8,128)S(1)} %copy-done.6, bf16[2048,512]{1,0:T(8,128)(2,1)S(1)} %copy-done.8, bf16[1280,512]{1,0:T(8,128)(2,1)} %down.2.before), custom_call_target="tpu_custom_call", output_to_operand_aliasing={{}: (4, {})} | custom-call | flops 40000000000 | bytes 120000000 | tf_op jit(solution)/shard_map/down/pallas_call | solution.py:962
  150.6 10.6 %collective-permute-done.14 = bf16[320,512]{1,0:T(8,128)(2,1)S(1)} collective-permute-done((bf16[320,512]{1,0:T(8,128)(2,1)S(1)}, bf16[320,512]{1,0:T(8,128)(2,1)S(1)}, u32[]{:S(2)}, u32[]{:S(2)}) %collective-permute-start.14) | collective-permute-done | bytes 327712 | tf_op jit(solution)/shard_map/ppermute | solution.py:673
  161.4 1.9 collective-permute-start.15
  163.3 3.3 %collective-permute-done.15 = bf16[144,512]{1,0:T(8,128)(2,1)S(1)} collective-permute-done((bf16[144,512]{1,0:T(8,128)(2,1)S(1)}, bf16[144,512]{1,0:T(8,128)(2,1)S(1)}, u32[]{:S(2)}, u32[]{:S(2)}) %collective-permute-start.15) | collective-permute-done | bytes 147488 | tf_op jit(solution)/shard_map/ppermute | solution.py:673
  167.3 1.2 collective-permute-done.16
  168.6 1.9 collective-permute-start.18
  170.4 0.8 collective-permute-start.17
  171.2 4.7 %collective-permute-done.17 = bf16[72,512]{1,0:T(8,128)(2,1)} collective-permute-done((bf16[72,512]{1,0:T(8,128)(2,1)}, bf16[72,512]{1,0:T(8,128)(2,1)}, u32[]{:S(2)}, u32[]{:S(2)}) %collective-permute-start.17) | collective-permute-done | bytes 73760 | tf_op jit(solution)/shard_map/ppermute | solution.py:673
  176.0 0.9 add_convert_fusion.13
  176.9 2.3 %collective-permute-done.18 = bf16[640,512]{1,0:T(8,128)(2,1)S(1)} collective-permute-done((bf16[640,512]{1,0:T(8,128)(2,1)S(1)}, bf16[640,512]{1,0:T(8,128)(2,1)S(1)}, u32[]{:S(2)}, u32[]{:S(2)}) %collective-permute-start.18) | collective-permute-done | bytes 655392 | tf_op jit(solution)/shard_map/ppermute | solution.py:673
  179.4 1.4 collective-permute-start.22
  181.4 5.1 %collective-permute-done.19 = bf16[72,512]{1,0:T(8,128)(2,1)S(1)} collective-permute-done((bf16[72,512]{1,0:T(8,128)(2,1)S(1)}, bf16[72,512]{1,0:T(8,128)(2,1)S(1)}, u32[]{:S(2)}, u32[]{:S(2)}) %collective-permute-start.19) | collective-permute-done | bytes 73760 | tf_op jit(solution)/shard_map/ppermute | solution.py:673
  186.6 4.3 %collective-permute-done.20 = bf16[72,512]{1,0:T(8,128)(2,1)S(1)} collective-permute-done((bf16[72,512]{1,0:T(8,128)(2,1)S(1)}, bf16[72,512]{1,0:T(8,128)(2,1)S(1)}, u32[]{:S(2)}, u32[]{:S(2)}) %collective-permute-start.20) | collective-permute-done | bytes 73760 | tf_op jit(solution)/shard_map/ppermute | solution.py:673
  191.6 2.5 %collective-permute-start.21 = (bf16[144,512]{1,0:T(8,128)(2,1)}, bf16[144,512]{1,0:T(8,128)(2,1)}, u32[]{:S(2)}, u32[]{:S(2)}) collective-permute-start(bf16[144,512]{1,0:T(8,128)(2,1)} %pad_maximum_fusion.9), channel_id=1, source_target_pairs={{0,16},{1,3},{2,18},{3,1},{4,20},{5,7},{6,22},{7,5},{8,24},{9,11},... | collective-permute-start | bytes 442376 | tf_op jit(solution)/shard_map/ppermute | solution.py:673
  194.2 3.4 %collective-permute-done.21 = bf16[144,512]{1,0:T(8,128)(2,1)} collective-permute-done((bf16[144,512]{1,0:T(8,128)(2,1)}, bf16[144,512]{1,0:T(8,128)(2,1)}, u32[]{:S(2)}, u32[]{:S(2)}) %collective-permute-start.21) | collective-permute-done | bytes 147488 | tf_op jit(solution)/shard_map/ppermute | solution.py:673
  197.6 1.0 broadcast_select_fusion.12
  198.7 1.5 broadcast_select_fusion.1
  201.1 6.1 %collective-permute-done.23 = bf16[288,512]{1,0:T(8,128)(2,1)S(1)} collective-permute-done((bf16[288,512]{1,0:T(8,128)(2,1)S(1)}, bf16[288,512]{1,0:T(8,128)(2,1)S(1)}, u32[]{:S(2)}, u32[]{:S(2)}) %collective-permute-start.23) | collective-permute-done | bytes 294944 | tf_op jit(solution)/shard_map/ppermute | solution.py:673
  207.4 5.4 %expand_early.1 = (f32[2048,512]{1,0:T(8,128)}, f32[512,2048]{1,0:T(8,128)}, f32[1,512]{1,0:T(1,128)}, f32[512,512]{1,0:T(8,128)}, f32[256,512]{1,0:T(8,128)}, /...) custom-call(bf16[2560,512]{1,0:T(8,128)(2,1)S(1)} %pad_maximum_fusion.own, ...), custom_call_target="tpu_custom_call" | custom-call | flops 49999998976 | bytes 150000000 | tf_op jit(solution)/shard_map/expand_early/pallas_call | solution.py:1023
  212.9 1.6 expand_late.1
  (164 shorter events, 11.4 us)
Async XLA Ops:
  1.4 11.1 %copy-start.30 = (bf16[7,7,992]{2,1,0:T(8,128)(2,1)S(1)}, bf16[7,7,992]{2,1,0:T(8,128)(2,1)}, u32[]{:S(2)}) copy-start(bf16[7,7,992]{2,1,0:T(8,128)(2,1)} %param.33) | copy-start | bytes 291652
  1.4 11.2 %copy-start.33 = (bf16[32,64]{1,0:T(8,128)(2,1)S(1)}, bf16[32,64]{1,0:T(8,128)(2,1)}, u32[]{:S(2)}) copy-start(bf16[32,64]{1,0:T(8,128)(2,1)} %param.34) | copy-start | bytes 12292
  1.4 11.9 %copy-start.32 = (bf16[64,128]{1,0:T(8,128)(2,1)S(1)}, bf16[64,128]{1,0:T(8,128)(2,1)}, u32[]{:S(2)}) copy-start(bf16[64,128]{1,0:T(8,128)(2,1)} %param.35) | copy-start | bytes 49156
  1.4 12.5 %copy-start.27 = (f32[672,49]{1,0:T(8,128)S(1)}, f32[672,49]{1,0:T(8,128)}, u32[]{:S(2)}) copy-start(f32[672,49]{1,0:T(8,128)} %constant.128.clone) | copy-start | bytes 395140
  3.1 13.7 %copy-start.26 = (bf16[32,40,512]{2,1,0:T(8,128)(2,1)}, bf16[32,40,512]{2,1,0:T(8,128)(2,1)S(1)}, u32[]{:S(2)}) copy-start(bf16[32,40,512]{2,1,0:T(8,128)(2,1)S(1)} %broadcast_select_fusion.2) | copy-start | bytes 3932164
  3.1 13.8 %collective-permute-start = (bf16[3,40,512]{2,1,0:T(8,128)(2,1)S(1)}, bf16[3,40,512]{2,1,0:T(8,128)(2,1)S(1)}, u32[]{:S(2)}, u32[]{:S(2)}) collective-permute-start(bf16[3,40,512]{2,1,0:T(8,128)(2,1)S(1)} %get-tuple-element.289), channel_id=1, source_target_pairs={{0,8},{8,16},{16,24},{1,9},{9,17},{17,25},{2,10},{10,18},{18,26},{... | collective-permute-start | bytes 368648 | tf_op jit(solution)/shard_map/ppermute | solution.py:758
  8.0 9.0 %collective-permute-start.1 = (bf16[3,40,512]{2,1,0:T(8,128)(2,1)S(1)}, bf16[3,40,512]{2,1,0:T(8,128)(2,1)S(1)}, u32[]{:S(2)}, u32[]{:S(2)}) collective-permute-start(bf16[3,40,512]{2,1,0:T(8,128)(2,1)S(1)} %get-tuple-element.288), channel_id=1, source_target_pairs={{8,0},{16,8},{24,16},{9,1},{17,9},{25,17},{10,2},{18,10},{26,18},{... | collective-permute-start | bytes 368648 | tf_op jit(solution)/shard_map/ppermute | solution.py:758
  16.8 9.4 %copy-start.31 = (s32[32,40]{1,0:T(8,128)S(1)}, s32[32,40]{1,0:T(8,128)}, u32[]{:S(2)}) copy-start(s32[32,40]{1,0:T(8,128)} %param.46) | copy-start | bytes 15364
  16.9 10.5 %copy-start.28 = (bf16[3,40,512]{2,1,0:T(8,128)(2,1)}, bf16[3,40,512]{2,1,0:T(8,128)(2,1)S(1)}, u32[]{:S(2)}) copy-start(bf16[3,40,512]{2,1,0:T(8,128)(2,1)S(1)} %collective-permute-done) | copy-start | bytes 368644
  17.0 10.5 %copy-start.29 = (bf16[3,40,512]{2,1,0:T(8,128)(2,1)}, bf16[3,40,512]{2,1,0:T(8,128)(2,1)S(1)}, u32[]{:S(2)}) copy-start(bf16[3,40,512]{2,1,0:T(8,128)(2,1)S(1)} %collective-permute-done.1) | copy-start | bytes 368644
  17.2 9.2 %collective-permute-start.3 = (bf16[38,3,512]{2,1,0:T(4,128)(2,1)S(1)}, bf16[38,3,512]{2,1,0:T(4,128)(2,1)S(1)}, u32[]{:S(2)}, u32[]{:S(2)}) collective-permute-start(bf16[38,3,512]{2,1,0:T(4,128)(2,1)S(1)} %pad_maximum_fusion.8), channel_id=1, source_target_pairs={{1,0},{2,1},{3,2},{4,3},{5,4},{6,5},{7,6},{9,8},{10,9},{11,10},{12... | collective-permute-start | bytes 350216 | tf_op jit(solution)/shard_map/ppermute | solution.py:765
  18.6 7.8 %collective-permute-start.2 = (bf16[38,3,512]{2,1,0:T(4,128)(2,1)S(1)}, bf16[38,3,512]{2,1,0:T(4,128)(2,1)S(1)}, u32[]{:S(2)}, u32[]{:S(2)}) collective-permute-start(bf16[38,3,512]{2,1,0:T(4,128)(2,1)S(1)} %pad_maximum_fusion.7), channel_id=1, source_target_pairs={{0,1},{1,2},{2,3},{3,4},{4,5},{5,6},{6,7},{8,9},{9,10},{10,11},{11... | collective-permute-start | bytes 350216 | tf_op jit(solution)/shard_map/ppermute | solution.py:765
  27.5 41.3 %copy-start.3 = (bf16[128,128]{1,0:T(8,128)(2,1)S(1)}, bf16[128,128]{1,0:T(8,128)(2,1)}, u32[]{:S(2)}) copy-start(bf16[128,128]{1,0:T(8,128)(2,1)} %scatter.9.w2) | copy-start | bytes 98308
  27.5 41.3 %copy-start.4 = (bf16[128,128]{1,0:T(8,128)(2,1)S(1)}, bf16[128,128]{1,0:T(8,128)(2,1)}, u32[]{:S(2)}) copy-start(bf16[128,128]{1,0:T(8,128)(2,1)} %scatter.6.w1) | copy-start | bytes 98308
  27.5 41.3 %copy-start.5 = (f32[8,512]{1,0:T(8,128)S(1)}, f32[8,512]{1,0:T(8,128)}, u32[]{:S(2)}) copy-start(f32[8,512]{1,0:T(8,128)} %convert_element_type.177.vecs) | copy-start | bytes 49156
  27.5 41.3 %copy-start.10 = (bf16[512,512]{1,0:T(8,128)(2,1)S(1)}, bf16[512,512]{1,0:T(8,128)(2,1)}, u32[]{:S(2)}) copy-start(bf16[512,512]{1,0:T(8,128)(2,1)} %out_w.3) | copy-start | bytes 1572868
  27.5 41.3 %copy-start.12 = (bf16[256,512]{1,0:T(8,128)(2,1)S(1)}, bf16[256,512]{1,0:T(8,128)(2,1)}, u32[]{:S(2)}) copy-start(bf16[256,512]{1,0:T(8,128)(2,1)} %w4.1) | copy-start | bytes 786436
  27.6 41.3 %copy-start.13 = (bf16[128,256]{1,0:T(8,128)(2,1)S(1)}, bf16[128,256]{1,0:T(8,128)(2,1)}, u32[]{:S(2)}) copy-start(bf16[128,256]{1,0:T(8,128)(2,1)} %w3.3) | copy-start | bytes 196612
  79.8 12.2 %copy-start.2 = (bf16[1280,1024]{1,0:T(8,128)(2,1)}, bf16[1280,1024]{1,0:T(8,128)(2,1)S(1)}, u32[]{:S(2)}) copy-start(bf16[1280,1024]{1,0:T(8,128)(2,1)S(1)} %get-tuple-element.178.gspread.own) | copy-start | bytes 7864324
  79.8 7.3 %collective-permute-start.6 = (bf16[2560,512]{1,0:T(8,128)(2,1)}, bf16[2560,512]{1,0:T(8,128)(2,1)}, u32[]{:S(2)}, u32[]{:S(2)}) collective-permute-start(bf16[2560,512]{1,0:T(8,128)(2,1)} %get-tuple-element.177), channel_id=1, source_target_pairs={{0,1},{1,0},{2,3},{3,2},{4,5},{5,4},{6,7},{7,6},{8,9},{9,8},{10,11... | collective-permute-start | bytes 7864328 | tf_op jit(solution)/shard_map/ppermute | solution.py:673
  81.1 20.2 %collective-permute-start.4 = (bf16[3,40,1024]{2,1,0:T(8,128)(2,1)S(1)}, bf16[3,40,1024]{2,1,0:T(8,128)(2,1)S(1)}, u32[]{:S(2)}, u32[]{:S(2)}) collective-permute-start(bf16[3,40,1024]{2,1,0:T(8,128)(2,1)S(1)} %bitcast.38), channel_id=1, source_target_pairs={{0,8},{8,16},{16,24},{1,9},{9,17},{17,25},{2,10},{10,18},{18,26},{... | collective-permute-start | bytes 737288 | tf_op jit(solution)/shard_map/ppermute | solution.py:758
  85.6 15.6 %collective-permute-start.5 = (bf16[3,40,1024]{2,1,0:T(8,128)(2,1)S(1)}, bf16[3,40,1024]{2,1,0:T(8,128)(2,1)S(1)}, u32[]{:S(2)}, u32[]{:S(2)}) collective-permute-start(bf16[3,40,1024]{2,1,0:T(8,128)(2,1)S(1)} %bitcast.37), channel_id=1, source_target_pairs={{8,0},{16,8},{24,16},{9,1},{17,9},{25,17},{10,2},{18,10},{26,18},{... | collective-permute-start | bytes 737288 | tf_op jit(solution)/shard_map/ppermute | solution.py:758
  101.6 7.7 %collective-permute-start.8 = (bf16[38,3,1024]{2,1,0:T(4,128)(2,1)S(1)}, bf16[38,3,1024]{2,1,0:T(4,128)(2,1)S(1)}, u32[]{:S(2)}, u32[]{:S(2)}) collective-permute-start(bf16[38,3,1024]{2,1,0:T(4,128)(2,1)S(1)} %pad_maximum_fusion.5), channel_id=1, source_target_pairs={{1,0},{2,1},{3,2},{4,3},{5,4},{6,5},{7,6},{9,8},{10,9},{11,10},{12... | collective-permute-start | bytes 700424 | tf_op jit(solution)/shard_map/ppermute | solution.py:765
  103.1 6.2 %collective-permute-start.7 = (bf16[38,3,1024]{2,1,0:T(4,128)(2,1)S(1)}, bf16[38,3,1024]{2,1,0:T(4,128)(2,1)S(1)}, u32[]{:S(2)}, u32[]{:S(2)}) collective-permute-start(bf16[38,3,1024]{2,1,0:T(4,128)(2,1)S(1)} %pad_maximum_fusion.4), channel_id=1, source_target_pairs={{0,1},{1,2},{2,3},{3,4},{4,5},{5,6},{6,7},{8,9},{9,10},{10,11},{11... | collective-permute-start | bytes 700424 | tf_op jit(solution)/shard_map/ppermute | solution.py:765
  106.2 18.9 %collective-permute-start.9 = (bf16[1280,512]{1,0:T(8,128)(2,1)}, bf16[1280,512]{1,0:T(8,128)(2,1)S(1)}, u32[]{:S(2)}, u32[]{:S(2)}) collective-permute-start(bf16[1280,512]{1,0:T(8,128)(2,1)} %get-tuple-element.183), channel_id=1, source_target_pairs={{0,8},{1,17},{2,10},{3,19},{4,12},{5,21},{6,14},{7,23},{8,0},{9,25... | collective-permute-start | bytes 3932168 | tf_op jit(solution)/shard_map/ppermute | solution.py:673
  109.4 15.8 %copy-start.25 = (bf16[1280,512]{1,0:T(8,128)(2,1)S(1)}, bf16[1280,512]{1,0:T(8,128)(2,1)}, u32[]{:S(2)}) copy-start(bf16[1280,512]{1,0:T(8,128)(2,1)} %get-tuple-element.185) | copy-start | bytes 3932164
  109.4 19.7 %copy-start.19 = (f32[1280,512]{1,0:T(8,128)S(1)}, f32[1280,512]{1,0:T(8,128)}, u32[]{:S(2)}) copy-start(f32[1280,512]{1,0:T(8,128)} %get-tuple-element.168.gmiddle) | copy-start | bytes 7864324
  120.9 8.2 %copy-start = (bf16[32,40,512]{2,1,0:T(8,128)(2,1)S(1)}, bf16[32,40,512]{2,1,0:T(8,128)(2,1)}, u32[]{:S(2)}) copy-start(bf16[32,40,512]{2,1,0:T(8,128)(2,1)} %param.29) | copy-start | bytes 3932164
  125.5 12.1 %collective-permute-start.10 = (bf16[640,512]{1,0:T(8,128)(2,1)S(1)}, bf16[640,512]{1,0:T(8,128)(2,1)S(1)}, u32[]{:S(2)}, u32[]{:S(2)}) collective-permute-start(bf16[640,512]{1,0:T(8,128)(2,1)S(1)} %get-tuple-element.193), channel_id=1, source_target_pairs={{0,16},{1,3},{2,18},{3,1},{4,20},{5,7},{6,22},{7,5},{8,24},{9,11},... | collective-permute-start | bytes 1966088 | tf_op jit(solution)/shard_map/ppermute | solution.py:673
  129.0 10.4 %slice-start = ((s8[5242880]{0:T(1024)(128)(4,1)}), s8[4194304]{0:T(1024)(128)(4,1)S(1)}, s32[]{:S(2)}) async-start(s8[5242880]{0:T(1024)(128)(4,1)} %bitcast.34), calls=%async_computation | async-start | bytes 8388608
  129.1 10.3 %copy-start.8 = (bf16[2048,512]{1,0:T(8,128)(2,1)S(1)}, bf16[2048,512]{1,0:T(8,128)(2,1)}, u32[]{:S(2)}) copy-start(bf16[2048,512]{1,0:T(8,128)(2,1)} %down_w.5) | copy-start | bytes 6291460
  129.1 10.3 %slice-start.1 = ((s8[5242880]{0:T(1024)(128)(4,1)}), s8[1048576]{0:T(1024)(128)(4,1)S(1)}, s32[]{:S(2)}) async-start(s8[5242880]{0:T(1024)(128)(4,1)} %bitcast.34), calls=%async_computation.1 | async-start | bytes 2097152
  129.1 10.3 %copy-start.18 = (f32[1280,512]{1,0:T(8,128)S(1)}, f32[1280,512]{1,0:T(8,128)}, u32[]{:S(2)}) copy-start(f32[1280,512]{1,0:T(8,128)} %get-tuple-element.199.middle) | copy-start | bytes 7864324
  135.0 6.7 %collective-permute-start.12 = (bf16[576,512]{1,0:T(8,128)(2,1)S(1)}, bf16[576,512]{1,0:T(8,128)(2,1)S(1)}, u32[]{:S(2)}, u32[]{:S(2)}) collective-permute-start(bf16[576,512]{1,0:T(8,128)(2,1)S(1)} %get-tuple-element.196), channel_id=1, source_target_pairs={{0,1},{1,0},{2,3},{3,2},{4,5},{5,4},{6,7},{7,6},{8,9},{9,8},{10,11... | collective-permute-start | bytes 1769480 | tf_op jit(solution)/shard_map/ppermute | solution.py:673
  137.8 7.1 %collective-permute-start.11 = (bf16[320,512]{1,0:T(8,128)(2,1)S(1)}, bf16[320,512]{1,0:T(8,128)(2,1)S(1)}, u32[]{:S(2)}, u32[]{:S(2)}) collective-permute-start(bf16[320,512]{1,0:T(8,128)(2,1)S(1)} %get-tuple-element.284), channel_id=1, source_target_pairs={{0,2},{1,9},{2,0},{3,11},{4,6},{5,13},{6,4},{7,15},{8,10},{9,1},{1... | collective-permute-start | bytes 983048 | tf_op jit(solution)/shard_map/ppermute | solution.py:673
  141.8 8.7 %collective-permute-start.13 = (bf16[288,512]{1,0:T(8,128)(2,1)S(1)}, bf16[288,512]{1,0:T(8,128)(2,1)S(1)}, u32[]{:S(2)}, u32[]{:S(2)}) collective-permute-start(bf16[288,512]{1,0:T(8,128)(2,1)S(1)} %get-tuple-element.290), channel_id=1, source_target_pairs={{0,8},{1,17},{2,10},{3,19},{4,12},{5,21},{6,14},{7,23},{8,0},{9,25... | collective-permute-start | bytes 884744 | tf_op jit(solution)/shard_map/ppermute | solution.py:673
  145.0 16.2 %collective-permute-start.14 = (bf16[320,512]{1,0:T(8,128)(2,1)S(1)}, bf16[320,512]{1,0:T(8,128)(2,1)S(1)}, u32[]{:S(2)}, u32[]{:S(2)}) collective-permute-start(bf16[320,512]{1,0:T(8,128)(2,1)S(1)} %add_convert_fusion.5), channel_id=1, source_target_pairs={{0,4},{1,5},{2,6},{3,7},{4,0},{5,1},{6,2},{7,3},{8,12},{9,13},{10,... | collective-permute-start | bytes 983048 | tf_op jit(solution)/shard_map/ppermute | solution.py:673
  161.3 7.1 %collective-permute-start.16 = (bf16[320,512]{1,0:T(8,128)(2,1)S(1)}, bf16[320,512]{1,0:T(8,128)(2,1)S(1)}, u32[]{:S(2)}, u32[]{:S(2)}) collective-permute-start(bf16[320,512]{1,0:T(8,128)(2,1)S(1)} %add_convert_fusion.4), channel_id=1, source_target_pairs={{0,2},{1,9},{2,0},{3,11},{4,6},{5,13},{6,4},{7,15},{8,10},{9,1},{1... | collective-permute-start | bytes 983048 | tf_op jit(solution)/shard_map/ppermute | solution.py:673
  161.4 5.2 %collective-permute-start.15 = (bf16[144,512]{1,0:T(8,128)(2,1)S(1)}, bf16[144,512]{1,0:T(8,128)(2,1)S(1)}, u32[]{:S(2)}, u32[]{:S(2)}) collective-permute-start(bf16[144,512]{1,0:T(8,128)(2,1)S(1)} %get-tuple-element.296), channel_id=1, source_target_pairs={{0,16},{1,3},{2,18},{3,1},{4,20},{5,7},{6,22},{7,5},{8,24},{9,11},... | collective-permute-start | bytes 442376 | tf_op jit(solution)/shard_map/ppermute | solution.py:673
  168.6 10.7 %collective-permute-start.18 = (bf16[640,512]{1,0:T(8,128)(2,1)S(1)}, bf16[640,512]{1,0:T(8,128)(2,1)S(1)}, u32[]{:S(2)}, u32[]{:S(2)}) collective-permute-start(bf16[640,512]{1,0:T(8,128)(2,1)S(1)} %pad_maximum_fusion.2), channel_id=1, source_target_pairs={{0,16},{1,3},{2,18},{3,1},{4,20},{5,7},{6,22},{7,5},{8,24},{9,11},... | collective-permute-start | bytes 1966088 | tf_op jit(solution)/shard_map/ppermute | solution.py:673
  170.4 5.5 %collective-permute-start.17 = (bf16[72,512]{1,0:T(8,128)(2,1)}, bf16[72,512]{1,0:T(8,128)(2,1)}, u32[]{:S(2)}, u32[]{:S(2)}) collective-permute-start(bf16[72,512]{1,0:T(8,128)(2,1)} %get-tuple-element.300), channel_id=1, source_target_pairs={{0,2},{1,9},{2,0},{3,11},{4,6},{5,13},{6,4},{7,15},{8,10},{9,1},{1... | collective-permute-start | bytes 221192 | tf_op jit(solution)/shard_map/ppermute | solution.py:673
  179.4 19.3 %collective-permute-start.22 = (bf16[1280,512]{1,0:T(8,128)(2,1)S(1)}, bf16[1280,512]{1,0:T(8,128)(2,1)}, u32[]{:S(2)}, u32[]{:S(2)}) collective-permute-start(bf16[1280,512]{1,0:T(8,128)(2,1)S(1)} %pad_maximum_fusion.1), channel_id=1, source_target_pairs={{0,8},{1,17},{2,10},{3,19},{4,12},{5,21},{6,14},{7,23},{8,0},{9,25... | collective-permute-start | bytes 3932168 | tf_op jit(solution)/shard_map/ppermute | solution.py:673
  180.8 5.8 %collective-permute-start.19 = (bf16[72,512]{1,0:T(8,128)(2,1)S(1)}, bf16[72,512]{1,0:T(8,128)(2,1)S(1)}, u32[]{:S(2)}, u32[]{:S(2)}) collective-permute-start(bf16[72,512]{1,0:T(8,128)(2,1)S(1)} %add_convert_fusion.13), channel_id=1, source_target_pairs={{0,4},{1,5},{2,6},{3,7},{4,0},{5,1},{6,2},{7,3},{8,12},{9,13},{10,... | collective-permute-start | bytes 221192 | tf_op jit(solution)/shard_map/ppermute | solution.py:673
  186.5 4.4 %collective-permute-start.20 = (bf16[72,512]{1,0:T(8,128)(2,1)S(1)}, bf16[72,512]{1,0:T(8,128)(2,1)S(1)}, u32[]{:S(2)}, u32[]{:S(2)}) collective-permute-start(bf16[72,512]{1,0:T(8,128)(2,1)S(1)} %add_convert_fusion.12), channel_id=1, source_target_pairs={{0,2},{1,9},{2,0},{3,11},{4,6},{5,13},{6,4},{7,15},{8,10},{9,1},{1... | collective-permute-start | bytes 221192 | tf_op jit(solution)/shard_map/ppermute | solution.py:673
  191.6 6.0 %collective-permute-start.21 = (bf16[144,512]{1,0:T(8,128)(2,1)}, bf16[144,512]{1,0:T(8,128)(2,1)}, u32[]{:S(2)}, u32[]{:S(2)}) collective-permute-start(bf16[144,512]{1,0:T(8,128)(2,1)} %pad_maximum_fusion.9), channel_id=1, source_target_pairs={{0,16},{1,3},{2,18},{3,1},{4,20},{5,7},{6,22},{7,5},{8,24},{9,11},... | collective-permute-start | bytes 442376 | tf_op jit(solution)/shard_map/ppermute | solution.py:673
  200.4 7.0 %collective-permute-start.24 = (bf16[2560,512]{1,0:T(8,128)(2,1)S(1)}, bf16[2560,512]{1,0:T(8,128)(2,1)S(1)}, u32[]{:S(2)}, u32[]{:S(2)}) collective-permute-start(bf16[2560,512]{1,0:T(8,128)(2,1)S(1)} %pad_maximum_fusion.own), channel_id=1, source_target_pairs={{0,1},{1,0},{2,3},{3,2},{4,5},{5,4},{6,7},{7,6},{8,9},{9,8},{10,11... | collective-permute-start | bytes 7864328 | tf_op jit(solution)/shard_map/ppermute | solution.py:673
  200.4 6.8 %collective-permute-start.23 = (bf16[288,512]{1,0:T(8,128)(2,1)S(1)}, bf16[288,512]{1,0:T(8,128)(2,1)S(1)}, u32[]{:S(2)}, u32[]{:S(2)}) collective-permute-start(bf16[288,512]{1,0:T(8,128)(2,1)S(1)} %pad_maximum_fusion.6), channel_id=1, source_target_pairs={{0,8},{1,17},{2,10},{3,19},{4,12},{5,21},{6,14},{7,23},{8,0},{9,25... | collective-permute-start | bytes 884744 | tf_op jit(solution)/shard_map/ppermute | solution.py:673
  207.3 5.6 %collective-permute-start.25 = (bf16[576,512]{1,0:T(8,128)(2,1)S(1)}, bf16[576,512]{1,0:T(8,128)(2,1)S(1)}, u32[]{:S(2)}, u32[]{:S(2)}) collective-permute-start(bf16[576,512]{1,0:T(8,128)(2,1)S(1)} %pad_maximum_fusion.3.own), channel_id=1, source_target_pairs={{0,1},{1,0},{2,3},{3,2},{4,5},{5,4},{6,7},{7,6},{8,9},{9,8},{10,11... | collective-permute-start | bytes 1769480 | tf_op jit(solution)/shard_map/ppermute | solution.py:673
  (24 other events, 137.6 us)
